TPU v7x, 512 devices: a whole 4x8x8 slice. The times are simulated.
512 devices in a mesh: fsdp: 8 (over y_lo, x), wide: 64 (over y_hi, z, core).
Axes of the slice: x: 4, y: 8 (y_hi: 4, y_lo: 2; y = y_hi * 2 + y_lo), z: 8, core: 2. Of those that a mesh axis runs over, the one named last changes fastest.
Arguments:
- patches: bfloat16 [131072, 1280], P(('fsdp', 'wide')), may hold values from -6 to 6
- ln_gain: float32 [1280], replicated, may hold values from 0.1 to 1.9
- qkv_weight: bfloat16 [1280, 3840], P(None, 'fsdp')
- proj_weight: bfloat16 [1280, 1280], P('fsdp'), may hold values from -0.15625 to 0.15625
- out_cotangent: bfloat16 [131072, 1280], P(('fsdp', 'wide')), may hold values from -0.0625 to 0.0625
- tile_counts: int32 [512], P(('fsdp', 'wide')), may hold values from 1 to 2, as said below
- segment_ids: int32 [131072], P(('fsdp', 'wide')), may hold values from 0 to 63, as said below
Outputs:
- output: bfloat16 [131072, 1280], P(('fsdp', 'wide'))
- proj_grad: bfloat16 [1280, 1280], P('fsdp')
Inputs may be any that keep to these rules, and one draw needn't show every extreme that they name: Each device's live patches are its first tile_counts times 128 slots; some device is full and some holds one tile. `segment_ids`: within one device's slots the image number never falls, changes only at multiples of 4 slots, rises by at most one there and starts at 0; some device reaches the largest value.
All inputs are finite; a program needn't handle non-finite values.
Results may differ from a plain program's by a relative error of at most 0.035.
Values may be sent and summed in bfloat16 or wider, within the bound.
No kernel may reach another device: no remote copies, remote signals or barrier semaphores. Data moves between devices by JAX's collectives and lax.ppermute only.
A program may use at most 64 MiB of HBM per device.

v0:
```python
import jax
import jax.numpy as jnp
from jax import lax
from jax.sharding import PartitionSpec as P

HEADS = 16
TILE = 128


epsilon = 1e-06


def shards(patches, ln_gain, qkv_weight, proj_weight, out_cotangent, tile_counts, segment_ids):
    row_count = patches.shape[0]
    width = patches.shape[1]
    alive = lax.iota(jnp.int32, row_count) < tile_counts[0] * TILE
    inputs = patches.astype(jnp.float32)
    row_mean = jnp.mean(inputs, axis=1, keepdims=True)
    centred = inputs - row_mean
    variance = jnp.mean(centred * centred, axis=1, keepdims=True)
    normed = (centred * lax.rsqrt(variance + epsilon) * ln_gain).astype(jnp.bfloat16)
    mixed = jnp.dot(
        normed,
        lax.all_gather(qkv_weight, "fsdp", axis=1, tiled=True),
        preferred_element_type=jnp.float32,
    ).astype(jnp.bfloat16)
    head_size = width // HEADS
    queries = mixed[:, :width].reshape(row_count, HEADS, head_size)
    keyset = mixed[:, width : 2 * width].reshape(row_count, HEADS, head_size)
    valueset = mixed[:, 2 * width :].reshape(row_count, HEADS, head_size)
    scores = jnp.einsum(
        "qhd,khd->hqk", queries, keyset, preferred_element_type=jnp.float32
    ) * head_size ** (-0.5)
    allowed = (segment_ids[:, None] == segment_ids[None, :]) & (alive[:, None] == alive[None, :])
    scores = jnp.where(allowed[None], scores, jnp.float32(-1e30))
    peak = jnp.max(scores, axis=2, keepdims=True)
    weights = jnp.exp(scores - peak)
    probs = (weights / jnp.sum(weights, axis=2, keepdims=True)).astype(jnp.bfloat16)
    context = jnp.einsum(
        "hqk,khd->qhd", probs, valueset, preferred_element_type=jnp.float32
    ).reshape(row_count, width)
    context = jnp.where(alive[:, None], context, jnp.float32(0.0)).astype(jnp.bfloat16)
    projected = jnp.dot(
        context,
        lax.all_gather(proj_weight, "fsdp", axis=0, tiled=True),
        preferred_element_type=jnp.float32,
    )
    output = jnp.where(alive[:, None], inputs + projected, jnp.float32(0.0)).astype(jnp.bfloat16)
    cotangent = jnp.where(alive[:, None], out_cotangent, jnp.zeros_like(out_cotangent))
    partial_value = lax.dot_general(
        context, cotangent, (((0,), (0,)), ((), ())), preferred_element_type=jnp.float32
    ).astype(jnp.bfloat16)
    partial_value = lax.optimization_barrier(partial_value).astype(jnp.float32)
    shared = lax.psum_scatter(
        partial_value.astype(jnp.bfloat16), "fsdp", scatter_dimension=0, tiled=True
    ).astype(jnp.float32)
    grad_sum = lax.psum(shared, "wide")
    return (output, grad_sum.astype(jnp.bfloat16))


def solution(mesh):
    return jax.shard_map(
        shards,
        mesh=mesh,
        in_specs=(
            P(("fsdp", "wide"), None),
            P(),
            P(None, "fsdp"),
            P("fsdp", None),
            P(("fsdp", "wide"), None),
            P(("fsdp", "wide")),
            P(("fsdp", "wide")),
        ),
        out_specs=(P(("fsdp", "wide"), None), P("fsdp", None)),
        check_vma=False,
    )
```

profile of v0, /device:TPU:1, one launch (start us, length us, event | category | flops | bytes accessed | tf_op | source)
XLA Modules:
  0.0 791.3 jit_solution(4114572842440063867)
XLA Ops:
  7.2 0.0 all-gather.3.cloned.1.call-start
  7.2 0.7 all-gather.3.cloned.1.call-update
  7.9 0.0 reduce-scatter.2.cloned.1.call-start
  8.6 1.3 convert_reduce_fusion
  9.9 1.4 fusion.10
  11.3 0.9 compare_and_fusion
  12.2 114.2 %all-gather.3.cloned.1.call-done = bf16[1280,3840]{0,1:T(8,128)(2,1)} async-done(((bf16[1280,480]{0,1:T(8,128)(2,1)}), bf16[1280,3840]{0,1:T(8,128)(2,1)}) %all-gather.3.cloned.1.call-update) | async-done | bytes 9830416 | tf_op jit(solution)/shard_map/all_gather | solution.py:24
  126.4 6.8 convolution_convert_fusion.1
  133.2 0.1 fusion.25
  133.3 0.2 copy.15
  133.6 0.2 copy.16
  133.8 0.2 copy.14
  134.1 3.5 fusion.26
  137.5 0.0 copy-start.1
  137.5 2.8 fusion.6
  140.3 0.2 copy.18
  140.6 0.0 copy-done.1
  140.6 0.0 copy-start
  140.6 2.9 convolution_convert_fusion
  143.5 0.0 reduce-scatter.2.cloned.1.call-update
  143.6 0.0 all-gather.5.cloned.1.call-start
  143.6 0.7 all-gather.5.cloned.1.call-update
  144.3 0.0 all-reduce.2.cloned.1.call-start
  144.3 46.3 %reduce-scatter.2.cloned.1.call-done = bf16[160,1280]{1,0:T(8,128)(2,1)} async-done(((bf16[1280,1280]{1,0:T(8,128)(2,1)}), bf16[160,1280]{1,0:T(8,128)(2,1)}) %reduce-scatter.2.cloned.1.call-update) | async-done | bytes 409616 | tf_op jit(solution)/shard_map/reduce_scatter | solution.py:54
  190.7 0.0 all-reduce.2.cloned.1.call-update
  190.7 54.5 %all-gather.5.cloned.1.call-done = bf16[1280,1280]{1,0:T(8,128)(2,1)} async-done(((bf16[160,1280]{1,0:T(8,128)(2,1)}), bf16[1280,1280]{1,0:T(8,128)(2,1)}) %all-gather.5.cloned.1.call-update) | async-done | bytes 3276816 | tf_op jit(solution)/shard_map/all_gather | solution.py:45
  245.2 0.0 copy-done
  245.2 3.9 fusion.3
  249.1 533.9 %all-reduce.2.cloned.1.call-done = bf16[160,1280]{1,0:T(8,128)(2,1)} async-done(((bf16[160,1280]{1,0:T(8,128)(2,1)}), bf16[160,1280]{1,0:T(8,128)(2,1)}) %all-reduce.2.cloned.1.call-update) | async-done | bytes 409616 | tf_op jit(solution)/shard_map/psum | solution.py:57
  783.0 1.8 copy.22
  (3 shorter events, 0.0 us)
Async XLA Ops:
  7.2 119.2 %all-gather.3.cloned.1.call-start = ((), (), s32[]{:S(2)}) async-start(), calls=%async_computation.1 | async-start | bytes 11059200 | tf_op jit(solution)/shard_map/all_gather | solution.py:24
  7.9 182.8 %reduce-scatter.2.cloned.1.call-start = ((), (), s32[]{:S(2)}) async-start(), calls=%async_computation.3 | async-start | bytes 3686400 | tf_op jit(solution)/shard_map/reduce_scatter | solution.py:54
  137.5 3.0 copy-start.1
  140.6 104.6 %copy-start = (bf16[256,1280]{1,0:T(8,128)(2,1)S(1)}, bf16[256,1280]{1,0:T(8,128)(2,1)}, u32[]{:S(2)}) copy-start(bf16[256,1280]{1,0:T(8,128)(2,1)} %param.7) | copy-start | bytes 1966084
  143.6 101.7 %all-gather.5.cloned.1.call-start = ((), (), s32[]{:S(2)}) async-start(), calls=%async_computation.2 | async-start | bytes 3686400 | tf_op jit(solution)/shard_map/all_gather | solution.py:45
  144.3 638.7 %all-reduce.2.cloned.1.call-start = ((), (), s32[]{:S(2)}) async-start(), calls=%async_computation.4 | async-start | bytes 819200 | tf_op jit(solution)/shard_map/psum | solution.py:57
Sparse Core Ops, SparseCore 0:
  10.1 116.2 all-gather.2
  143.7 46.9 reduce-scatter.1
  192.9 52.2 all-gather.4
  248.2 534.6 all-reduce.1
where the time goes:
time: 792 us; the launch traced here: 791 us
  waiting for transfers between devices  750 us (95%)
  matrix products  19.9 us (3%)
  between operations  14.5 us (2%)
    psum x1, waiting for transfers between devices, shards(): grad_sum = lax.psum(shared, 'wide')  534 us
    all_gather x1, waiting for transfers between devices, shards(): lax.all_gather(qkv_weight, 'fsdp', axis=1, tiled=True)  114 us
    all_gather x1, waiting for transfers between devices, shards(): lax.all_gather(proj_weight, 'fsdp', axis=0, tiled=True)  54.5 us
    reduce_scatter x1, waiting for transfers between devices, shards(): lax.psum_scatter(partial_value.astype(jnp.bfloat16), 'fsdp', scatter_dime...  46.3 us
  transfers between devices with their start and end apart: 4, of which 4 were waited for; matrix products, arithmetic and copies ran while one was open for 1% of the time, Pallas kernels for 0%

commit v1 on v0

v1 whole, which is shorter than its diff:
```python
import functools
import math

import jax
import jax.numpy as jnp
import numpy as np
from jax import lax
from jax.experimental import pallas as pl
from jax.experimental.pallas import tpu as pltpu
from jax.sharding import Mesh
from jax.sharding import PartitionSpec as P

HEADS = 16
HEAD = 80
TILE = 128
ROWS = 256
WIDTH = 1280
EPSILON = 1e-06
BF16 = jnp.bfloat16
F32 = jnp.float32

Y_HI, Z, CORES = 4, 8, 2

HEAD_SETS = ((1, 2, 5, 6), (0, 3, 4, 7))


def block_tables():
    sends = np.zeros((8, 2, 2), np.int32)
    orders = np.zeros((2, 16), np.int32)
    for half, heads in enumerate(HEAD_SETS):
        for shard in range(8):
            picked = [k for k in range(3) if (3 * shard + k) % 8 in heads] + ([3] if shard in heads else [])
            assert len(picked) == 2
            for place, k in enumerate(picked):
                sends[shard, half, place] = k
                if k == 3:
                    slot = 12 + heads.index(shard)
                else:
                    kind, m = divmod(3 * shard + k, 8)
                    slot = 4 * kind + heads.index(m)
                orders[half, slot] = 2 * shard + place
    return sends, orders


SENDS, ORDERS = block_tables()
OWN_HALF = np.array([1 if j in HEAD_SETS[1] else 0 for j in range(8)], np.int32)


def norm_kernel(count_ref, patches_ref, gain_ref, images_ref, message_ref):
    inputs = patches_ref[...].astype(F32)
    row_mean = jnp.mean(inputs, axis=1, keepdims=True)
    centred = inputs - row_mean
    variance = jnp.mean(centred * centred, axis=1, keepdims=True)
    message_ref[:ROWS, :] = (centred * lax.rsqrt(variance + EPSILON) * gain_ref[...]).astype(BF16)
    dead = lax.broadcasted_iota(jnp.int32, (1, ROWS), 1) >= count_ref[0] * TILE
    code = (images_ref[...] + jnp.where(dead, 64, 0)).astype(F32)
    message_ref[ROWS:, :] = jnp.zeros((16, WIDTH), BF16)
    message_ref[ROWS:, :ROWS] = jnp.broadcast_to(code, (16, ROWS)).astype(BF16)


def attention_kernel(order_ref, x0_ref, x1_ref, x2_ref, x3_ref, blocks_ref, context_ref, weight_ref):
    scale = HEAD**-0.5 * math.log2(math.e)
    hidden = -1e30 * HEAD**0.5
    for slot in range(12):
        weight_ref[slot * HEAD : (slot + 1) * HEAD, :] = blocks_ref[order_ref[slot]]
    for part, x_ref in enumerate((x0_ref, x1_ref, x2_ref, x3_ref)):
        mixed = lax.dot_general(
            weight_ref[...], x_ref[:ROWS, :], (((1,), (1,)), ((), ())), preferred_element_type=F32
        ).astype(BF16)
        code = x_ref[ROWS : ROWS + 16, :ROWS].astype(F32)[0:1, :]
        square = jnp.broadcast_to(code, (ROWS, ROWS))
        allowed = square == square.T
        alive = code < 64.0
        for head in range(4):
            queries = mixed[head * HEAD : (head + 1) * HEAD, :]
            keyset = mixed[(4 + head) * HEAD : (5 + head) * HEAD, :]
            valueset = mixed[(8 + head) * HEAD : (9 + head) * HEAD, :]
            scores = lax.dot_general(keyset, queries, (((0,), (0,)), ((), ())), preferred_element_type=F32)
            scores = jnp.where(allowed, scores, hidden)
            peak = jnp.max(scores, axis=0, keepdims=True)
            weights = jnp.exp2((scores - peak) * scale)
            total = jnp.sum(weights, axis=0, keepdims=True)
            context = jnp.dot(valueset, weights.astype(BF16), preferred_element_type=F32)
            context = jnp.where(alive, context / total, 0.0)
            context_ref[part, head * HEAD : (head + 1) * HEAD, :] = context.astype(BF16)


def gradient_kernel(context_ref, c0_ref, c1_ref, c2_ref, c3_ref, grad_ref):
    for start in range(0, WIDTH, 256):
        total = None
        for part, c_ref in enumerate((c0_ref, c1_ref, c2_ref, c3_ref)):
            term = jnp.dot(context_ref[part], c_ref[:, start : start + 256], preferred_element_type=F32)
            total = term if total is None else total + term
        grad_ref[:, start : start + 256] = total.astype(BF16)


def project_kernel(order_ref, context_ref, blocks_ref, keep_ref, send_ref, weight_ref):
    for slot in range(4):
        weight_ref[slot * HEAD : (slot + 1) * HEAD, :] = blocks_ref[order_ref[12 + slot]]
    for part in range(4):
        projected = lax.dot_general(
            context_ref[part], weight_ref[...], (((0,), (0,)), ((), ())), preferred_element_type=F32
        )
        target = send_ref if part % 2 else keep_ref
        target[part // 2] = projected.astype(BF16)


VMEM = pl.BlockSpec(memory_space=pltpu.VMEM)
SMEM = pl.BlockSpec(memory_space=pltpu.SMEM)


def call(kernel, out_shape, in_specs, out_specs, scratch=(), limit=24 << 20, flops=0, read=0):
    return pl.pallas_call(
        kernel,
        out_shape=out_shape,
        in_specs=in_specs,
        out_specs=out_specs,
        scratch_shapes=scratch,
        compiler_params=pltpu.CompilerParams(vmem_limit_bytes=limit),
        cost_estimate=pl.CostEstimate(flops=flops, bytes_accessed=read, transcendentals=0),
    )


def array(*shape):
    return jax.ShapeDtypeStruct(shape, BF16)


def shards(patches, ln_gain, qkv_weight, proj_weight, out_cotangent, tile_counts, segment_ids):
    core = lax.axis_index("core")
    half = lax.axis_index("z") % 2
    shard = lax.axis_index("y_lo") * 4 + lax.axis_index("x")
    core_pairs = [(0, 1), (1, 0)]
    z_pairs = [(i, i ^ 1) for i in range(Z)]
    x_pairs = [(i, i ^ 1) for i in range(4)]

    def to_core(value):
        return lax.ppermute(value, "core", core_pairs)

    def to_pair(value):
        return lax.ppermute(value, "z", z_pairs)

    blocks = jnp.concatenate([qkv_weight.T.reshape(6, HEAD, WIDTH), proj_weight.reshape(2, HEAD, WIDTH)])
    sends = jnp.asarray(SENDS)[shard, half]
    own = jnp.concatenate([lax.dynamic_index_in_dim(blocks, 2 * sends[i] + core, 0) for i in range(2)])
    gathered = lax.all_to_all(
        jnp.broadcast_to(own[None], (8, 2, HEAD, WIDTH)), ("y_lo", "x"), 0, 0
    ).reshape(16, HEAD, WIDTH)
    order = jnp.asarray(ORDERS)[half]

    message = call(
        norm_kernel, array(ROWS + 16, WIDTH), [SMEM, VMEM, VMEM, VMEM], VMEM, read=3 * ROWS * WIDTH
    )(tile_counts, patches, ln_gain.reshape(1, WIDTH), segment_ids.reshape(1, ROWS))
    message_pair = to_pair(message)
    message_core = to_core(message)
    message_both = to_core(message_pair)

    cotangent_pair = to_pair(out_cotangent)
    cotangent_core = to_core(out_cotangent)
    cotangent_both = to_core(cotangent_pair)

    context = call(
        attention_kernel,
        array(4, 4 * HEAD, ROWS),
        [SMEM] + [VMEM] * 5,
        VMEM,
        [pltpu.VMEM((12 * HEAD, WIDTH), BF16)],
        flops=2 * 1024 * 1280 * 960 + 4 * 16 * 256 * 256 * 128,
        read=8 << 20,
    )(order, message, message_core, message_pair, message_both, gathered)

    grad = call(
        gradient_kernel, array(4 * HEAD, WIDTH), [VMEM] * 5, VMEM, flops=2 * 1024 * 1280 * 320, read=4 << 20
    )(context, out_cotangent, cotangent_core, cotangent_pair, cotangent_both)
    grad = lax.all_to_all(grad.reshape(8, 40, WIDTH), ("y_lo", "x"), 0, 0)
    grad = jnp.sum(grad.astype(F32), axis=0).astype(BF16)
    grad = lax.all_to_all(jnp.broadcast_to(grad[None], (Y_HI, 40, WIDTH)), "y_hi", 0, 0)
    grad = jnp.sum(grad.astype(F32), axis=0).astype(BF16)
    grad = lax.all_to_all(jnp.broadcast_to(grad[None], (Z, 40, WIDTH)), "z", 0, 0)
    grad = jnp.sum(grad.astype(F32).reshape(Z // 2, 2, 40, WIDTH), axis=0).astype(BF16)
    mine = jnp.asarray(OWN_HALF)[shard] == 1
    keep = jnp.where(mine, grad[1], grad[0])
    got = lax.ppermute(jnp.where(mine, grad[0], grad[1]), "x", x_pairs)
    even = shard % 2 == 0
    head_grad = jnp.concatenate([jnp.where(even, keep, got), jnp.where(even, got, keep)])
    other_grad = to_core(head_grad)
    first = core == 0
    proj_grad = jnp.concatenate([jnp.where(first, head_grad, other_grad), jnp.where(first, other_grad, head_grad)])

    keep_out, send_out = call(
        project_kernel,
        (array(2, ROWS, WIDTH), array(2, ROWS, WIDTH)),
        [SMEM, VMEM, VMEM],
        (VMEM, VMEM),
        [pltpu.VMEM((4 * HEAD, WIDTH), BF16)],
        flops=2 * 1024 * 1280 * 320,
        read=6 << 20,
    )(order, context, gathered)
    from_core = to_core(send_out)
    from_pair = to_pair((keep_out[1].astype(F32) + from_core[1].astype(F32)).astype(BF16))
    projected = keep_out[0].astype(F32) + from_core[0].astype(F32) + from_pair.astype(F32)
    alive = lax.iota(jnp.int32, ROWS) < tile_counts[0] * TILE
    output = jnp.where(alive[:, None], patches.astype(F32) + projected, F32(0.0)).astype(BF16)
    return output, proj_grad


def solution(mesh):
    fine = Mesh(mesh.devices.reshape(2, 4, Y_HI, Z, CORES), ("y_lo", "x", "y_hi", "z", "core"))
    fsdp = ("y_lo", "x")
    every = ("y_lo", "x", "y_hi", "z", "core")
    return jax.shard_map(
        shards,
        mesh=fine,
        in_specs=(P(every, None), P(), P(None, fsdp), P(fsdp, None), P(every, None), P(every), P(every)),
        out_specs=(P(every, None), P(fsdp, None)),
        check_vma=False,
    )
```

time: 792 us -> 168 us (0.21)
  the two profiles are of different devices: /device:TPU:1 before, /device:TPU:18 now
where the time goes in v1:
time: 168 us; the launch traced here: 167 us
  starting transfers between devices  45.5 us (27%)
  waiting for transfers between devices  42.8 us (25%)
  blocking collectives  36.5 us (22%)
  local copies, waits for them, and re-layouts  15.9 us (9%)
  Pallas kernels  15.6 us (9%)
  other arithmetic  7.18 us (4%)
  between operations  3.62 us (2%)
    ppermute x3, waiting for transfers between devices, to_pair(): return lax.ppermute(value, 'z', z_pairs)  32.7 us
    all_to_all x1, blocking collectives, shards(): grad = lax.all_to_all(grad.reshape(8, 40, WIDTH), ('y_lo', 'x'), 0, 0)  18.3 us
    all_to_all x1, blocking collectives, shards(): lax.all_to_all(jnp.broadcast_to(grad[None], (Y_HI, 40, WIDTH)), 'y_hi', 0...  18.2 us
    ppermute x6, starting transfers between devices, to_core(): return lax.ppermute(value, 'core', core_pairs)  12.1 us
    unnamed x36, local copies, waits for them, and re-layouts  11.1 us
    all_to_all x1, starting transfers between devices, shards(): lax.all_to_all(jnp.broadcast_to(grad[None], (Z, 40, WIDTH)), 'z', 0, 0)  9.68 us
    all_to_all x1, waiting for transfers between devices, shards(): lax.all_to_all(jnp.broadcast_to(grad[None], (Z, 40, WIDTH)), 'z', 0, 0)  9.64 us
    pallas_call x1, Pallas kernels, shards(): call(attention_kernel, array(4, 4 * HEAD, ROWS), [SMEM] + [VMEM] * 5, VME...  9.04 us
  transfers between devices with their start and end apart: 12, of which 5 were waited for; matrix products, arithmetic and copies ran while one was open for 2% of the time, Pallas kernels for 8%

profile of v1, /device:TPU:18, one launch (start us, length us, event | category | flops | bytes accessed | tf_op | source)
XLA Modules:
  0.0 167.0 jit_solution(3225200954608324546)
XLA Ops:
  0.6 0.7 constant_dynamic-slice_fusion
  1.3 0.6 fusion.7
  3.2 1.2 fusion.5
  4.5 2.0 %broadcast_in_dim.15 = bf16[8,2,80,1280]{3,2,1,0:T(8,128)(2,1)} broadcast(bf16[2,80,1280]{2,1,0:T(8,128)(2,1)S(1)} %pad_maximum_fusion), dimensions={1,2,3} | broadcast | bytes 3686400 | tf_op jit(solution)/shard_map/broadcast_in_dim | solution.py:146
  6.5 6.0 %all-to-all-start = ((bf16[8,2,80,1280]{3,2,1,0:T(8,128)(2,1)}), bf16[8,2,80,1280]{3,2,1,0:T(8,128)(2,1)S(1)}, u32[]{:S(2)}, u32[]{:S(2)}) async-start(bf16[8,2,80,1280]{3,2,1,0:T(8,128)(2,1)} %broadcast_in_dim.15), calls=%async_computation | async-start | bytes 6553600 | tf_op jit(solution)/shard_map/all_to_all | solution.py:145
  13.1 0.0 copy-done.15
  13.1 0.0 copy-done.8
  13.1 0.0 copy-start.2
  13.1 1.1 copy-done.2
  14.2 0.4 shard_map.113.x0_ref
  14.7 4.3 %collective-permute-start.1 = (bf16[272,1280]{1,0:T(8,128)(2,1)S(1)}, bf16[272,1280]{1,0:T(8,128)(2,1)S(1)}, u32[]{:S(2)}, u32[]{:S(2)}) collective-permute-start(bf16[272,1280]{1,0:T(8,128)(2,1)S(1)} %shard_map.113.x0_ref), channel_id=1, source_target_pairs={{0,2},{2,0},{4,6},{6,4},{8,10},{10,8},{12,14},{14,12},{1,3},{3,1},... | collective-permute-start | bytes 2088968 | tf_op jit(solution)/shard_map/ppermute | solution.py:140
  18.9 1.9 %collective-permute-start.6 = (bf16[256,1280]{1,0:T(8,128)(2,1)}, bf16[256,1280]{1,0:T(8,128)(2,1)}, u32[]{:S(2)}, u32[]{:S(2)}) collective-permute-start(bf16[256,1280]{1,0:T(8,128)(2,1)} %c0_ref.1), channel_id=1, source_target_pairs={{0,2},{2,0},{4,6},{6,4},{8,10},{10,8},{12,14},{14,12},{1,3},{3,1},... | collective-permute-start | bytes 1966088 | tf_op jit(solution)/shard_map/ppermute | solution.py:140
  20.9 1.9 %collective-permute-start = (bf16[272,1280]{1,0:T(8,128)(2,1)S(1)}, bf16[272,1280]{1,0:T(8,128)(2,1)S(1)}, u32[]{:S(2)}, u32[]{:S(2)}) collective-permute-start(bf16[272,1280]{1,0:T(8,128)(2,1)S(1)} %shard_map.113.x0_ref), channel_id=1, source_target_pairs={{0,1},{1,0},{2,3},{3,2},{4,5},{5,4},{6,7},{7,6},{8,9},{9,8},{10,11... | collective-permute-start | bytes 2088968 | tf_op jit(solution)/shard_map/ppermute | solution.py:137
  22.8 0.0 copy-start.6
  22.8 0.8 copy-done.6
  23.7 11.8 %collective-permute-done.1.x2_ref = bf16[272,1280]{1,0:T(8,128)(2,1)S(1)} collective-permute-done((bf16[272,1280]{1,0:T(8,128)(2,1)S(1)}, bf16[272,1280]{1,0:T(8,128)(2,1)S(1)}, u32[]{:S(2)}, u32[]{:S(2)}) %collective-permute-start.1) | collective-permute-done | bytes 696352 | tf_op jit(solution)/shard_map/ppermute | solution.py:140
  35.4 1.9 %collective-permute-start.2 = (bf16[272,1280]{1,0:T(8,128)(2,1)S(1)}, bf16[272,1280]{1,0:T(8,128)(2,1)S(1)}, u32[]{:S(2)}, u32[]{:S(2)}) collective-permute-start(bf16[272,1280]{1,0:T(8,128)(2,1)S(1)} %collective-permute-done.1.x2_ref), channel_id=1, source_target_pairs={{0,1},{1,0},{2,3},{3,2},{4,5},{5,4},{6,7},{7,6},{8,9},{9,8},{10,11... | collective-permute-start | bytes 2088968 | tf_op jit(solution)/shard_map/ppermute | solution.py:137
  37.4 0.0 copy-start.9
  37.4 0.8 copy-done.9
  38.2 2.4 %collective-permute-start.5 = (bf16[256,1280]{1,0:T(8,128)(2,1)}, bf16[256,1280]{1,0:T(8,128)(2,1)}, u32[]{:S(2)}, u32[]{:S(2)}) collective-permute-start(bf16[256,1280]{1,0:T(8,128)(2,1)} %c0_ref.1), channel_id=1, source_target_pairs={{0,1},{1,0},{2,3},{3,2},{4,5},{5,4},{6,7},{7,6},{8,9},{9,8},{10,11... | collective-permute-start | bytes 1966088 | tf_op jit(solution)/shard_map/ppermute | solution.py:137
  40.6 7.5 %collective-permute-done.6.c2_ref = bf16[256,1280]{1,0:T(8,128)(2,1)} collective-permute-done((bf16[256,1280]{1,0:T(8,128)(2,1)}, bf16[256,1280]{1,0:T(8,128)(2,1)}, u32[]{:S(2)}, u32[]{:S(2)}) %collective-permute-start.6) | collective-permute-done | bytes 655392 | tf_op jit(solution)/shard_map/ppermute | solution.py:140
  48.1 1.9 %collective-permute-start.7 = (bf16[256,1280]{1,0:T(8,128)(2,1)}, bf16[256,1280]{1,0:T(8,128)(2,1)}, u32[]{:S(2)}, u32[]{:S(2)}) collective-permute-start(bf16[256,1280]{1,0:T(8,128)(2,1)} %collective-permute-done.6.c2_ref), channel_id=1, source_target_pairs={{0,1},{1,0},{2,3},{3,2},{4,5},{5,4},{6,7},{7,6},{8,9},{9,8},{10,11... | collective-permute-start | bytes 1966088 | tf_op jit(solution)/shard_map/ppermute | solution.py:137
  50.0 0.0 copy-done.16
  50.1 0.0 collective-permute-done.x1_ref
  50.1 0.0 copy-start.11
  50.1 0.8 copy-done.11
  50.9 0.0 collective-permute-done.2.x3_ref
  50.9 0.9 copy-done.13
  51.8 0.0 all-to-all-done
  51.8 1.1 copy-done.7
  52.9 1.1 copy-done.10
  54.0 1.1 copy-done.12
  55.1 1.1 copy-done.14
  56.2 9.0 %shard_map.114.context_ref = bf16[4,320,256]{2,1,0:T(8,128)(2,1)S(1)} custom-call(s32[16]{0:T(128)S(1)} %fusion.6.order_ref, bf16[272,1280]{1,0:T(8,128)(2,1)S(1)} %copy-done.7, bf16[272,1280]{1,0:T(8,128)(2,1)S(1)} %copy-done.12, bf16[272,1280]{1,0:T(8,128)(2,1)S(1)} %copy-done.10, bf16[272,1280]{1,0:T(8,128)(2,1)S(1)} %copy-done.14, ...), custom_call_target="tpu_custom_call" | custom-call | flops 3053453312 | bytes 8388608 | tf_op jit(solution)/shard_map/pallas_call | solution.py:161
  65.3 0.0 copy-start
  65.3 0.0 collective-permute-done.5.c1_ref
  65.3 0.0 collective-permute-done.7.c3_ref
  65.3 2.9 %shard_map.116 = bf16[320,1280]{1,0:T(8,128)(2,1)S(1)} custom-call(bf16[4,320,256]{2,1,0:T(8,128)(2,1)S(1)} %shard_map.114.context_ref, bf16[256,1280]{1,0:T(8,128)(2,1)} %c0_ref.1, bf16[256,1280]{1,0:T(8,128)(2,1)} %collective-permute-done.5.c1_ref, bf16[256,1280]{1,0:T(8,128)(2,1)} %collective-permute-done.6.c2_ref, ...), custom_call_target="tpu_custom_call" | custom-call | flops 838860800 | bytes 4194304 | tf_op jit(solution)/shard_map/pallas_call | solution.py:171
  68.3 18.3 %all_to_all.20 = bf16[8,40,1280]{2,1,0:T(8,128)(2,1)} all-to-all(bf16[8,40,1280]{2,1,0:T(8,128)(2,1)S(1)} %bitcast.31), channel_id=1, replica_groups=mesh['y_lo'=2,'x'=4,'y_hi'=4,'z'=8,'core'=2] {'y_lo','x'}, dimensions={0} | all-to-all | bytes 1638400 | tf_op jit(solution)/shard_map/all_to_all | solution.py:174
  86.5 1.3 reduce_sum.33
  87.8 18.2 %all_to_all.21 = bf16[4,40,1280]{2,1,0:T(8,128)(2,1)} all-to-all(bf16[4,40,1280]{2,1,0:T(8,128)(2,1)S(1)} %broadcast_in_dim.34), channel_id=1, replica_groups=mesh['y_lo'=2,'x'=4,'y_hi'=4,'z'=8,'core'=2] {'y_hi'}, dimensions={0} | all-to-all | bytes 819200 | tf_op jit(solution)/shard_map/all_to_all | solution.py:176
  106.0 1.1 reduce_sum.34
  107.1 0.9 broadcast_in_dim.35
  108.0 9.7 %all-to-all-start.3 = ((bf16[8,40,1280]{2,1,0:T(8,128)(2,1)}), bf16[8,40,1280]{2,1,0:T(8,128)(2,1)}, u32[]{:S(2)}, u32[]{:S(2)}) async-start(bf16[8,40,1280]{2,1,0:T(8,128)(2,1)} %broadcast_in_dim.35), calls=%async_computation.3 | async-start | bytes 1638400 | tf_op jit(solution)/shard_map/all_to_all | solution.py:178
  117.7 1.1 copy-done.1
  118.8 3.2 %shard_map.115 = (bf16[2,256,1280]{2,1,0:T(8,128)(2,1)S(1)}, bf16[2,256,1280]{2,1,0:T(8,128)(2,1)}) custom-call(s32[16]{0:T(128)S(1)} %fusion.6.order_ref, bf16[4,320,256]{2,1,0:T(8,128)(2,1)S(1)} %copy-done.1, bf16[16,80,1280]{2,1,0:T(8,128)(2,1)S(1)} %bitcast.30), custom_call_target="tpu_custom_call" | custom-call | flops 838860800 | bytes 6291456 | tf_op jit(solution)/shard_map/pallas_call | solution.py:189
  122.0 1.1 copy-done.4
  123.0 2.0 %collective-permute-start.3 = (bf16[2,256,1280]{2,1,0:T(8,128)(2,1)}, bf16[2,256,1280]{2,1,0:T(8,128)(2,1)S(1)}, u32[]{:S(2)}, u32[]{:S(2)}) collective-permute-start(bf16[2,256,1280]{2,1,0:T(8,128)(2,1)} %get-tuple-element.5), channel_id=1, source_target_pairs={{0,1},{1,0},{2,3},{3,2},{4,5},{5,4},{6,7},{7,6},{8,9},{9,8},{10,11... | collective-permute-start | bytes 3932168 | tf_op jit(solution)/shard_map/ppermute | solution.py:137
  125.1 0.0 copy-done.17
  125.1 0.6 dynamic_slice.20
  126.4 9.6 %all-to-all-done.3 = bf16[8,40,1280]{2,1,0:T(8,128)(2,1)} async-done(((bf16[8,40,1280]{2,1,0:T(8,128)(2,1)}), bf16[8,40,1280]{2,1,0:T(8,128)(2,1)}, u32[]{:S(2)}, u32[]{:S(2)}) %all-to-all-start.3) | async-done | bytes 819232 | tf_op jit(solution)/shard_map/all_to_all | solution.py:178
  136.0 1.3 reduce.2
  137.3 9.0 %collective-permute-start.8 = (bf16[40,1280]{1,0:T(8,128)(2,1)S(1)}, bf16[40,1280]{1,0:T(8,128)(2,1)S(1)}, u32[]{:S(2)}, u32[]{:S(2)}) collective-permute-start(bf16[40,1280]{1,0:T(8,128)(2,1)S(1)} %select_bitcast_fusion), channel_id=1, source_target_pairs={{0,64},{64,0},{128,192},{192,128},{1,65},{65,1},{129,193},{193,129... | collective-permute-start | bytes 307208 | tf_op jit(solution)/shard_map/ppermute | solution.py:182
  146.4 0.0 collective-permute-done.3
  146.4 0.0 copy-start.3
  146.4 0.2 fusion.3
  146.6 2.5 %collective-permute-start.4 = (bf16[256,1280]{1,0:T(8,128)(2,1)S(1)}, bf16[256,1280]{1,0:T(8,128)(2,1)S(1)}, u32[]{:S(2)}, u32[]{:S(2)}) collective-permute-start(bf16[256,1280]{1,0:T(8,128)(2,1)S(1)} %fusion.3), channel_id=1, source_target_pairs={{0,2},{2,0},{4,6},{6,4},{8,10},{10,8},{12,14},{14,12},{1,3},{3,1},... | collective-permute-start | bytes 1966088 | tf_op jit(solution)/shard_map/ppermute | solution.py:140
  149.0 0.4 collective-permute-done.8
  149.5 1.9 %collective-permute-start.9 = (bf16[80,1280]{1,0:T(8,128)(2,1)S(1)}, bf16[80,1280]{1,0:T(8,128)(2,1)S(1)}, u32[]{:S(2)}, u32[]{:S(2)}) collective-permute-start(bf16[80,1280]{1,0:T(8,128)(2,1)S(1)} %pad_maximum_fusion.2), channel_id=1, source_target_pairs={{0,1},{1,0},{2,3},{3,2},{4,5},{5,4},{6,7},{7,6},{8,9},{9,8},{10,11... | collective-permute-start | bytes 614408 | tf_op jit(solution)/shard_map/ppermute | solution.py:137
  151.4 13.5 %collective-permute-done.4 = bf16[256,1280]{1,0:T(8,128)(2,1)S(1)} collective-permute-done((bf16[256,1280]{1,0:T(8,128)(2,1)S(1)}, bf16[256,1280]{1,0:T(8,128)(2,1)S(1)}, u32[]{:S(2)}, u32[]{:S(2)}) %collective-permute-start.4) | collective-permute-done | bytes 655392 | tf_op jit(solution)/shard_map/ppermute | solution.py:140
  164.8 1.3 fusion.2
  166.1 0.0 collective-permute-done.9
  166.1 0.1 broadcast_select_fusion.1
  166.2 0.8 pad_maximum_fusion.1
  (23 shorter events, 0.2 us)
Async XLA Ops:
  6.5 6.6 %copy-start.15 = (f32[1280]{0:T(1024)S(1)}, f32[1280]{0:T(1024)}, u32[]{:S(2)}) copy-start(f32[1280]{0:T(1024)} %param.11) | copy-start | bytes 15364
  6.5 6.7 %copy-start.8 = (s32[256]{0:T(256)S(1)}, s32[256]{0:T(256)}, u32[]{:S(2)}) copy-start(s32[256]{0:T(256)} %param.16) | copy-start | bytes 3076
  6.5 45.4 %all-to-all-start = ((bf16[8,2,80,1280]{3,2,1,0:T(8,128)(2,1)}), bf16[8,2,80,1280]{3,2,1,0:T(8,128)(2,1)S(1)}, u32[]{:S(2)}, u32[]{:S(2)}) async-start(bf16[8,2,80,1280]{3,2,1,0:T(8,128)(2,1)} %broadcast_in_dim.15), calls=%async_computation | async-start | bytes 6553600 | tf_op jit(solution)/shard_map/all_to_all | solution.py:145
  12.4 37.6 %copy-start.16 = (s32[2,16]{1,0:T(2,128)S(1)}, s32[2,16]{1,0:T(2,128)}, u32[]{:S(2)}) copy-start(s32[2,16]{1,0:T(2,128)} %constant.67.clone) | copy-start | bytes 388
  13.1 1.1 copy-start.2
  14.7 20.8 %collective-permute-start.1 = (bf16[272,1280]{1,0:T(8,128)(2,1)S(1)}, bf16[272,1280]{1,0:T(8,128)(2,1)S(1)}, u32[]{:S(2)}, u32[]{:S(2)}) collective-permute-start(bf16[272,1280]{1,0:T(8,128)(2,1)S(1)} %shard_map.113.x0_ref), channel_id=1, source_target_pairs={{0,2},{2,0},{4,6},{6,4},{8,10},{10,8},{12,14},{14,12},{1,3},{3,1},... | collective-permute-start | bytes 2088968 | tf_op jit(solution)/shard_map/ppermute | solution.py:140
  18.9 29.2 %collective-permute-start.6 = (bf16[256,1280]{1,0:T(8,128)(2,1)}, bf16[256,1280]{1,0:T(8,128)(2,1)}, u32[]{:S(2)}, u32[]{:S(2)}) collective-permute-start(bf16[256,1280]{1,0:T(8,128)(2,1)} %c0_ref.1), channel_id=1, source_target_pairs={{0,2},{2,0},{4,6},{6,4},{8,10},{10,8},{12,14},{14,12},{1,3},{3,1},... | collective-permute-start | bytes 1966088 | tf_op jit(solution)/shard_map/ppermute | solution.py:140
  20.9 29.2 %collective-permute-start = (bf16[272,1280]{1,0:T(8,128)(2,1)S(1)}, bf16[272,1280]{1,0:T(8,128)(2,1)S(1)}, u32[]{:S(2)}, u32[]{:S(2)}) collective-permute-start(bf16[272,1280]{1,0:T(8,128)(2,1)S(1)} %shard_map.113.x0_ref), channel_id=1, source_target_pairs={{0,1},{1,0},{2,3},{3,2},{4,5},{5,4},{6,7},{7,6},{8,9},{9,8},{10,11... | collective-permute-start | bytes 2088968 | tf_op jit(solution)/shard_map/ppermute | solution.py:137
  22.8 0.9 copy-start.6
  35.4 15.5 %collective-permute-start.2 = (bf16[272,1280]{1,0:T(8,128)(2,1)S(1)}, bf16[272,1280]{1,0:T(8,128)(2,1)S(1)}, u32[]{:S(2)}, u32[]{:S(2)}) collective-permute-start(bf16[272,1280]{1,0:T(8,128)(2,1)S(1)} %collective-permute-done.1.x2_ref), channel_id=1, source_target_pairs={{0,1},{1,0},{2,3},{3,2},{4,5},{5,4},{6,7},{7,6},{8,9},{9,8},{10,11... | collective-permute-start | bytes 2088968 | tf_op jit(solution)/shard_map/ppermute | solution.py:137
  37.4 0.9 copy-start.9
  38.2 27.1 %collective-permute-start.5 = (bf16[256,1280]{1,0:T(8,128)(2,1)}, bf16[256,1280]{1,0:T(8,128)(2,1)}, u32[]{:S(2)}, u32[]{:S(2)}) collective-permute-start(bf16[256,1280]{1,0:T(8,128)(2,1)} %c0_ref.1), channel_id=1, source_target_pairs={{0,1},{1,0},{2,3},{3,2},{4,5},{5,4},{6,7},{7,6},{8,9},{9,8},{10,11... | collective-permute-start | bytes 1966088 | tf_op jit(solution)/shard_map/ppermute | solution.py:137
  48.1 17.2 %collective-permute-start.7 = (bf16[256,1280]{1,0:T(8,128)(2,1)}, bf16[256,1280]{1,0:T(8,128)(2,1)}, u32[]{:S(2)}, u32[]{:S(2)}) collective-permute-start(bf16[256,1280]{1,0:T(8,128)(2,1)} %collective-permute-done.6.c2_ref), channel_id=1, source_target_pairs={{0,1},{1,0},{2,3},{3,2},{4,5},{5,4},{6,7},{7,6},{8,9},{9,8},{10,11... | collective-permute-start | bytes 1966088 | tf_op jit(solution)/shard_map/ppermute | solution.py:137
  50.1 0.9 copy-start.11
  50.9 0.9 copy-start.13
  51.8 1.1 copy-start.7
  52.9 1.1 copy-start.10
  54.0 1.1 copy-start.12
  55.1 1.1 copy-start.14
  65.3 3.0 %copy-start = (bf16[4,320,256]{2,1,0:T(8,128)(2,1)}, bf16[4,320,256]{2,1,0:T(8,128)(2,1)S(1)}, u32[]{:S(2)}) copy-start(bf16[4,320,256]{2,1,0:T(8,128)(2,1)S(1)} %shard_map.114.context_ref) | copy-start | bytes 1966084
  108.0 28.0 %all-to-all-start.3 = ((bf16[8,40,1280]{2,1,0:T(8,128)(2,1)}), bf16[8,40,1280]{2,1,0:T(8,128)(2,1)}, u32[]{:S(2)}, u32[]{:S(2)}) async-start(bf16[8,40,1280]{2,1,0:T(8,128)(2,1)} %broadcast_in_dim.35), calls=%async_computation.3 | async-start | bytes 1638400 | tf_op jit(solution)/shard_map/all_to_all | solution.py:178
  117.7 1.1 copy-start.1
  118.8 6.3 %copy-start.17 = (s32[8]{0:T(128)S(1)}, s32[8]{0:T(128)}, u32[]{:S(2)}) copy-start(s32[8]{0:T(128)} %constant.68.clone) | copy-start | bytes 100
  122.0 1.1 copy-start.4
  123.0 23.3 %copy-start.5 = (bf16[2,256,1280]{2,1,0:T(8,128)(2,1)S(1)}, bf16[2,256,1280]{2,1,0:T(8,128)(2,1)}, u32[]{:S(2)}) copy-start(bf16[2,256,1280]{2,1,0:T(8,128)(2,1)} %copy-done.4) | copy-start | bytes 3932164
  123.0 23.3 %collective-permute-start.3 = (bf16[2,256,1280]{2,1,0:T(8,128)(2,1)}, bf16[2,256,1280]{2,1,0:T(8,128)(2,1)S(1)}, u32[]{:S(2)}, u32[]{:S(2)}) collective-permute-start(bf16[2,256,1280]{2,1,0:T(8,128)(2,1)} %get-tuple-element.5), channel_id=1, source_target_pairs={{0,1},{1,0},{2,3},{3,2},{4,5},{5,4},{6,7},{7,6},{8,9},{9,8},{10,11... | collective-permute-start | bytes 3932168 | tf_op jit(solution)/shard_map/ppermute | solution.py:137
  137.3 12.1 %collective-permute-start.8 = (bf16[40,1280]{1,0:T(8,128)(2,1)S(1)}, bf16[40,1280]{1,0:T(8,128)(2,1)S(1)}, u32[]{:S(2)}, u32[]{:S(2)}) collective-permute-start(bf16[40,1280]{1,0:T(8,128)(2,1)S(1)} %select_bitcast_fusion), channel_id=1, source_target_pairs={{0,64},{64,0},{128,192},{192,128},{1,65},{65,1},{129,193},{193,129... | collective-permute-start | bytes 307208 | tf_op jit(solution)/shard_map/ppermute | solution.py:182
  146.4 18.5 %copy-start.3 = (bf16[256,1280]{1,0:T(8,128)(2,1)S(1)}, bf16[256,1280]{1,0:T(8,128)(2,1)}, u32[]{:S(2)}) copy-start(bf16[256,1280]{1,0:T(8,128)(2,1)} %patches_ref.1) | copy-start | bytes 1966084
  146.6 18.3 %collective-permute-start.4 = (bf16[256,1280]{1,0:T(8,128)(2,1)S(1)}, bf16[256,1280]{1,0:T(8,128)(2,1)S(1)}, u32[]{:S(2)}, u32[]{:S(2)}) collective-permute-start(bf16[256,1280]{1,0:T(8,128)(2,1)S(1)} %fusion.3), channel_id=1, source_target_pairs={{0,2},{2,0},{4,6},{6,4},{8,10},{10,8},{12,14},{14,12},{1,3},{3,1},... | collective-permute-start | bytes 1966088 | tf_op jit(solution)/shard_map/ppermute | solution.py:140
  149.5 16.7 %collective-permute-start.9 = (bf16[80,1280]{1,0:T(8,128)(2,1)S(1)}, bf16[80,1280]{1,0:T(8,128)(2,1)S(1)}, u32[]{:S(2)}, u32[]{:S(2)}) collective-permute-start(bf16[80,1280]{1,0:T(8,128)(2,1)S(1)} %pad_maximum_fusion.2), channel_id=1, source_target_pairs={{0,1},{1,0},{2,3},{3,2},{4,5},{5,4},{6,7},{7,6},{8,9},{9,8},{10,11... | collective-permute-start | bytes 614408 | tf_op jit(solution)/shard_map/ppermute | solution.py:137

commit v2 on v1

v2 whole, which is shorter than its diff:
```python
import math

import jax
import jax.numpy as jnp
import numpy as np
from jax import lax
from jax.experimental import pallas as pl
from jax.experimental.pallas import tpu as pltpu
from jax.sharding import Mesh
from jax.sharding import PartitionSpec as P

HEADS = 16
HEAD = 80
TILE = 128
ROWS = 256
NOTE = 16
WIDTH = 1280
EPSILON = 1e-06
BF16 = jnp.bfloat16
F32 = jnp.float32

Y_HI, Z_QUAD, Z_PAIR, CORES = 4, 4, 2, 2
AXES = ("y_lo", "x", "y_hi", "z_quad", "z_pair", "core")
FSDP = ("y_lo", "x")

HEAD_SETS = ((1, 2, 5, 6), (0, 3, 4, 7))


def block_tables():
    sends = np.zeros((8, 2, 2), np.int32)
    orders = np.zeros((2, 16), np.int32)
    for half, heads in enumerate(HEAD_SETS):
        for shard in range(8):
            picked = [k for k in range(3) if (3 * shard + k) % 8 in heads] + ([3] if shard in heads else [])
            assert len(picked) == 2
            for place, k in enumerate(picked):
                sends[shard, half, place] = k
                if k == 3:
                    slot = 12 + heads.index(shard)
                else:
                    kind, m = divmod(3 * shard + k, 8)
                    slot = 4 * kind + heads.index(m)
                orders[half, slot] = 2 * shard + place
    return sends.reshape(-1), orders.reshape(-1)


SENDS, ORDERS = block_tables()


def owns(x, half):
    return int(x in (0, 3)) == half


CORE_SWAP = [(0, 1), (1, 0)]
PAIR_SWAP = [(0, 1), (1, 0)]
TO_OWNER = [
    (2 * x + half, 2 * x + (1 - half) if owns(x, half) else 2 * (x ^ 1) + half) for x in range(4) for half in range(2)
]
ACROSS = [(2 * x + half, 2 * (x ^ 1) + (1 - half)) for x in range(4) for half in range(2) if not owns(x, half)]


def front_kernel(
    place_ref,
    sends_ref,
    count_ref,
    patches_ref,
    gain_ref,
    images_ref,
    qkv_ref,
    proj_ref,
    out_ref,
    blocks_ref,
    rows_ref,
    message_ref,
    held_ref,
    read_sems,
    write_sems,
    sems,
):
    fetch = pltpu.make_async_copy(patches_ref, rows_ref, sems.at[0])
    fetch.start()
    core = place_ref[1]
    for i in range(2):
        choice = sends_ref[2 * place_ref[0] + i]

        @pl.when(choice < 3)
        def _():
            pltpu.make_async_copy(qkv_ref.at[2 * jnp.minimum(choice, 2) + core], held_ref.at[i], read_sems.at[i]).start()

        @pl.when(choice == 3)
        def _():
            pltpu.make_async_copy(proj_ref.at[core], held_ref.at[i], read_sems.at[i]).start()

    copies = []
    for i in range(2):
        pltpu.make_async_copy(proj_ref.at[0], held_ref.at[i], read_sems.at[i]).wait()
        for peer in range(8):
            copies.append(pltpu.make_async_copy(held_ref.at[i], blocks_ref.at[peer, i], write_sems.at[8 * i + peer]))
            copies[-1].start()

    fetch.wait()
    inputs = rows_ref[...].astype(F32)
    row_mean = jnp.mean(inputs, axis=1, keepdims=True)
    centred = inputs - row_mean
    variance = jnp.mean(centred * centred, axis=1, keepdims=True)
    message_ref[:ROWS, :] = (centred * lax.rsqrt(variance + EPSILON) * gain_ref[...].reshape(1, WIDTH)).astype(BF16)
    dead = lax.broadcasted_iota(jnp.int32, (1, ROWS), 1) >= count_ref[0] * TILE
    code = (images_ref[...].reshape(1, ROWS) + jnp.where(dead, 64, 0)).astype(F32)
    message_ref[ROWS:, :] = jnp.zeros((NOTE, WIDTH), BF16)
    message_ref[ROWS:, :ROWS] = jnp.broadcast_to(code, (NOTE, ROWS)).astype(BF16)
    copies.append(pltpu.make_async_copy(message_ref, out_ref, sems.at[1]))
    copies[-1].start()
    for copy in copies:
        copy.wait()


def attention_kernel(
    place_ref,
    order_ref,
    x0_ref,
    x1_ref,
    x2_ref,
    x3_ref,
    blocks_ref,
    out_ref,
    x_ref,
    weight_ref,
    context_ref,
    x_sems,
    sems,
    out_sem,
):
    scale = HEAD**-0.5 * math.log2(math.e)
    hidden = -1e30 * HEAD**0.5
    copies = []
    for slot in range(12):
        source = blocks_ref.at[order_ref[16 * place_ref[2] + slot]]
        copies.append(pltpu.make_async_copy(source, weight_ref.at[slot * HEAD : (slot + 1) * HEAD], sems.at[slot]))
    arrivals = [
        pltpu.make_async_copy(ref, x_ref.at[part], x_sems.at[part])
        for part, ref in enumerate((x0_ref, x1_ref, x2_ref, x3_ref))
    ]
    for copy in copies + arrivals:
        copy.start()
    for copy in copies + arrivals:
        copy.wait()
    for part in range(4):
        mixed = lax.dot_general(
            weight_ref[...], x_ref[part, :ROWS, :], (((1,), (1,)), ((), ())), preferred_element_type=F32
        ).astype(BF16)
        code = x_ref[part, ROWS:, :ROWS].astype(F32)[0:1, :]
        square = jnp.broadcast_to(code, (ROWS, ROWS))
        allowed = square == square.T
        alive = code < 64.0
        for head in range(4):
            queries = mixed[head * HEAD : (head + 1) * HEAD, :]
            keyset = mixed[(4 + head) * HEAD : (5 + head) * HEAD, :]
            valueset = mixed[(8 + head) * HEAD : (9 + head) * HEAD, :]
            scores = lax.dot_general(keyset, queries, (((0,), (0,)), ((), ())), preferred_element_type=F32)
            scores = jnp.where(allowed, scores, hidden)
            peak = jnp.max(scores, axis=0, keepdims=True)
            weights = jnp.exp2((scores - peak) * scale)
            total = jnp.sum(weights, axis=0, keepdims=True)
            context = jnp.dot(valueset, weights.astype(BF16), preferred_element_type=F32)
            context = jnp.where(alive, context / total, 0.0)
            context_ref[head * HEAD : (head + 1) * HEAD, part * ROWS : (part + 1) * ROWS] = context.astype(BF16)
    store = pltpu.make_async_copy(context_ref, out_ref, out_sem)
    store.start()
    store.wait()


def gradient_kernel(from_ref, c0_ref, c1_ref, c2_ref, c3_ref, grad_ref, context_ref, c_ref, sems):
    copies = [
        pltpu.make_async_copy(ref, c_ref.at[part * ROWS : (part + 1) * ROWS], sems.at[part])
        for part, ref in enumerate((c0_ref, c1_ref, c2_ref, c3_ref))
    ]
    copies.append(pltpu.make_async_copy(from_ref, context_ref, sems.at[4]))
    for copy in copies:
        copy.start()
    for copy in copies:
        copy.wait()
    for start in range(0, WIDTH, 256):
        columns = slice(start, start + 256)
        grad_ref[:, columns] = jnp.dot(
            context_ref[...], c_ref[:, columns], preferred_element_type=F32
        ).astype(BF16)


def project_kernel(
    place_ref, order_ref, from_ref, blocks_ref, keep_ref, send_ref, context_ref, held_ref, weight_ref, sems, sem, out_sems
):
    copies = [pltpu.make_async_copy(from_ref, context_ref, sem)]
    copies[0].start()
    for slot in range(4):
        source = blocks_ref.at[order_ref[16 * place_ref[2] + 12 + slot]]
        copies.append(pltpu.make_async_copy(source, weight_ref.at[slot * HEAD : (slot + 1) * HEAD], sems.at[slot]))
        copies[-1].start()
    for copy in copies:
        copy.wait()
    stores = []
    for part in (1, 3, 0, 2):
        projected = lax.dot_general(
            context_ref[:, part * ROWS : (part + 1) * ROWS],
            weight_ref[...],
            (((0,), (0,)), ((), ())),
            preferred_element_type=F32,
        )
        held_ref[part] = projected.astype(BF16)
        target = send_ref if part % 2 else keep_ref
        stores.append(pltpu.make_async_copy(held_ref.at[part], target.at[part // 2], out_sems.at[part]))
        stores[-1].start()
    for store in stores:
        store.wait()


def sum_kernel(terms_ref, copies_ref):
    total = terms_ref[0].astype(F32)
    for i in range(1, terms_ref.shape[0]):
        total = total + terms_ref[i].astype(F32)
    total = total.astype(BF16)
    for i in range(copies_ref.shape[0]):
        copies_ref[i] = total


VMEM = pl.BlockSpec(memory_space=pltpu.VMEM)
SMEM = pl.BlockSpec(memory_space=pltpu.SMEM)
HBM = pl.BlockSpec(memory_space=pltpu.HBM)
DMA = pltpu.SemaphoreType.DMA


def call(kernel, out_shape, in_specs, out_specs, scratch=(), limit=60 << 20, flops=0, read=0):
    return pl.pallas_call(
        kernel,
        out_shape=out_shape,
        in_specs=in_specs,
        out_specs=out_specs,
        scratch_shapes=scratch,
        compiler_params=pltpu.CompilerParams(vmem_limit_bytes=limit),
        cost_estimate=pl.CostEstimate(flops=flops, bytes_accessed=read, transcendentals=0),
    )


def array(*shape):
    return jax.ShapeDtypeStruct(shape, BF16)


def sum_of(terms, copies):
    return call(
        sum_kernel,
        array(copies, *terms.shape[1:]),
        [VMEM],
        VMEM,
        limit=16 << 20,
        read=2 * (copies + terms.shape[0]) * 40 * WIDTH
    )(terms)


def shards(patches, ln_gain, qkv_weight, proj_weight, out_cotangent, tile_counts, segment_ids):
    core = lax.axis_index("core")
    half = lax.axis_index("z_pair")
    x = lax.axis_index("x")
    shard = lax.axis_index("y_lo") * 4 + x
    place = jnp.stack([2 * shard + half, core, half])
    sends, orders = jnp.asarray(SENDS), jnp.asarray(ORDERS)

    def to_core(value):
        return lax.ppermute(value, "core", CORE_SWAP)

    def to_pair(value):
        return lax.ppermute(value, "z_pair", PAIR_SWAP)

    message, own = call(
        front_kernel,
        (array(ROWS + NOTE, WIDTH), array(8, 2, HEAD, WIDTH)),
        [SMEM, SMEM, SMEM, HBM, VMEM, VMEM, HBM, HBM],
        (HBM, HBM),
        [
            pltpu.VMEM((ROWS, WIDTH), BF16),
            pltpu.VMEM((ROWS + NOTE, WIDTH), BF16),
            pltpu.VMEM((2, HEAD, WIDTH), BF16),
            DMA((2,)),
            DMA((16,)),
            DMA((2,)),
        ],
        read=6 << 20,
    )(
        place,
        sends,
        tile_counts,
        patches,
        ln_gain,
        segment_ids,
        qkv_weight.T.reshape(6, HEAD, WIDTH),
        proj_weight.reshape(2, HEAD, WIDTH),
    )
    blocks = lax.all_to_all(own, FSDP, 0, 0).reshape(16, HEAD, WIDTH)

    message_pair = to_pair(message)
    message_core = to_core(message)
    cotangent_core = to_core(out_cotangent)
    message_pair, cotangent_late = lax.optimization_barrier((message_pair, out_cotangent))
    message_both = to_core(message_pair)
    cotangent_pair = to_pair(cotangent_late)

    context = call(
        attention_kernel,
        array(4 * HEAD, 4 * ROWS),
        [SMEM, SMEM] + [HBM] * 5,
        HBM,
        [
            pltpu.VMEM((4, ROWS + NOTE, WIDTH), BF16),
            pltpu.VMEM((12 * HEAD, WIDTH), BF16),
            pltpu.VMEM((4 * HEAD, 4 * ROWS), BF16),
            DMA((4,)),
            DMA((12,)),
            DMA,
        ],
        limit=52 << 20,
        flops=2 * 1024 * 1280 * 960 + 4 * 16 * 256 * 256 * 128,
        read=8 << 20,
    )(place, orders, message, message_core, message_pair, message_both, blocks)

    context, cotangent_pair = lax.optimization_barrier((context, cotangent_pair))
    cotangent_both = to_core(cotangent_pair)

    grad = call(
        gradient_kernel,
        array(4 * HEAD, WIDTH),
        [HBM] * 5,
        VMEM,
        [pltpu.VMEM((4 * HEAD, 4 * ROWS), BF16), pltpu.VMEM((4 * ROWS, WIDTH), BF16), DMA((5,))],
        flops=2 * 1024 * 1280 * 320,
        read=4 << 20,
    )(context, out_cotangent, cotangent_core, cotangent_pair, cotangent_both)

    keep_out, send_out = call(
        project_kernel,
        (array(2, ROWS, WIDTH), array(2, ROWS, WIDTH)),
        [SMEM, SMEM, HBM, HBM],
        (HBM, HBM),
        [
            pltpu.VMEM((4 * HEAD, 4 * ROWS), BF16),
            pltpu.VMEM((4, ROWS, WIDTH), BF16),
            pltpu.VMEM((4 * HEAD, WIDTH), BF16),
            DMA((4,)),
            DMA,
            DMA((4,)),
        ],
        limit=52 << 20,
        flops=2 * 1024 * 1280 * 320,
        read=6 << 20,
    )(place, orders, context, blocks)

    from_core = to_core(send_out)
    for_pair = (keep_out[1].astype(F32) + from_core[1].astype(F32)).astype(BF16)
    grad = lax.all_to_all(grad.reshape(8, 40, WIDTH), FSDP, 0, 0)
    grad, for_pair = lax.optimization_barrier((grad, for_pair))
    from_pair = to_pair(for_pair)
    grad = sum_of(grad, Y_HI)
    grad = lax.all_to_all(grad, "y_hi", 0, 0)
    grad, from_pair = lax.optimization_barrier((grad, from_pair))
    grad = sum_of(grad, Z_QUAD)

    projected = keep_out[0].astype(F32) + from_core[0].astype(F32) + from_pair.astype(F32)
    alive = lax.iota(jnp.int32, ROWS) < tile_counts[0] * TILE
    output = jnp.where(alive[:, None], patches.astype(F32) + projected, F32(0.0)).astype(BF16)

    grad = lax.all_to_all(grad, "z_quad", 0, 0)
    grad, output = lax.optimization_barrier((grad, output))
    grad = sum_of(grad, 1)[0]

    first = lax.ppermute(grad, ("x", "z_pair"), TO_OWNER)
    second = lax.ppermute(grad, ("x", "z_pair"), ACROSS)
    owner = ((x == 0) | (x == 3)) == (half == 1)
    near = jnp.where(owner, grad, first)
    far = jnp.where(owner, first, second)
    even = x % 2 == 0
    head_grad = jnp.concatenate([jnp.where(even, near, far), jnp.where(even, far, near)])
    other_grad = to_core(head_grad)
    proj_grad = jnp.concatenate(
        [jnp.where(core == 0, head_grad, other_grad), jnp.where(core == 0, other_grad, head_grad)]
    )
    return output, proj_grad


def solution(mesh):
    fine = Mesh(mesh.devices.reshape(2, 4, Y_HI, Z_QUAD, Z_PAIR, CORES), AXES)
    return jax.shard_map(
        shards,
        mesh=fine,
        in_specs=(P(AXES, None), P(), P(None, FSDP), P(FSDP, None), P(AXES, None), P(AXES), P(AXES)),
        out_specs=(P(AXES, None), P(FSDP, None)),
        check_vma=False,
    )
```

time: 168 us -> 153 us (0.911)
  the two profiles are of different devices: /device:TPU:18 before, /device:TPU:1 now
where the time goes in v2:
time: 153 us; the launch traced here: 152 us
  starting transfers between devices  72.1 us (47%)
  waiting for transfers between devices  47.6 us (31%)
  Pallas kernels  25.7 us (17%)
  other arithmetic  5.13 us (3%)
  between operations  1.6 us (1%)
    ppermute x6, starting transfers between devices, to_core(): return lax.ppermute(value, 'core', CORE_SWAP)  32 us
    pallas_call x1, Pallas kernels, shards(): call(attention_kernel, array(4 * HEAD, 4 * ROWS), [SMEM, SMEM] + [HBM] *...  11.8 us
    ppermute x3, starting transfers between devices, to_pair(): return lax.ppermute(value, 'z_pair', PAIR_SWAP)  11.4 us
    all_to_all x1, waiting for transfers between devices, shards(): grad = lax.all_to_all(grad.reshape(8, 40, WIDTH), FSDP, 0, 0)  11 us
    all_to_all x1, waiting for transfers between devices, shards(): blocks = lax.all_to_all(own, FSDP, 0, 0).reshape(16, HEAD, WIDTH)  9.83 us
    all_to_all x1, waiting for transfers between devices, shards(): grad = lax.all_to_all(grad, 'y_hi', 0, 0)  9.13 us
    all_to_all x1, starting transfers between devices, shards(): grad = lax.all_to_all(grad, 'z_quad', 0, 0)  9.12 us
    ppermute x3, waiting for transfers between devices, to_pair(): return lax.ppermute(value, 'z_pair', PAIR_SWAP)  6.43 us
  transfers between devices with their start and end apart: 15, of which 8 were waited for; matrix products, arithmetic and copies ran while one was open for 2% of the time, Pallas kernels for 14%

profile of v2, /device:TPU:1, one launch (start us, length us, event | category | flops | bytes accessed | tf_op | source)
XLA Modules:
  0.0 152.2 jit_solution(16369506387408723948)
XLA Ops:
  1.3 0.6 pad_add_fusion.place_ref
  1.9 3.9 %shard_map.104 = (bf16[272,1280]{1,0:T(8,128)(2,1)}, bf16[8,2,80,1280]{3,2,1,0:T(8,128)(2,1)}) custom-call(s32[3]{0:T(128)} %pad_add_fusion.place_ref, s32[32]{0:T(128)} %constant.44.clone.sends_ref, s32[1]{0:T(128)S(6)} %copy.11.count_ref, bf16[256,1280]{1,0:T(8,128)(2,1)} %patches_ref.1, f32[1280]{0:T(1024)} %gain_ref.1, s32[256]{0:T(256)} %images_ref.1, ...), custom_call_target="tpu_custom_call" | custom-call | bytes 6291456 | tf_op jit(solution)/shard_map/pallas_call | solution.py:272
  5.8 0.0 copy-start.3
  5.8 0.0 copy-start.6
  5.8 0.0 copy-start.1
  5.9 0.0 copy-start.2
  5.9 6.0 %all-to-all-start = ((bf16[8,2,80,1280]{3,2,1,0:T(8,128)(2,1)}), bf16[8,2,80,1280]{3,2,1,0:T(8,128)(2,1)}, u32[]{:S(2)}, u32[]{:S(2)}) async-start(bf16[8,2,80,1280]{3,2,1,0:T(8,128)(2,1)} %get-tuple-element.18), calls=%async_computation | async-start | bytes 6553600 | tf_op jit(solution)/shard_map/all_to_all | solution.py:296
  11.9 0.0 copy-done.3
  11.9 4.0 %collective-permute-start.1 = (bf16[272,1280]{1,0:T(8,128)(2,1)S(1)}, bf16[272,1280]{1,0:T(8,128)(2,1)S(1)}, u32[]{:S(2)}, u32[]{:S(2)}) collective-permute-start(bf16[272,1280]{1,0:T(8,128)(2,1)S(1)} %copy-done.3), channel_id=1, source_target_pairs={{0,2},{2,0},{1,3},{3,1},{4,6},{6,4},{5,7},{7,5},{8,10},{10,8},{9,1... | collective-permute-start | bytes 2088968 | tf_op jit(solution)/shard_map/ppermute | solution.py:270
  15.9 5.3 %collective-permute-start = (bf16[272,1280]{1,0:T(8,128)(2,1)S(1)}, bf16[272,1280]{1,0:T(8,128)(2,1)S(1)}, u32[]{:S(2)}, u32[]{:S(2)}) collective-permute-start(bf16[272,1280]{1,0:T(8,128)(2,1)S(1)} %copy-done.3), channel_id=1, source_target_pairs={{0,1},{1,0},{2,3},{3,2},{4,5},{5,4},{6,7},{7,6},{8,9},{9,8},{10,11... | collective-permute-start | bytes 2088968 | tf_op jit(solution)/shard_map/ppermute | solution.py:267
  21.2 6.4 %collective-permute-done.1.x2_ref = bf16[272,1280]{1,0:T(8,128)(2,1)S(1)} collective-permute-done((bf16[272,1280]{1,0:T(8,128)(2,1)S(1)}, bf16[272,1280]{1,0:T(8,128)(2,1)S(1)}, u32[]{:S(2)}, u32[]{:S(2)}) %collective-permute-start.1) | collective-permute-done | bytes 696352 | tf_op jit(solution)/shard_map/ppermute | solution.py:270
  27.6 0.0 copy-start.7
  27.6 6.7 %collective-permute-start.2 = (bf16[272,1280]{1,0:T(8,128)(2,1)S(1)}, bf16[272,1280]{1,0:T(8,128)(2,1)}, u32[]{:S(2)}, u32[]{:S(2)}) collective-permute-start(bf16[272,1280]{1,0:T(8,128)(2,1)S(1)} %collective-permute-done.1.x2_ref), channel_id=1, source_target_pairs={{0,1},{1,0},{2,3},{3,2},{4,5},{5,4},{6,7},{7,6},{8,9},{9,8},{10,11... | collective-permute-start | bytes 2088968 | tf_op jit(solution)/shard_map/ppermute | solution.py:267
  34.3 0.0 copy-done.6
  34.4 3.4 %collective-permute-start.3 = (bf16[256,1280]{1,0:T(8,128)(2,1)S(1)}, bf16[256,1280]{1,0:T(8,128)(2,1)}, u32[]{:S(2)}, u32[]{:S(2)}) collective-permute-start(bf16[256,1280]{1,0:T(8,128)(2,1)S(1)} %copy-done.6), channel_id=1, source_target_pairs={{0,2},{2,0},{1,3},{3,1},{4,6},{6,4},{5,7},{7,5},{8,10},{10,8},{9,1... | collective-permute-start | bytes 1966088 | tf_op jit(solution)/shard_map/ppermute | solution.py:270
  37.7 2.2 %collective-permute-start.4 = (bf16[256,1280]{1,0:T(8,128)(2,1)S(1)}, bf16[256,1280]{1,0:T(8,128)(2,1)}, u32[]{:S(2)}, u32[]{:S(2)}) collective-permute-start(bf16[256,1280]{1,0:T(8,128)(2,1)S(1)} %copy-done.6), channel_id=1, source_target_pairs={{0,1},{1,0},{2,3},{3,2},{4,5},{5,4},{6,7},{7,6},{8,9},{9,8},{10,11... | collective-permute-start | bytes 1966088 | tf_op jit(solution)/shard_map/ppermute | solution.py:267
  39.9 0.0 collective-permute-done.x1_ref
  39.9 0.0 copy-start.8
  40.0 0.0 collective-permute-done.2.x3_ref
  40.0 9.8 %all-to-all-done = bf16[8,2,80,1280]{3,2,1,0:T(8,128)(2,1)} async-done(((bf16[8,2,80,1280]{3,2,1,0:T(8,128)(2,1)}), bf16[8,2,80,1280]{3,2,1,0:T(8,128)(2,1)}, u32[]{:S(2)}, u32[]{:S(2)}) %all-to-all-start) | async-done | bytes 3276832 | tf_op jit(solution)/shard_map/all_to_all | solution.py:296
  49.8 0.0 copy-done.7
  49.8 0.0 copy-done.8
  49.8 0.0 copy-done.1
  49.8 0.0 copy-done.2
  49.8 11.8 %shard_map.105.from_ref = bf16[320,1024]{1,0:T(8,128)(2,1)S(1)} custom-call(s32[3]{0:T(128)S(1)} %copy-done.1, s32[32]{0:T(128)S(1)} %copy-done.2, bf16[272,1280]{1,0:T(8,128)(2,1)S(1)} %copy-done.3, bf16[272,1280]{1,0:T(8,128)(2,1)} %copy-done.8, bf16[272,1280]{1,0:T(8,128)(2,1)} %copy-done.7, bf16[272,1280]{1,0:T(8,128)(2,1)} %collective-permute-done.2.x3_ref, ...), custom_call_target="tpu_custom_call" | custom-call | flops 3053453312 | bytes 8388608 | tf_op jit(solution)/shard_map/pallas_call | solution.py:305
  61.6 0.0 copy-start
  61.6 0.0 collective-permute-done.3.c2_ref
  61.7 3.7 %collective-permute-start.5 = (bf16[256,1280]{1,0:T(8,128)(2,1)}, bf16[256,1280]{1,0:T(8,128)(2,1)}, u32[]{:S(2)}, u32[]{:S(2)}) collective-permute-start(bf16[256,1280]{1,0:T(8,128)(2,1)} %collective-permute-done.3.c2_ref), channel_id=1, source_target_pairs={{0,1},{1,0},{2,3},{3,2},{4,5},{5,4},{6,7},{7,6},{8,9},{9,8},{10,11... | collective-permute-start | bytes 1966088 | tf_op jit(solution)/shard_map/ppermute | solution.py:267
  65.4 4.4 %shard_map.107 = (bf16[2,256,1280]{2,1,0:T(8,128)(2,1)S(1)}, bf16[2,256,1280]{2,1,0:T(8,128)(2,1)}) custom-call(s32[3]{0:T(128)S(1)} %copy-done.1, s32[32]{0:T(128)S(1)} %copy-done.2, bf16[320,1024]{1,0:T(8,128)(2,1)S(1)} %shard_map.105.from_ref, bf16[16,80,1280]{2,1,0:T(8,128)(2,1)} %bitcast.6.blocks_ref), custom_call_target="tpu_custom_call" | custom-call | flops 838860800 | bytes 6291456 | tf_op jit(solution)/shard_map/pallas_call | solution.py:336
  69.8 0.0 copy-done
  69.8 1.9 %collective-permute-start.6 = (bf16[2,256,1280]{2,1,0:T(8,128)(2,1)}, bf16[2,256,1280]{2,1,0:T(8,128)(2,1)S(1)}, u32[]{:S(2)}, u32[]{:S(2)}) collective-permute-start(bf16[2,256,1280]{2,1,0:T(8,128)(2,1)} %get-tuple-element.23), channel_id=1, source_target_pairs={{0,1},{1,0},{2,3},{3,2},{4,5},{5,4},{6,7},{7,6},{8,9},{9,8},{10,11... | collective-permute-start | bytes 3932168 | tf_op jit(solution)/shard_map/ppermute | solution.py:267
  71.7 0.0 collective-permute-done.4.c1_ref
  71.7 0.0 collective-permute-done.5.c3_ref
  71.7 3.8 %shard_map.106 = bf16[320,1280]{1,0:T(8,128)(2,1)} custom-call(bf16[320,1024]{1,0:T(8,128)(2,1)} %copy-done, bf16[256,1280]{1,0:T(8,128)(2,1)} %c0_ref.1, bf16[256,1280]{1,0:T(8,128)(2,1)} %collective-permute-done.4.c1_ref, bf16[256,1280]{1,0:T(8,128)(2,1)} %collective-permute-done.3.c2_ref, bf16[256,1280]{1,0:T(8,128)(2,1)} %collective-permute-done.5.c3_ref), custom_call_target="tpu_custom_call" | custom-call | flops 838860800 | bytes 4194304 | tf_op jit(solution)/shard_map/pallas_call | solution.py:326
  75.6 3.6 %all-to-all-start.1 = ((bf16[8,40,1280]{2,1,0:T(8,128)(2,1)}), bf16[8,40,1280]{2,1,0:T(8,128)(2,1)S(1)}, u32[]{:S(2)}, u32[]{:S(2)}) async-start(bf16[8,40,1280]{2,1,0:T(8,128)(2,1)} %bitcast.25), calls=%async_computation.1 | async-start | bytes 1638400 | tf_op jit(solution)/shard_map/all_to_all | solution.py:356
  79.1 0.0 collective-permute-done.6
  79.1 0.0 copy-start.5
  79.1 1.1 fusion.3
  80.3 11.0 %all-to-all-done.1.terms_ref = bf16[8,40,1280]{2,1,0:T(8,128)(2,1)S(1)} async-done(((bf16[8,40,1280]{2,1,0:T(8,128)(2,1)}), bf16[8,40,1280]{2,1,0:T(8,128)(2,1)S(1)}, u32[]{:S(2)}, u32[]{:S(2)}) %all-to-all-start.1) | async-done | bytes 819232 | tf_op jit(solution)/shard_map/all_to_all | solution.py:356
  91.3 4.0 %collective-permute-start.7 = (bf16[256,1280]{1,0:T(8,128)(2,1)}, bf16[256,1280]{1,0:T(8,128)(2,1)}, u32[]{:S(2)}, u32[]{:S(2)}) collective-permute-start(bf16[256,1280]{1,0:T(8,128)(2,1)} %fusion.3), channel_id=1, source_target_pairs={{0,2},{2,0},{1,3},{3,1},{4,6},{6,4},{5,7},{7,5},{8,10},{10,8},{9,1... | collective-permute-start | bytes 1966088 | tf_op jit(solution)/shard_map/ppermute | solution.py:270
  95.3 0.9 shard_map.108
  96.1 0.0 copy-done.5
  96.1 0.0 copy-start.4
  96.1 6.3 %all-to-all-start.2 = ((bf16[4,40,1280]{2,1,0:T(8,128)(2,1)}), bf16[4,40,1280]{2,1,0:T(8,128)(2,1)S(1)}, u32[]{:S(2)}, u32[]{:S(2)}) async-start(bf16[4,40,1280]{2,1,0:T(8,128)(2,1)} %shard_map.108), calls=%async_computation.2 | async-start | bytes 819200 | tf_op jit(solution)/shard_map/all_to_all | solution.py:360
  102.4 9.1 %all-to-all-done.2.terms_ref = bf16[4,40,1280]{2,1,0:T(8,128)(2,1)S(1)} async-done(((bf16[4,40,1280]{2,1,0:T(8,128)(2,1)}), bf16[4,40,1280]{2,1,0:T(8,128)(2,1)S(1)}, u32[]{:S(2)}, u32[]{:S(2)}) %all-to-all-start.2) | async-done | bytes 409632 | tf_op jit(solution)/shard_map/all_to_all | solution.py:360
  111.5 0.0 collective-permute-done.7
  111.5 0.8 shard_map.109
  112.4 9.1 %all-to-all-start.3 = ((bf16[4,40,1280]{2,1,0:T(8,128)(2,1)}), bf16[4,40,1280]{2,1,0:T(8,128)(2,1)S(1)}, u32[]{:S(2)}, u32[]{:S(2)}) async-start(bf16[4,40,1280]{2,1,0:T(8,128)(2,1)} %shard_map.109), calls=%async_computation.3 | async-start | bytes 819200 | tf_op jit(solution)/shard_map/all_to_all | solution.py:368
  121.5 0.0 copy-done.4
  121.5 2.5 %fusion.2 = bf16[256,1280]{1,0:T(8,128)(2,1)} fusion(bf16[256,1280]{1,0:T(8,128)(2,1)} %collective-permute-done.7, bf16[256,1280]{1,0:T(8,128)(2,1)S(1)} %copy-done.4, bf16[2,256,1280]{2,1,0:T(8,128)(2,1)} %copy-done.5, bf16[2,256,1280]{2,1,0:T(8,128)(2,1)S(1)} %get-tuple-element.22, pred[256]{0:T(512)(128)(4,1)S(1)} %iota_compare_fusion), kind=kLoop, calls=%fused_computation.3 | loop fusion | flops 2949120 | bytes 3277056 | tf_op jit(solution)/shard_map/convert_element_type | solution.py:366
  124.0 6.4 %all-to-all-done.3.terms_ref = bf16[4,40,1280]{2,1,0:T(8,128)(2,1)S(1)} async-done(((bf16[4,40,1280]{2,1,0:T(8,128)(2,1)}), bf16[4,40,1280]{2,1,0:T(8,128)(2,1)S(1)}, u32[]{:S(2)}, u32[]{:S(2)}) %all-to-all-start.3) | async-done | bytes 409632 | tf_op jit(solution)/shard_map/all_to_all | solution.py:368
  130.4 0.1 shard_map.110
  130.5 1.9 %collective-permute-start.9 = (bf16[40,1280]{1,0:T(8,128)(2,1)S(1)}, bf16[40,1280]{1,0:T(8,128)(2,1)S(1)}, u32[]{:S(2)}, u32[]{:S(2)}) collective-permute-start(bf16[40,1280]{1,0:T(8,128)(2,1)S(1)} %bitcast.23), channel_id=1, source_target_pairs={{0,66},{66,0},{130,192},{192,130},{1,67},{67,1},{131,193},{193,131... | collective-permute-start | bytes 307208 | tf_op jit(solution)/shard_map/ppermute | solution.py:373
  132.4 1.9 %collective-permute-start.8 = (bf16[40,1280]{1,0:T(8,128)(2,1)S(1)}, bf16[40,1280]{1,0:T(8,128)(2,1)S(1)}, u32[]{:S(2)}, u32[]{:S(2)}) collective-permute-start(bf16[40,1280]{1,0:T(8,128)(2,1)S(1)} %bitcast.24), channel_id=1, source_target_pairs={{0,64},{2,0},{64,66},{66,2},{128,130},{130,194},{192,128},{194,192... | collective-permute-start | bytes 307208 | tf_op jit(solution)/shard_map/ppermute | solution.py:372
  134.4 2.7 %collective-permute-done.9 = bf16[40,1280]{1,0:T(8,128)(2,1)S(1)} collective-permute-done((bf16[40,1280]{1,0:T(8,128)(2,1)S(1)}, bf16[40,1280]{1,0:T(8,128)(2,1)S(1)}, u32[]{:S(2)}, u32[]{:S(2)}) %collective-permute-start.9) | collective-permute-done | bytes 102432 | tf_op jit(solution)/shard_map/ppermute | solution.py:373
  137.1 1.1 collective-permute-done.8
  138.2 12.1 %collective-permute-start.10 = (bf16[80,1280]{1,0:T(8,128)(2,1)S(1)}, bf16[80,1280]{1,0:T(8,128)(2,1)S(1)}, u32[]{:S(2)}, u32[]{:S(2)}) collective-permute-start(bf16[80,1280]{1,0:T(8,128)(2,1)S(1)} %pad_maximum_fusion.1), channel_id=1, source_target_pairs={{0,1},{1,0},{2,3},{3,2},{4,5},{5,4},{6,7},{7,6},{8,9},{9,8},{10,11... | collective-permute-start | bytes 614408 | tf_op jit(solution)/shard_map/ppermute | solution.py:267
  150.3 1.1 collective-permute-done.10
  151.3 0.1 broadcast_select_fusion.1
  151.4 0.8 pad_maximum_fusion
  (3 shorter events, 0.0 us)
Async XLA Ops:
  5.8 6.1 %copy-start.3 = (bf16[272,1280]{1,0:T(8,128)(2,1)S(1)}, bf16[272,1280]{1,0:T(8,128)(2,1)}, u32[]{:S(2)}) copy-start(bf16[272,1280]{1,0:T(8,128)(2,1)} %get-tuple-element.16.x0_ref) | copy-start | bytes 2088964
  5.8 28.5 %copy-start.6 = (bf16[256,1280]{1,0:T(8,128)(2,1)S(1)}, bf16[256,1280]{1,0:T(8,128)(2,1)}, u32[]{:S(2)}) copy-start(bf16[256,1280]{1,0:T(8,128)(2,1)} %c0_ref.1) | copy-start | bytes 1966084
  5.8 44.0 %copy-start.1 = (s32[3]{0:T(128)S(1)}, s32[3]{0:T(128)}, u32[]{:S(2)}) copy-start(s32[3]{0:T(128)} %pad_add_fusion.place_ref) | copy-start | bytes 40
  5.9 44.0 %copy-start.2 = (s32[32]{0:T(128)S(1)}, s32[32]{0:T(128)}, u32[]{:S(2)}) copy-start(s32[32]{0:T(128)} %constant.45.clone.order_ref) | copy-start | bytes 388
  5.9 43.9 %all-to-all-start = ((bf16[8,2,80,1280]{3,2,1,0:T(8,128)(2,1)}), bf16[8,2,80,1280]{3,2,1,0:T(8,128)(2,1)}, u32[]{:S(2)}, u32[]{:S(2)}) async-start(bf16[8,2,80,1280]{3,2,1,0:T(8,128)(2,1)} %get-tuple-element.18), calls=%async_computation | async-start | bytes 6553600 | tf_op jit(solution)/shard_map/all_to_all | solution.py:296
  11.9 15.8 %collective-permute-start.1 = (bf16[272,1280]{1,0:T(8,128)(2,1)S(1)}, bf16[272,1280]{1,0:T(8,128)(2,1)S(1)}, u32[]{:S(2)}, u32[]{:S(2)}) collective-permute-start(bf16[272,1280]{1,0:T(8,128)(2,1)S(1)} %copy-done.3), channel_id=1, source_target_pairs={{0,2},{2,0},{1,3},{3,1},{4,6},{6,4},{5,7},{7,5},{8,10},{10,8},{9,1... | collective-permute-start | bytes 2088968 | tf_op jit(solution)/shard_map/ppermute | solution.py:270
  15.9 24.1 %collective-permute-start = (bf16[272,1280]{1,0:T(8,128)(2,1)S(1)}, bf16[272,1280]{1,0:T(8,128)(2,1)S(1)}, u32[]{:S(2)}, u32[]{:S(2)}) collective-permute-start(bf16[272,1280]{1,0:T(8,128)(2,1)S(1)} %copy-done.3), channel_id=1, source_target_pairs={{0,1},{1,0},{2,3},{3,2},{4,5},{5,4},{6,7},{7,6},{8,9},{9,8},{10,11... | collective-permute-start | bytes 2088968 | tf_op jit(solution)/shard_map/ppermute | solution.py:267
  27.6 22.2 %copy-start.7 = (bf16[272,1280]{1,0:T(8,128)(2,1)}, bf16[272,1280]{1,0:T(8,128)(2,1)S(1)}, u32[]{:S(2)}) copy-start(bf16[272,1280]{1,0:T(8,128)(2,1)S(1)} %collective-permute-done.1.x2_ref) | copy-start | bytes 2088964
  27.6 12.3 %collective-permute-start.2 = (bf16[272,1280]{1,0:T(8,128)(2,1)S(1)}, bf16[272,1280]{1,0:T(8,128)(2,1)}, u32[]{:S(2)}, u32[]{:S(2)}) collective-permute-start(bf16[272,1280]{1,0:T(8,128)(2,1)S(1)} %collective-permute-done.1.x2_ref), channel_id=1, source_target_pairs={{0,1},{1,0},{2,3},{3,2},{4,5},{5,4},{6,7},{7,6},{8,9},{9,8},{10,11... | collective-permute-start | bytes 2088968 | tf_op jit(solution)/shard_map/ppermute | solution.py:267
  34.4 27.3 %collective-permute-start.3 = (bf16[256,1280]{1,0:T(8,128)(2,1)S(1)}, bf16[256,1280]{1,0:T(8,128)(2,1)}, u32[]{:S(2)}, u32[]{:S(2)}) collective-permute-start(bf16[256,1280]{1,0:T(8,128)(2,1)S(1)} %copy-done.6), channel_id=1, source_target_pairs={{0,2},{2,0},{1,3},{3,1},{4,6},{6,4},{5,7},{7,5},{8,10},{10,8},{9,1... | collective-permute-start | bytes 1966088 | tf_op jit(solution)/shard_map/ppermute | solution.py:270
  37.7 34.0 %collective-permute-start.4 = (bf16[256,1280]{1,0:T(8,128)(2,1)S(1)}, bf16[256,1280]{1,0:T(8,128)(2,1)}, u32[]{:S(2)}, u32[]{:S(2)}) collective-permute-start(bf16[256,1280]{1,0:T(8,128)(2,1)S(1)} %copy-done.6), channel_id=1, source_target_pairs={{0,1},{1,0},{2,3},{3,2},{4,5},{5,4},{6,7},{7,6},{8,9},{9,8},{10,11... | collective-permute-start | bytes 1966088 | tf_op jit(solution)/shard_map/ppermute | solution.py:267
  39.9 9.9 %copy-start.8 = (bf16[272,1280]{1,0:T(8,128)(2,1)}, bf16[272,1280]{1,0:T(8,128)(2,1)S(1)}, u32[]{:S(2)}) copy-start(bf16[272,1280]{1,0:T(8,128)(2,1)S(1)} %collective-permute-done.x1_ref) | copy-start | bytes 2088964
  61.6 8.1 %copy-start = (bf16[320,1024]{1,0:T(8,128)(2,1)}, bf16[320,1024]{1,0:T(8,128)(2,1)S(1)}, u32[]{:S(2)}) copy-start(bf16[320,1024]{1,0:T(8,128)(2,1)S(1)} %shard_map.105.from_ref) | copy-start | bytes 1966084
  61.7 10.0 %collective-permute-start.5 = (bf16[256,1280]{1,0:T(8,128)(2,1)}, bf16[256,1280]{1,0:T(8,128)(2,1)}, u32[]{:S(2)}, u32[]{:S(2)}) collective-permute-start(bf16[256,1280]{1,0:T(8,128)(2,1)} %collective-permute-done.3.c2_ref), channel_id=1, source_target_pairs={{0,1},{1,0},{2,3},{3,2},{4,5},{5,4},{6,7},{7,6},{8,9},{9,8},{10,11... | collective-permute-start | bytes 1966088 | tf_op jit(solution)/shard_map/ppermute | solution.py:267
  69.8 9.4 %collective-permute-start.6 = (bf16[2,256,1280]{2,1,0:T(8,128)(2,1)}, bf16[2,256,1280]{2,1,0:T(8,128)(2,1)S(1)}, u32[]{:S(2)}, u32[]{:S(2)}) collective-permute-start(bf16[2,256,1280]{2,1,0:T(8,128)(2,1)} %get-tuple-element.23), channel_id=1, source_target_pairs={{0,1},{1,0},{2,3},{3,2},{4,5},{5,4},{6,7},{7,6},{8,9},{9,8},{10,11... | collective-permute-start | bytes 3932168 | tf_op jit(solution)/shard_map/ppermute | solution.py:267
  75.6 15.7 %all-to-all-start.1 = ((bf16[8,40,1280]{2,1,0:T(8,128)(2,1)}), bf16[8,40,1280]{2,1,0:T(8,128)(2,1)S(1)}, u32[]{:S(2)}, u32[]{:S(2)}) async-start(bf16[8,40,1280]{2,1,0:T(8,128)(2,1)} %bitcast.25), calls=%async_computation.1 | async-start | bytes 1638400 | tf_op jit(solution)/shard_map/all_to_all | solution.py:356
  79.1 17.0 %copy-start.5 = (bf16[2,256,1280]{2,1,0:T(8,128)(2,1)}, bf16[2,256,1280]{2,1,0:T(8,128)(2,1)S(1)}, u32[]{:S(2)}) copy-start(bf16[2,256,1280]{2,1,0:T(8,128)(2,1)S(1)} %collective-permute-done.6) | copy-start | bytes 3932164
  91.3 20.3 %collective-permute-start.7 = (bf16[256,1280]{1,0:T(8,128)(2,1)}, bf16[256,1280]{1,0:T(8,128)(2,1)}, u32[]{:S(2)}, u32[]{:S(2)}) collective-permute-start(bf16[256,1280]{1,0:T(8,128)(2,1)} %fusion.3), channel_id=1, source_target_pairs={{0,2},{2,0},{1,3},{3,1},{4,6},{6,4},{5,7},{7,5},{8,10},{10,8},{9,1... | collective-permute-start | bytes 1966088 | tf_op jit(solution)/shard_map/ppermute | solution.py:270
  96.1 25.3 %copy-start.4 = (bf16[256,1280]{1,0:T(8,128)(2,1)S(1)}, bf16[256,1280]{1,0:T(8,128)(2,1)}, u32[]{:S(2)}) copy-start(bf16[256,1280]{1,0:T(8,128)(2,1)} %patches_ref.1) | copy-start | bytes 1966084
  96.1 15.4 %all-to-all-start.2 = ((bf16[4,40,1280]{2,1,0:T(8,128)(2,1)}), bf16[4,40,1280]{2,1,0:T(8,128)(2,1)S(1)}, u32[]{:S(2)}, u32[]{:S(2)}) async-start(bf16[4,40,1280]{2,1,0:T(8,128)(2,1)} %shard_map.108), calls=%async_computation.2 | async-start | bytes 819200 | tf_op jit(solution)/shard_map/all_to_all | solution.py:360
  112.4 18.0 %all-to-all-start.3 = ((bf16[4,40,1280]{2,1,0:T(8,128)(2,1)}), bf16[4,40,1280]{2,1,0:T(8,128)(2,1)S(1)}, u32[]{:S(2)}, u32[]{:S(2)}) async-start(bf16[4,40,1280]{2,1,0:T(8,128)(2,1)} %shard_map.109), calls=%async_computation.3 | async-start | bytes 819200 | tf_op jit(solution)/shard_map/all_to_all | solution.py:368
  130.5 6.6 %collective-permute-start.9 = (bf16[40,1280]{1,0:T(8,128)(2,1)S(1)}, bf16[40,1280]{1,0:T(8,128)(2,1)S(1)}, u32[]{:S(2)}, u32[]{:S(2)}) collective-permute-start(bf16[40,1280]{1,0:T(8,128)(2,1)S(1)} %bitcast.23), channel_id=1, source_target_pairs={{0,66},{66,0},{130,192},{192,130},{1,67},{67,1},{131,193},{193,131... | collective-permute-start | bytes 307208 | tf_op jit(solution)/shard_map/ppermute | solution.py:373
  132.4 5.7 %collective-permute-start.8 = (bf16[40,1280]{1,0:T(8,128)(2,1)S(1)}, bf16[40,1280]{1,0:T(8,128)(2,1)S(1)}, u32[]{:S(2)}, u32[]{:S(2)}) collective-permute-start(bf16[40,1280]{1,0:T(8,128)(2,1)S(1)} %bitcast.24), channel_id=1, source_target_pairs={{0,64},{2,0},{64,66},{66,2},{128,130},{130,194},{192,128},{194,192... | collective-permute-start | bytes 307208 | tf_op jit(solution)/shard_map/ppermute | solution.py:372
  138.2 13.2 %collective-permute-start.10 = (bf16[80,1280]{1,0:T(8,128)(2,1)S(1)}, bf16[80,1280]{1,0:T(8,128)(2,1)S(1)}, u32[]{:S(2)}, u32[]{:S(2)}) collective-permute-start(bf16[80,1280]{1,0:T(8,128)(2,1)S(1)} %pad_maximum_fusion.1), channel_id=1, source_target_pairs={{0,1},{1,0},{2,3},{3,2},{4,5},{5,4},{6,7},{7,6},{8,9},{9,8},{10,11... | collective-permute-start | bytes 614408 | tf_op jit(solution)/shard_map/ppermute | solution.py:267

commit v3 on v2

--- a/solution.py
+++ b/solution.py
@@ -122,12 +122,19 @@
     x2_ref,
     x3_ref,
     blocks_ref,
+    c0_ref,
+    c1_ref,
+    c2_ref,
+    c3_ref,
     out_ref,
+    grad_ref,
     x_ref,
     weight_ref,
     context_ref,
+    c_ref,
     x_sems,
     sems,
+    c_sems,
     out_sem,
 ):
     scale = HEAD**-0.5 * math.log2(math.e)
@@ -140,7 +147,11 @@
         pltpu.make_async_copy(ref, x_ref.at[part], x_sems.at[part])
         for part, ref in enumerate((x0_ref, x1_ref, x2_ref, x3_ref))
     ]
-    for copy in copies + arrivals:
+    cotangents = [
+        pltpu.make_async_copy(ref, c_ref.at[part * ROWS : (part + 1) * ROWS], c_sems.at[part])
+        for part, ref in enumerate((c0_ref, c1_ref, c2_ref, c3_ref))
+    ]
+    for copy in copies + arrivals + cotangents:
         copy.start()
     for copy in copies + arrivals:
         copy.wait()
@@ -166,24 +177,14 @@
             context_ref[head * HEAD : (head + 1) * HEAD, part * ROWS : (part + 1) * ROWS] = context.astype(BF16)
     store = pltpu.make_async_copy(context_ref, out_ref, out_sem)
     store.start()
-    store.wait()
-
-
-def gradient_kernel(from_ref, c0_ref, c1_ref, c2_ref, c3_ref, grad_ref, context_ref, c_ref, sems):
-    copies = [
-        pltpu.make_async_copy(ref, c_ref.at[part * ROWS : (part + 1) * ROWS], sems.at[part])
-        for part, ref in enumerate((c0_ref, c1_ref, c2_ref, c3_ref))
-    ]
-    copies.append(pltpu.make_async_copy(from_ref, context_ref, sems.at[4]))
-    for copy in copies:
-        copy.start()
-    for copy in copies:
+    for copy in cotangents:
         copy.wait()
     for start in range(0, WIDTH, 256):
         columns = slice(start, start + 256)
         grad_ref[:, columns] = jnp.dot(
             context_ref[...], c_ref[:, columns], preferred_element_type=F32
         ).astype(BF16)
+    store.wait()
 
 
 def project_kernel(
@@ -296,42 +297,43 @@
     blocks = lax.all_to_all(own, FSDP, 0, 0).reshape(16, HEAD, WIDTH)
 
     message_pair = to_pair(message)
+    cotangent_pair = to_pair(out_cotangent)
     message_core = to_core(message)
     cotangent_core = to_core(out_cotangent)
-    message_pair, cotangent_late = lax.optimization_barrier((message_pair, out_cotangent))
     message_both = to_core(message_pair)
-    cotangent_pair = to_pair(cotangent_late)
-
-    context = call(
+    cotangent_both = to_core(cotangent_pair)
+
+    context, grad = call(
         attention_kernel,
-        array(4 * HEAD, 4 * ROWS),
-        [SMEM, SMEM] + [HBM] * 5,
-        HBM,
+        (array(4 * HEAD, 4 * ROWS), array(4 * HEAD, WIDTH)),
+        [SMEM, SMEM] + [HBM] * 9,
+        (HBM, VMEM),
         [
             pltpu.VMEM((4, ROWS + NOTE, WIDTH), BF16),
             pltpu.VMEM((12 * HEAD, WIDTH), BF16),
             pltpu.VMEM((4 * HEAD, 4 * ROWS), BF16),
+            pltpu.VMEM((4 * ROWS, WIDTH), BF16),
             DMA((4,)),
             DMA((12,)),
+            DMA((4,)),
             DMA,
         ],
         limit=52 << 20,
-        flops=2 * 1024 * 1280 * 960 + 4 * 16 * 256 * 256 * 128,
-        read=8 << 20,
-    )(place, orders, message, message_core, message_pair, message_both, blocks)
-
-    context, cotangent_pair = lax.optimization_barrier((context, cotangent_pair))
-    cotangent_both = to_core(cotangent_pair)
-
-    grad = call(
-        gradient_kernel,
-        array(4 * HEAD, WIDTH),
-        [HBM] * 5,
-        VMEM,
-        [pltpu.VMEM((4 * HEAD, 4 * ROWS), BF16), pltpu.VMEM((4 * ROWS, WIDTH), BF16), DMA((5,))],
-        flops=2 * 1024 * 1280 * 320,
-        read=4 << 20,
-    )(context, out_cotangent, cotangent_core, cotangent_pair, cotangent_both)
+        flops=2 * 1024 * 1280 * 1280 + 4 * 16 * 256 * 256 * 128,
+        read=12 << 20,
+    )(
+        place,
+        orders,
+        message,
+        message_core,
+        message_pair,
+        message_both,
+        blocks,
+        out_cotangent,
+        cotangent_core,
+        cotangent_pair,
+        cotangent_both,
+    )
 
     keep_out, send_out = call(
         project_kernel,
@@ -351,35 +353,29 @@
         read=6 << 20,
     )(place, orders, context, blocks)
 
+    grad = lax.all_to_all(grad.reshape(8, 40, WIDTH), FSDP, 0, 0)
+    grad, keep_late = lax.optimization_barrier((grad, keep_out))
+    grad = sum_of(grad, Z_QUAD)
     from_core = to_core(send_out)
     for_pair = (keep_out[1].astype(F32) + from_core[1].astype(F32)).astype(BF16)
-    grad = lax.all_to_all(grad.reshape(8, 40, WIDTH), FSDP, 0, 0)
-    grad, for_pair = lax.optimization_barrier((grad, for_pair))
+    grad = lax.all_to_all(grad, "z_quad", 0, 0)
+    grad, from_core_late = lax.optimization_barrier((grad, from_core))
+    grad = sum_of(grad, Y_HI)
     from_pair = to_pair(for_pair)
-    grad = sum_of(grad, Y_HI)
-    grad = lax.all_to_all(grad, "y_hi", 0, 0)
-    grad, from_pair = lax.optimization_barrier((grad, from_pair))
-    grad = sum_of(grad, Z_QUAD)
-
-    projected = keep_out[0].astype(F32) + from_core[0].astype(F32) + from_pair.astype(F32)
+    projected = keep_late[0].astype(F32) + from_core_late[0].astype(F32) + from_pair.astype(F32)
     alive = lax.iota(jnp.int32, ROWS) < tile_counts[0] * TILE
     output = jnp.where(alive[:, None], patches.astype(F32) + projected, F32(0.0)).astype(BF16)
-
-    grad = lax.all_to_all(grad, "z_quad", 0, 0)
+    grad = lax.all_to_all(grad, "y_hi", 0, 0)
     grad, output = lax.optimization_barrier((grad, output))
     grad = sum_of(grad, 1)[0]
 
     first = lax.ppermute(grad, ("x", "z_pair"), TO_OWNER)
     second = lax.ppermute(grad, ("x", "z_pair"), ACROSS)
     owner = ((x == 0) | (x == 3)) == (half == 1)
-    near = jnp.where(owner, grad, first)
-    far = jnp.where(owner, first, second)
-    even = x % 2 == 0
-    head_grad = jnp.concatenate([jnp.where(even, near, far), jnp.where(even, far, near)])
-    other_grad = to_core(head_grad)
-    proj_grad = jnp.concatenate(
-        [jnp.where(core == 0, head_grad, other_grad), jnp.where(core == 0, other_grad, head_grad)]
-    )
+    two = lax.broadcasted_iota(jnp.int32, (2, 1, 1), 0)
+    head_grad = jnp.where(two == x % 2, jnp.where(owner, grad, first), jnp.where(owner, first, second))
+    head_grad = head_grad.reshape(HEAD, WIDTH)
+    proj_grad = jnp.where(two == core, head_grad, to_core(head_grad)).reshape(2 * HEAD, WIDTH)
     return output, proj_grad
 
 

time: 153 us -> 143 us (0.935)
  waiting for transfers between devices: 47.6 us -> 25.7 us
  starting transfers between devices: 72.1 us -> 83.5 us
    all_to_all x1, waiting for transfers between devices: 9.83 us -> 0.01 us  [shards(): blocks = lax.all_to_all(own, FSDP, 0, 0).reshape(16, HEAD, WIDTH)]
    all_to_all x1, waiting for transfers between devices: 9.13 us -> 0.02 us  [shards(): grad = lax.all_to_all(grad, 'y_hi', 0, 0)]
    ppermute x6, starting transfers between devices: 32 us -> 38.9 us  [to_core(): return lax.ppermute(value, 'core', CORE_SWAP)]
    all_to_all x1, waiting for transfers between devices: 11 us -> 5.33 us  [shards(): grad = lax.all_to_all(grad.reshape(8, 40, WIDTH), FSDP, 0, 0)]
    ppermute x1, starting transfers between devices: 1.94 us -> 6.98 us  [shards(): second = lax.ppermute(grad, ('x', 'z_pair'), ACROSS)]
    ppermute x3, waiting for transfers between devices: 6.43 us -> 10 us  [to_pair(): return lax.ppermute(value, 'z_pair', PAIR_SWAP)]
    ppermute x1, waiting for transfers between devices: 2.7 us -> 0.01 us  [shards(): second = lax.ppermute(grad, ('x', 'z_pair'), ACROSS)]
    ppermute x1, waiting for transfers between devices: 1.05 us -> 3.3 us  [shards(): first = lax.ppermute(grad, ('x', 'z_pair'), TO_OWNER)]
  transfers between devices with their start and end apart: 15 -> 15, of which waited for: 8 -> 7; matrix products, arithmetic and copies ran while one was open for 2% -> 3% of each run, Pallas kernels for 14% -> 4%
where the time goes in v3:
time: 143 us; the launch traced here: 142 us
  starting transfers between devices  83.5 us (58%)
  waiting for transfers between devices  25.7 us (18%)
  Pallas kernels  24.3 us (17%)
  other arithmetic  5.96 us (4%)
  between operations  1.54 us (1%)
    ppermute x6, starting transfers between devices, to_core(): return lax.ppermute(value, 'core', CORE_SWAP)  38.9 us
    pallas_call x1, Pallas kernels, shards(): call(attention_kernel, (array(4 * HEAD, 4 * ROWS), array(4 * HEAD, WIDTH)...  14.2 us
    ppermute x3, waiting for transfers between devices, to_pair(): return lax.ppermute(value, 'z_pair', PAIR_SWAP)  10 us
    all_to_all x1, starting transfers between devices, shards(): grad = lax.all_to_all(grad, 'z_quad', 0, 0)  9.38 us
    ppermute x3, starting transfers between devices, to_pair(): return lax.ppermute(value, 'z_pair', PAIR_SWAP)  9.12 us
    ppermute x1, starting transfers between devices, shards(): second = lax.ppermute(grad, ('x', 'z_pair'), ACROSS)  6.98 us
    all_to_all x1, starting transfers between devices, shards(): grad = lax.all_to_all(grad, 'y_hi', 0, 0)  6.12 us
    all_to_all x1, starting transfers between devices, shards(): blocks = lax.all_to_all(own, FSDP, 0, 0).reshape(16, HEAD, WIDTH)  6.01 us
  transfers between devices with their start and end apart: 15, of which 7 were waited for; matrix products, arithmetic and copies ran while one was open for 3% of the time, Pallas kernels for 4%

profile of v3, /device:TPU:1, one launch (start us, length us, event | category | flops | bytes accessed | tf_op | source)
XLA Modules:
  0.0 142.1 jit_solution(5337537029399059215)
XLA Ops:
  1.3 0.6 pad_add_fusion.place_ref
  1.9 3.9 %shard_map.104 = (bf16[272,1280]{1,0:T(8,128)(2,1)}, bf16[8,2,80,1280]{3,2,1,0:T(8,128)(2,1)}) custom-call(s32[3]{0:T(128)} %pad_add_fusion.place_ref, s32[32]{0:T(128)} %constant.44.clone.sends_ref, s32[1]{0:T(128)S(6)} %copy.11.count_ref, bf16[256,1280]{1,0:T(8,128)(2,1)} %patches_ref.1, f32[1280]{0:T(1024)} %gain_ref.1, s32[256]{0:T(256)} %images_ref.1, ...), custom_call_target="tpu_custom_call" | custom-call | bytes 6291456 | tf_op jit(solution)/shard_map/pallas_call | solution.py:273
  5.8 0.0 copy-start.4
  5.8 0.0 copy-start.2
  5.8 0.0 copy-start
  5.9 0.0 copy-start.1
  5.9 6.0 %all-to-all-start = ((bf16[8,2,80,1280]{3,2,1,0:T(8,128)(2,1)}), bf16[8,2,80,1280]{3,2,1,0:T(8,128)(2,1)}, u32[]{:S(2)}, u32[]{:S(2)}) async-start(bf16[8,2,80,1280]{3,2,1,0:T(8,128)(2,1)} %get-tuple-element.15), calls=%async_computation | async-start | bytes 6553600 | tf_op jit(solution)/shard_map/all_to_all | solution.py:297
  11.9 0.0 copy-done.4
  11.9 4.0 %collective-permute-start.1 = (bf16[272,1280]{1,0:T(8,128)(2,1)S(1)}, bf16[272,1280]{1,0:T(8,128)(2,1)S(1)}, u32[]{:S(2)}, u32[]{:S(2)}) collective-permute-start(bf16[272,1280]{1,0:T(8,128)(2,1)S(1)} %copy-done.4), channel_id=1, source_target_pairs={{0,2},{2,0},{1,3},{3,1},{4,6},{6,4},{5,7},{7,5},{8,10},{10,8},{9,1... | collective-permute-start | bytes 2088968 | tf_op jit(solution)/shard_map/ppermute | solution.py:271
  15.9 0.0 copy-done.2
  15.9 1.9 %collective-permute-start.4 = (bf16[256,1280]{1,0:T(8,128)(2,1)S(1)}, bf16[256,1280]{1,0:T(8,128)(2,1)S(1)}, u32[]{:S(2)}, u32[]{:S(2)}) collective-permute-start(bf16[256,1280]{1,0:T(8,128)(2,1)S(1)} %copy-done.2), channel_id=1, source_target_pairs={{0,2},{2,0},{1,3},{3,1},{4,6},{6,4},{5,7},{7,5},{8,10},{10,8},{9,1... | collective-permute-start | bytes 1966088 | tf_op jit(solution)/shard_map/ppermute | solution.py:271
  17.8 7.3 %collective-permute-start = (bf16[272,1280]{1,0:T(8,128)(2,1)S(1)}, bf16[272,1280]{1,0:T(8,128)(2,1)S(1)}, u32[]{:S(2)}, u32[]{:S(2)}) collective-permute-start(bf16[272,1280]{1,0:T(8,128)(2,1)S(1)} %copy-done.4), channel_id=1, source_target_pairs={{0,1},{1,0},{2,3},{3,2},{4,5},{5,4},{6,7},{7,6},{8,9},{9,8},{10,11... | collective-permute-start | bytes 2088968 | tf_op jit(solution)/shard_map/ppermute | solution.py:268
  25.2 2.5 %collective-permute-done.1.x2_ref = bf16[272,1280]{1,0:T(8,128)(2,1)S(1)} collective-permute-done((bf16[272,1280]{1,0:T(8,128)(2,1)S(1)}, bf16[272,1280]{1,0:T(8,128)(2,1)S(1)}, u32[]{:S(2)}, u32[]{:S(2)}) %collective-permute-start.1) | collective-permute-done | bytes 696352 | tf_op jit(solution)/shard_map/ppermute | solution.py:271
  27.6 0.0 copy-start.5
  27.6 12.1 %collective-permute-start.2 = (bf16[272,1280]{1,0:T(8,128)(2,1)S(1)}, bf16[272,1280]{1,0:T(8,128)(2,1)}, u32[]{:S(2)}, u32[]{:S(2)}) collective-permute-start(bf16[272,1280]{1,0:T(8,128)(2,1)S(1)} %collective-permute-done.1.x2_ref), channel_id=1, source_target_pairs={{0,1},{1,0},{2,3},{3,2},{4,5},{5,4},{6,7},{7,6},{8,9},{9,8},{10,11... | collective-permute-start | bytes 2088968 | tf_op jit(solution)/shard_map/ppermute | solution.py:268
  39.7 1.9 %collective-permute-start.3 = (bf16[256,1280]{1,0:T(8,128)(2,1)S(1)}, bf16[256,1280]{1,0:T(8,128)(2,1)S(1)}, u32[]{:S(2)}, u32[]{:S(2)}) collective-permute-start(bf16[256,1280]{1,0:T(8,128)(2,1)S(1)} %copy-done.2), channel_id=1, source_target_pairs={{0,1},{1,0},{2,3},{3,2},{4,5},{5,4},{6,7},{7,6},{8,9},{9,8},{10,11... | collective-permute-start | bytes 1966088 | tf_op jit(solution)/shard_map/ppermute | solution.py:268
  41.6 0.0 collective-permute-done.4.c2_ref
  41.7 0.0 copy-start.7
  41.7 6.7 %collective-permute-start.5 = (bf16[256,1280]{1,0:T(8,128)(2,1)S(1)}, bf16[256,1280]{1,0:T(8,128)(2,1)S(1)}, u32[]{:S(2)}, u32[]{:S(2)}) collective-permute-start(bf16[256,1280]{1,0:T(8,128)(2,1)S(1)} %collective-permute-done.4.c2_ref), channel_id=1, source_target_pairs={{0,1},{1,0},{2,3},{3,2},{4,5},{5,4},{6,7},{7,6},{8,9},{9,8},{10,11... | collective-permute-start | bytes 1966088 | tf_op jit(solution)/shard_map/ppermute | solution.py:268
  48.4 0.0 collective-permute-done.3.c1_ref
  48.4 0.0 collective-permute-done.x1_ref
  48.4 0.0 copy-done.7
  48.4 0.0 copy-start.6
  48.4 1.7 %collective-permute-done.5.c3_ref = bf16[256,1280]{1,0:T(8,128)(2,1)S(1)} collective-permute-done((bf16[256,1280]{1,0:T(8,128)(2,1)S(1)}, bf16[256,1280]{1,0:T(8,128)(2,1)S(1)}, u32[]{:S(2)}, u32[]{:S(2)}) %collective-permute-start.5) | collective-permute-done | bytes 655392 | tf_op jit(solution)/shard_map/ppermute | solution.py:268
  50.1 0.0 copy-start.8
  50.1 0.8 copy-done.8
  50.9 0.0 collective-permute-done.2.x3_ref
  50.9 0.0 all-to-all-done
  50.9 0.0 copy-done.6
  50.9 0.0 copy-done.5
  50.9 0.0 copy-done
  50.9 0.0 copy-done.1
  51.0 14.2 %shard_map.105 = (bf16[320,1024]{1,0:T(8,128)(2,1)S(1)}, bf16[320,1280]{1,0:T(8,128)(2,1)}) custom-call(s32[3]{0:T(128)S(1)} %copy-done, s32[32]{0:T(128)S(1)} %copy-done.1, bf16[272,1280]{1,0:T(8,128)(2,1)} %get-tuple-element.14.x0_ref, bf16[272,1280]{1,0:T(8,128)(2,1)} %copy-done.6, bf16[272,1280]{1,0:T(8,128)(2,1)} %copy-done.5, ...), custom_call_target="tpu_custom_call" | custom-call | flops 3892314112 | bytes 12582912 | tf_op jit(solution)/shard_map/pallas_call | solution.py:306
  65.2 5.1 %all-to-all-start.1 = ((bf16[8,40,1280]{2,1,0:T(8,128)(2,1)}), bf16[8,40,1280]{2,1,0:T(8,128)(2,1)S(1)}, u32[]{:S(2)}, u32[]{:S(2)}) async-start(bf16[8,40,1280]{2,1,0:T(8,128)(2,1)} %bitcast.33), calls=%async_computation.1 | async-start | bytes 1638400 | tf_op jit(solution)/shard_map/all_to_all | solution.py:356
  70.3 4.4 %shard_map.106 = (bf16[2,256,1280]{2,1,0:T(8,128)(2,1)S(1)}, bf16[2,256,1280]{2,1,0:T(8,128)(2,1)}) custom-call(s32[3]{0:T(128)S(1)} %copy-done, s32[32]{0:T(128)S(1)} %copy-done.1, bf16[320,1024]{1,0:T(8,128)(2,1)S(1)} %get-tuple-element.17.from_ref, bf16[16,80,1280]{2,1,0:T(8,128)(2,1)} %bitcast.6.blocks_ref), custom_call_target="tpu_custom_call" | custom-call | flops 838860800 | bytes 6291456 | tf_op jit(solution)/shard_map/pallas_call | solution.py:338
  74.7 2.6 %collective-permute-start.6 = (bf16[2,256,1280]{2,1,0:T(8,128)(2,1)}, bf16[2,256,1280]{2,1,0:T(8,128)(2,1)}, u32[]{:S(2)}, u32[]{:S(2)}) collective-permute-start(bf16[2,256,1280]{2,1,0:T(8,128)(2,1)} %get-tuple-element.20), channel_id=1, source_target_pairs={{0,1},{1,0},{2,3},{3,2},{4,5},{5,4},{6,7},{7,6},{8,9},{9,8},{10,11... | collective-permute-start | bytes 3932168 | tf_op jit(solution)/shard_map/ppermute | solution.py:268
  77.3 5.3 %all-to-all-done.1.terms_ref = bf16[8,40,1280]{2,1,0:T(8,128)(2,1)S(1)} async-done(((bf16[8,40,1280]{2,1,0:T(8,128)(2,1)}), bf16[8,40,1280]{2,1,0:T(8,128)(2,1)S(1)}, u32[]{:S(2)}, u32[]{:S(2)}) %all-to-all-start.1) | async-done | bytes 819232 | tf_op jit(solution)/shard_map/all_to_all | solution.py:356
  82.6 0.9 shard_map.107
  83.5 9.4 %all-to-all-start.2 = ((bf16[4,40,1280]{2,1,0:T(8,128)(2,1)}), bf16[4,40,1280]{2,1,0:T(8,128)(2,1)S(1)}, u32[]{:S(2)}, u32[]{:S(2)}) async-start(bf16[4,40,1280]{2,1,0:T(8,128)(2,1)} %shard_map.107), calls=%async_computation.2 | async-start | bytes 819200 | tf_op jit(solution)/shard_map/all_to_all | solution.py:361
  92.8 0.0 collective-permute-done.6
  92.9 2.1 %fusion.3 = bf16[256,1280]{1,0:T(8,128)(2,1)} fusion(bf16[2,256,1280]{2,1,0:T(8,128)(2,1)} %collective-permute-done.6, bf16[2,256,1280]{2,1,0:T(8,128)(2,1)S(1)} %get-tuple-element.22), kind=kLoop, calls=%fused_computation.5 | loop fusion | flops 1310720 | bytes 1966080 | tf_op jit(solution)/shard_map/convert_element_type | solution.py:360
  94.9 0.0 copy-start.3
  94.9 3.2 %collective-permute-start.7 = (bf16[256,1280]{1,0:T(8,128)(2,1)}, bf16[256,1280]{1,0:T(8,128)(2,1)S(1)}, u32[]{:S(2)}, u32[]{:S(2)}) collective-permute-start(bf16[256,1280]{1,0:T(8,128)(2,1)} %fusion.3), channel_id=1, source_target_pairs={{0,2},{2,0},{1,3},{3,1},{4,6},{6,4},{5,7},{7,5},{8,10},{10,8},{9,1... | collective-permute-start | bytes 1966088 | tf_op jit(solution)/shard_map/ppermute | solution.py:271
  98.1 4.5 %all-to-all-done.2.terms_ref = bf16[4,40,1280]{2,1,0:T(8,128)(2,1)S(1)} async-done(((bf16[4,40,1280]{2,1,0:T(8,128)(2,1)}), bf16[4,40,1280]{2,1,0:T(8,128)(2,1)S(1)}, u32[]{:S(2)}, u32[]{:S(2)}) %all-to-all-start.2) | async-done | bytes 409632 | tf_op jit(solution)/shard_map/all_to_all | solution.py:361
  102.6 0.8 shard_map.108
  103.4 6.1 %all-to-all-start.3 = ((bf16[4,40,1280]{2,1,0:T(8,128)(2,1)}), bf16[4,40,1280]{2,1,0:T(8,128)(2,1)S(1)}, u32[]{:S(2)}, u32[]{:S(2)}) async-start(bf16[4,40,1280]{2,1,0:T(8,128)(2,1)} %shard_map.108), calls=%async_computation.3 | async-start | bytes 819200 | tf_op jit(solution)/shard_map/all_to_all | solution.py:368
  109.5 7.5 %collective-permute-done.7 = bf16[256,1280]{1,0:T(8,128)(2,1)S(1)} collective-permute-done((bf16[256,1280]{1,0:T(8,128)(2,1)}, bf16[256,1280]{1,0:T(8,128)(2,1)S(1)}, u32[]{:S(2)}, u32[]{:S(2)}) %collective-permute-start.7) | collective-permute-done | bytes 655392 | tf_op jit(solution)/shard_map/ppermute | solution.py:271
  117.0 0.0 copy-done.3
  117.0 2.3 %fusion.2 = bf16[256,1280]{1,0:T(8,128)(2,1)} fusion(bf16[256,1280]{1,0:T(8,128)(2,1)S(1)} %collective-permute-done.7, bf16[256,1280]{1,0:T(8,128)(2,1)S(1)} %copy-done.3, bf16[2,256,1280]{2,1,0:T(8,128)(2,1)} %collective-permute-done.6, bf16[2,256,1280]{2,1,0:T(8,128)(2,1)S(1)} %get-tuple-element.22, pred[256]{0:T(512)(128)(4,1)S(1)} %iota_compare_fusion), kind=kLoop, calls=%fused_computation.3 | loop fusion | flops 2949120 | bytes 3277056 | tf_op jit(solution)/shard_map/convert_element_type | solution.py:367
  119.3 0.0 all-to-all-done.3.terms_ref
  119.4 0.1 shard_map.109
  119.4 7.0 %collective-permute-start.9 = (bf16[40,1280]{1,0:T(8,128)(2,1)S(1)}, bf16[40,1280]{1,0:T(8,128)(2,1)S(1)}, u32[]{:S(2)}, u32[]{:S(2)}) collective-permute-start(bf16[40,1280]{1,0:T(8,128)(2,1)S(1)} %bitcast.30), channel_id=1, source_target_pairs={{0,66},{66,0},{130,192},{192,130},{1,67},{67,1},{131,193},{193,131... | collective-permute-start | bytes 307208 | tf_op jit(solution)/shard_map/ppermute | solution.py:373
  126.4 1.9 %collective-permute-start.8 = (bf16[40,1280]{1,0:T(8,128)(2,1)S(1)}, bf16[40,1280]{1,0:T(8,128)(2,1)S(1)}, u32[]{:S(2)}, u32[]{:S(2)}) collective-permute-start(bf16[40,1280]{1,0:T(8,128)(2,1)S(1)} %bitcast.31), channel_id=1, source_target_pairs={{0,64},{2,0},{64,66},{66,2},{128,130},{130,194},{192,128},{194,192... | collective-permute-start | bytes 307208 | tf_op jit(solution)/shard_map/ppermute | solution.py:372
  128.3 0.1 broadcast_in_dim.66
  128.4 0.1 broadcast_in_dim.67
  128.5 0.0 collective-permute-done.9
  128.5 3.3 %collective-permute-done.8 = bf16[40,1280]{1,0:T(8,128)(2,1)S(1)} collective-permute-done((bf16[40,1280]{1,0:T(8,128)(2,1)S(1)}, bf16[40,1280]{1,0:T(8,128)(2,1)S(1)}, u32[]{:S(2)}, u32[]{:S(2)}) %collective-permute-start.8) | collective-permute-done | bytes 102432 | tf_op jit(solution)/shard_map/ppermute | solution.py:372
  131.8 0.1 bitcast_select_fusion.1
  131.9 8.3 %collective-permute-start.10 = (bf16[80,1280]{1,0:T(8,128)(2,1)S(1)}, bf16[80,1280]{1,0:T(8,128)(2,1)S(1)}, u32[]{:S(2)}, u32[]{:S(2)}) collective-permute-start(bf16[80,1280]{1,0:T(8,128)(2,1)S(1)} %bitcast_select_fusion.1), channel_id=1, source_target_pairs={{0,1},{1,0},{2,3},{3,2},{4,5},{5,4},{6,7},{7,6},{8,9},{9,8},{10,11... | collective-permute-start | bytes 614408 | tf_op jit(solution)/shard_map/ppermute | solution.py:268
  140.2 0.1 broadcast_in_dim.63
  140.3 0.1 broadcast_in_dim.64
  140.4 0.9 collective-permute-done.10
  141.3 0.9 bitcast_select_fusion
  (4 shorter events, 0.0 us)
Async XLA Ops:
  5.8 6.1 %copy-start.4 = (bf16[272,1280]{1,0:T(8,128)(2,1)S(1)}, bf16[272,1280]{1,0:T(8,128)(2,1)}, u32[]{:S(2)}) copy-start(bf16[272,1280]{1,0:T(8,128)(2,1)} %get-tuple-element.14.x0_ref) | copy-start | bytes 2088964
  5.8 10.1 %copy-start.2 = (bf16[256,1280]{1,0:T(8,128)(2,1)S(1)}, bf16[256,1280]{1,0:T(8,128)(2,1)}, u32[]{:S(2)}) copy-start(bf16[256,1280]{1,0:T(8,128)(2,1)} %c0_ref.1) | copy-start | bytes 1966084
  5.8 45.1 %copy-start = (s32[3]{0:T(128)S(1)}, s32[3]{0:T(128)}, u32[]{:S(2)}) copy-start(s32[3]{0:T(128)} %pad_add_fusion.place_ref) | copy-start | bytes 40
  5.9 45.1 %copy-start.1 = (s32[32]{0:T(128)S(1)}, s32[32]{0:T(128)}, u32[]{:S(2)}) copy-start(s32[32]{0:T(128)} %constant.45.clone.order_ref) | copy-start | bytes 388
  5.9 45.0 %all-to-all-start = ((bf16[8,2,80,1280]{3,2,1,0:T(8,128)(2,1)}), bf16[8,2,80,1280]{3,2,1,0:T(8,128)(2,1)}, u32[]{:S(2)}, u32[]{:S(2)}) async-start(bf16[8,2,80,1280]{3,2,1,0:T(8,128)(2,1)} %get-tuple-element.15), calls=%async_computation | async-start | bytes 6553600 | tf_op jit(solution)/shard_map/all_to_all | solution.py:297
  11.9 15.8 %collective-permute-start.1 = (bf16[272,1280]{1,0:T(8,128)(2,1)S(1)}, bf16[272,1280]{1,0:T(8,128)(2,1)S(1)}, u32[]{:S(2)}, u32[]{:S(2)}) collective-permute-start(bf16[272,1280]{1,0:T(8,128)(2,1)S(1)} %copy-done.4), channel_id=1, source_target_pairs={{0,2},{2,0},{1,3},{3,1},{4,6},{6,4},{5,7},{7,5},{8,10},{10,8},{9,1... | collective-permute-start | bytes 2088968 | tf_op jit(solution)/shard_map/ppermute | solution.py:271
  15.9 25.8 %collective-permute-start.4 = (bf16[256,1280]{1,0:T(8,128)(2,1)S(1)}, bf16[256,1280]{1,0:T(8,128)(2,1)S(1)}, u32[]{:S(2)}, u32[]{:S(2)}) collective-permute-start(bf16[256,1280]{1,0:T(8,128)(2,1)S(1)} %copy-done.2), channel_id=1, source_target_pairs={{0,2},{2,0},{1,3},{3,1},{4,6},{6,4},{5,7},{7,5},{8,10},{10,8},{9,1... | collective-permute-start | bytes 1966088 | tf_op jit(solution)/shard_map/ppermute | solution.py:271
  17.8 30.6 %collective-permute-start = (bf16[272,1280]{1,0:T(8,128)(2,1)S(1)}, bf16[272,1280]{1,0:T(8,128)(2,1)S(1)}, u32[]{:S(2)}, u32[]{:S(2)}) collective-permute-start(bf16[272,1280]{1,0:T(8,128)(2,1)S(1)} %copy-done.4), channel_id=1, source_target_pairs={{0,1},{1,0},{2,3},{3,2},{4,5},{5,4},{6,7},{7,6},{8,9},{9,8},{10,11... | collective-permute-start | bytes 2088968 | tf_op jit(solution)/shard_map/ppermute | solution.py:268
  27.6 23.3 %copy-start.5 = (bf16[272,1280]{1,0:T(8,128)(2,1)}, bf16[272,1280]{1,0:T(8,128)(2,1)S(1)}, u32[]{:S(2)}) copy-start(bf16[272,1280]{1,0:T(8,128)(2,1)S(1)} %collective-permute-done.1.x2_ref) | copy-start | bytes 2088964
  27.6 23.3 %collective-permute-start.2 = (bf16[272,1280]{1,0:T(8,128)(2,1)S(1)}, bf16[272,1280]{1,0:T(8,128)(2,1)}, u32[]{:S(2)}, u32[]{:S(2)}) collective-permute-start(bf16[272,1280]{1,0:T(8,128)(2,1)S(1)} %collective-permute-done.1.x2_ref), channel_id=1, source_target_pairs={{0,1},{1,0},{2,3},{3,2},{4,5},{5,4},{6,7},{7,6},{8,9},{9,8},{10,11... | collective-permute-start | bytes 2088968 | tf_op jit(solution)/shard_map/ppermute | solution.py:268
  39.7 8.7 %collective-permute-start.3 = (bf16[256,1280]{1,0:T(8,128)(2,1)S(1)}, bf16[256,1280]{1,0:T(8,128)(2,1)S(1)}, u32[]{:S(2)}, u32[]{:S(2)}) collective-permute-start(bf16[256,1280]{1,0:T(8,128)(2,1)S(1)} %copy-done.2), channel_id=1, source_target_pairs={{0,1},{1,0},{2,3},{3,2},{4,5},{5,4},{6,7},{7,6},{8,9},{9,8},{10,11... | collective-permute-start | bytes 1966088 | tf_op jit(solution)/shard_map/ppermute | solution.py:268
  41.7 6.7 %copy-start.7 = (bf16[256,1280]{1,0:T(8,128)(2,1)}, bf16[256,1280]{1,0:T(8,128)(2,1)S(1)}, u32[]{:S(2)}) copy-start(bf16[256,1280]{1,0:T(8,128)(2,1)S(1)} %collective-permute-done.4.c2_ref) | copy-start | bytes 1966084
  41.7 8.4 %collective-permute-start.5 = (bf16[256,1280]{1,0:T(8,128)(2,1)S(1)}, bf16[256,1280]{1,0:T(8,128)(2,1)S(1)}, u32[]{:S(2)}, u32[]{:S(2)}) collective-permute-start(bf16[256,1280]{1,0:T(8,128)(2,1)S(1)} %collective-permute-done.4.c2_ref), channel_id=1, source_target_pairs={{0,1},{1,0},{2,3},{3,2},{4,5},{5,4},{6,7},{7,6},{8,9},{9,8},{10,11... | collective-permute-start | bytes 1966088 | tf_op jit(solution)/shard_map/ppermute | solution.py:268
  48.4 2.5 %copy-start.6 = (bf16[272,1280]{1,0:T(8,128)(2,1)}, bf16[272,1280]{1,0:T(8,128)(2,1)S(1)}, u32[]{:S(2)}) copy-start(bf16[272,1280]{1,0:T(8,128)(2,1)S(1)} %collective-permute-done.x1_ref) | copy-start | bytes 2088964
  50.1 0.8 copy-start.8
  65.2 17.4 %all-to-all-start.1 = ((bf16[8,40,1280]{2,1,0:T(8,128)(2,1)}), bf16[8,40,1280]{2,1,0:T(8,128)(2,1)S(1)}, u32[]{:S(2)}, u32[]{:S(2)}) async-start(bf16[8,40,1280]{2,1,0:T(8,128)(2,1)} %bitcast.33), calls=%async_computation.1 | async-start | bytes 1638400 | tf_op jit(solution)/shard_map/all_to_all | solution.py:356
  74.7 18.1 %collective-permute-start.6 = (bf16[2,256,1280]{2,1,0:T(8,128)(2,1)}, bf16[2,256,1280]{2,1,0:T(8,128)(2,1)}, u32[]{:S(2)}, u32[]{:S(2)}) collective-permute-start(bf16[2,256,1280]{2,1,0:T(8,128)(2,1)} %get-tuple-element.20), channel_id=1, source_target_pairs={{0,1},{1,0},{2,3},{3,2},{4,5},{5,4},{6,7},{7,6},{8,9},{9,8},{10,11... | collective-permute-start | bytes 3932168 | tf_op jit(solution)/shard_map/ppermute | solution.py:268
  83.5 19.1 %all-to-all-start.2 = ((bf16[4,40,1280]{2,1,0:T(8,128)(2,1)}), bf16[4,40,1280]{2,1,0:T(8,128)(2,1)S(1)}, u32[]{:S(2)}, u32[]{:S(2)}) async-start(bf16[4,40,1280]{2,1,0:T(8,128)(2,1)} %shard_map.107), calls=%async_computation.2 | async-start | bytes 819200 | tf_op jit(solution)/shard_map/all_to_all | solution.py:361
  94.9 22.1 %copy-start.3 = (bf16[256,1280]{1,0:T(8,128)(2,1)S(1)}, bf16[256,1280]{1,0:T(8,128)(2,1)}, u32[]{:S(2)}) copy-start(bf16[256,1280]{1,0:T(8,128)(2,1)} %patches_ref.1) | copy-start | bytes 1966084
  94.9 22.1 %collective-permute-start.7 = (bf16[256,1280]{1,0:T(8,128)(2,1)}, bf16[256,1280]{1,0:T(8,128)(2,1)S(1)}, u32[]{:S(2)}, u32[]{:S(2)}) collective-permute-start(bf16[256,1280]{1,0:T(8,128)(2,1)} %fusion.3), channel_id=1, source_target_pairs={{0,2},{2,0},{1,3},{3,1},{4,6},{6,4},{5,7},{7,5},{8,10},{10,8},{9,1... | collective-permute-start | bytes 1966088 | tf_op jit(solution)/shard_map/ppermute | solution.py:271
  103.4 15.9 %all-to-all-start.3 = ((bf16[4,40,1280]{2,1,0:T(8,128)(2,1)}), bf16[4,40,1280]{2,1,0:T(8,128)(2,1)S(1)}, u32[]{:S(2)}, u32[]{:S(2)}) async-start(bf16[4,40,1280]{2,1,0:T(8,128)(2,1)} %shard_map.108), calls=%async_computation.3 | async-start | bytes 819200 | tf_op jit(solution)/shard_map/all_to_all | solution.py:368
  119.4 9.1 %collective-permute-start.9 = (bf16[40,1280]{1,0:T(8,128)(2,1)S(1)}, bf16[40,1280]{1,0:T(8,128)(2,1)S(1)}, u32[]{:S(2)}, u32[]{:S(2)}) collective-permute-start(bf16[40,1280]{1,0:T(8,128)(2,1)S(1)} %bitcast.30), channel_id=1, source_target_pairs={{0,66},{66,0},{130,192},{192,130},{1,67},{67,1},{131,193},{193,131... | collective-permute-start | bytes 307208 | tf_op jit(solution)/shard_map/ppermute | solution.py:373
  126.4 5.4 %collective-permute-start.8 = (bf16[40,1280]{1,0:T(8,128)(2,1)S(1)}, bf16[40,1280]{1,0:T(8,128)(2,1)S(1)}, u32[]{:S(2)}, u32[]{:S(2)}) collective-permute-start(bf16[40,1280]{1,0:T(8,128)(2,1)S(1)} %bitcast.31), channel_id=1, source_target_pairs={{0,64},{2,0},{64,66},{66,2},{128,130},{130,194},{192,128},{194,192... | collective-permute-start | bytes 307208 | tf_op jit(solution)/shard_map/ppermute | solution.py:372
  131.9 9.4 %collective-permute-start.10 = (bf16[80,1280]{1,0:T(8,128)(2,1)S(1)}, bf16[80,1280]{1,0:T(8,128)(2,1)S(1)}, u32[]{:S(2)}, u32[]{:S(2)}) collective-permute-start(bf16[80,1280]{1,0:T(8,128)(2,1)S(1)} %bitcast_select_fusion.1), channel_id=1, source_target_pairs={{0,1},{1,0},{2,3},{3,2},{4,5},{5,4},{6,7},{7,6},{8,9},{9,8},{10,11... | collective-permute-start | bytes 614408 | tf_op jit(solution)/shard_map/ppermute | solution.py:268

commit v4 on v3

--- a/solution.py
+++ b/solution.py
@@ -57,6 +57,10 @@
     (2 * x + half, 2 * x + (1 - half) if owns(x, half) else 2 * (x ^ 1) + half) for x in range(4) for half in range(2)
 ]
 ACROSS = [(2 * x + half, 2 * (x ^ 1) + (1 - half)) for x in range(4) for half in range(2) if not owns(x, half)]
+
+
+def half_of(place_ref):
+    return place_ref[0] // CORES % Z_PAIR
 
 
 def front_kernel(
@@ -77,11 +81,10 @@
     write_sems,
     sems,
 ):
-    fetch = pltpu.make_async_copy(patches_ref, rows_ref, sems.at[0])
-    fetch.start()
-    core = place_ref[1]
+    shard = place_ref[0] // (Y_HI * Z_QUAD * Z_PAIR * CORES)
+    core = place_ref[0] % CORES
     for i in range(2):
-        choice = sends_ref[2 * place_ref[0] + i]
+        choice = sends_ref[4 * shard + 2 * half_of(place_ref) + i]
 
         @pl.when(choice < 3)
         def _():
@@ -91,6 +94,8 @@
         def _():
             pltpu.make_async_copy(proj_ref.at[core], held_ref.at[i], read_sems.at[i]).start()
 
+    fetch = pltpu.make_async_copy(patches_ref, rows_ref, sems.at[0])
+    fetch.start()
     copies = []
     for i in range(2):
         pltpu.make_async_copy(proj_ref.at[0], held_ref.at[i], read_sems.at[i]).wait()
@@ -141,7 +146,7 @@
     hidden = -1e30 * HEAD**0.5
     copies = []
     for slot in range(12):
-        source = blocks_ref.at[order_ref[16 * place_ref[2] + slot]]
+        source = blocks_ref.at[order_ref[16 * half_of(place_ref) + slot]]
         copies.append(pltpu.make_async_copy(source, weight_ref.at[slot * HEAD : (slot + 1) * HEAD], sems.at[slot]))
     arrivals = [
         pltpu.make_async_copy(ref, x_ref.at[part], x_sems.at[part])
@@ -155,25 +160,35 @@
         copy.start()
     for copy in copies + arrivals:
         copy.wait()
-    for part in range(4):
-        mixed = lax.dot_general(
+    everything = [
+        lax.dot_general(
             weight_ref[...], x_ref[part, :ROWS, :], (((1,), (1,)), ((), ())), preferred_element_type=F32
         ).astype(BF16)
+        for part in range(4)
+    ]
+    for part in range(4):
+        mixed = everything[part]
         code = x_ref[part, ROWS:, :ROWS].astype(F32)[0:1, :]
         square = jnp.broadcast_to(code, (ROWS, ROWS))
         allowed = square == square.T
         alive = code < 64.0
+        def piece(kind, head):
+            return mixed[(4 * kind + head) * HEAD : (4 * kind + head + 1) * HEAD, :]
+
+        scores = [
+            lax.dot_general(piece(1, head), piece(0, head), (((0,), (0,)), ((), ())), preferred_element_type=F32)
+            for head in range(4)
+        ]
+        weights, totals = [], []
         for head in range(4):
-            queries = mixed[head * HEAD : (head + 1) * HEAD, :]
-            keyset = mixed[(4 + head) * HEAD : (5 + head) * HEAD, :]
-            valueset = mixed[(8 + head) * HEAD : (9 + head) * HEAD, :]
-            scores = lax.dot_general(keyset, queries, (((0,), (0,)), ((), ())), preferred_element_type=F32)
-            scores = jnp.where(allowed, scores, hidden)
-            peak = jnp.max(scores, axis=0, keepdims=True)
-            weights = jnp.exp2((scores - peak) * scale)
-            total = jnp.sum(weights, axis=0, keepdims=True)
-            context = jnp.dot(valueset, weights.astype(BF16), preferred_element_type=F32)
-            context = jnp.where(alive, context / total, 0.0)
+            masked = jnp.where(allowed, scores[head], hidden)
+            peak = jnp.max(masked, axis=0, keepdims=True)
+            weight = jnp.exp2((masked - peak) * scale)
+            totals.append(jnp.sum(weight, axis=0, keepdims=True))
+            weights.append(weight.astype(BF16))
+        for head in range(4):
+            context = jnp.dot(piece(2, head), weights[head], preferred_element_type=F32)
+            context = jnp.where(alive, context / totals[head], 0.0)
             context_ref[head * HEAD : (head + 1) * HEAD, part * ROWS : (part + 1) * ROWS] = context.astype(BF16)
     store = pltpu.make_async_copy(context_ref, out_ref, out_sem)
     store.start()
@@ -193,7 +208,7 @@
     copies = [pltpu.make_async_copy(from_ref, context_ref, sem)]
     copies[0].start()
     for slot in range(4):
-        source = blocks_ref.at[order_ref[16 * place_ref[2] + 12 + slot]]
+        source = blocks_ref.at[order_ref[16 * half_of(place_ref) + 12 + slot]]
         copies.append(pltpu.make_async_copy(source, weight_ref.at[slot * HEAD : (slot + 1) * HEAD], sems.at[slot]))
         copies[-1].start()
     for copy in copies:
@@ -261,7 +276,7 @@
     half = lax.axis_index("z_pair")
     x = lax.axis_index("x")
     shard = lax.axis_index("y_lo") * 4 + x
-    place = jnp.stack([2 * shard + half, core, half])
+    place = lax.axis_index(AXES).reshape(1)
     sends, orders = jnp.asarray(SENDS), jnp.asarray(ORDERS)
 
     def to_core(value):
@@ -362,15 +377,16 @@
     grad, from_core_late = lax.optimization_barrier((grad, from_core))
     grad = sum_of(grad, Y_HI)
     from_pair = to_pair(for_pair)
+    grad = lax.all_to_all(grad, "y_hi", 0, 0)
+    grad, from_pair = lax.optimization_barrier((grad, from_pair))
+    grad = sum_of(grad, 1)[0]
+
+    first = lax.ppermute(grad, ("x", "z_pair"), TO_OWNER)
+    second = lax.ppermute(grad, ("x", "z_pair"), ACROSS)
     projected = keep_late[0].astype(F32) + from_core_late[0].astype(F32) + from_pair.astype(F32)
     alive = lax.iota(jnp.int32, ROWS) < tile_counts[0] * TILE
     output = jnp.where(alive[:, None], patches.astype(F32) + projected, F32(0.0)).astype(BF16)
-    grad = lax.all_to_all(grad, "y_hi", 0, 0)
-    grad, output = lax.optimization_barrier((grad, output))
-    grad = sum_of(grad, 1)[0]
-
-    first = lax.ppermute(grad, ("x", "z_pair"), TO_OWNER)
-    second = lax.ppermute(grad, ("x", "z_pair"), ACROSS)
+    second, output = lax.optimization_barrier((second, output))
     owner = ((x == 0) | (x == 3)) == (half == 1)
     two = lax.broadcasted_iota(jnp.int32, (2, 1, 1), 0)
     head_grad = jnp.where(two == x % 2, jnp.where(owner, grad, first), jnp.where(owner, first, second))

time: 143 us -> 138 us (0.965)
  Pallas kernels: 24.3 us -> 20.4 us
    pallas_call x1, Pallas kernels: 14.2 us -> 10.4 us  [shards(): call(attention_kernel, (array(4 * HEAD, 4 * ROWS), array(4 * HEAD, WIDTH)...]
    ppermute x1, waiting for transfers between devices: 3.3 us -> 0.01 us  [shards(): first = lax.ppermute(grad, ('x', 'z_pair'), TO_OWNER)]
    all_to_all x1, waiting for transfers between devices: 0.02 us -> 2.28 us  [shards(): grad = lax.all_to_all(grad, 'y_hi', 0, 0)]
where the time goes in v4:
time: 138 us; the launch traced here: 137 us
  starting transfers between devices  84.2 us (61%)
  waiting for transfers between devices  24.6 us (18%)
  Pallas kernels  20.4 us (15%)
  other arithmetic  5.37 us (4%)
  between operations  1.54 us (1%)
    ppermute x6, starting transfers between devices, to_core(): return lax.ppermute(value, 'core', CORE_SWAP)  38.3 us
    pallas_call x1, Pallas kernels, shards(): call(attention_kernel, (array(4 * HEAD, 4 * ROWS), array(4 * HEAD, WIDTH)...  10.4 us
    ppermute x3, waiting for transfers between devices, to_pair(): return lax.ppermute(value, 'z_pair', PAIR_SWAP)  9.87 us
    all_to_all x1, starting transfers between devices, shards(): grad = lax.all_to_all(grad, 'z_quad', 0, 0)  9.39 us
    ppermute x3, starting transfers between devices, to_pair(): return lax.ppermute(value, 'z_pair', PAIR_SWAP)  9.09 us
    ppermute x1, starting transfers between devices, shards(): second = lax.ppermute(grad, ('x', 'z_pair'), ACROSS)  8.32 us
    all_to_all x1, starting transfers between devices, shards(): grad = lax.all_to_all(grad, 'y_hi', 0, 0)  6.01 us
    all_to_all x1, starting transfers between devices, shards(): blocks = lax.all_to_all(own, FSDP, 0, 0).reshape(16, HEAD, WIDTH)  6.01 us
  transfers between devices with their start and end apart: 15, of which 7 were waited for; matrix products, arithmetic and copies ran while one was open for 3% of the time, Pallas kernels for 4%

profile of v4, /device:TPU:1, one launch (start us, length us, event | category | flops | bytes accessed | tf_op | source)
XLA Modules:
  0.0 137.3 jit_solution(18248763812165417904)
XLA Ops:
  1.3 3.9 %shard_map.104 = (bf16[272,1280]{1,0:T(8,128)(2,1)}, bf16[8,2,80,1280]{3,2,1,0:T(8,128)(2,1)}) custom-call(s32[1]{0:T(128)} %bitcast.place_ref, s32[32]{0:T(128)} %constant.57.clone.sends_ref, s32[1]{0:T(128)S(6)} %copy.11.count_ref, bf16[256,1280]{1,0:T(8,128)(2,1)} %patches_ref.1, f32[1280]{0:T(1024)} %gain_ref.1, s32[256]{0:T(256)} %images_ref.1, ...), custom_call_target="tpu_custom_call" | custom-call | bytes 6291456 | tf_op jit(solution)/shard_map/pallas_call | solution.py:288
  5.2 0.0 copy-start.3
  5.3 0.0 copy-start.1
  5.3 0.0 copy-start
  5.3 6.0 %all-to-all-start = ((bf16[8,2,80,1280]{3,2,1,0:T(8,128)(2,1)}), bf16[8,2,80,1280]{3,2,1,0:T(8,128)(2,1)}, u32[]{:S(2)}, u32[]{:S(2)}) async-start(bf16[8,2,80,1280]{3,2,1,0:T(8,128)(2,1)} %get-tuple-element.17), calls=%async_computation | async-start | bytes 6553600 | tf_op jit(solution)/shard_map/all_to_all | solution.py:312
  11.3 0.0 copy-done.3
  11.3 4.0 %collective-permute-start.1 = (bf16[272,1280]{1,0:T(8,128)(2,1)S(1)}, bf16[272,1280]{1,0:T(8,128)(2,1)S(1)}, u32[]{:S(2)}, u32[]{:S(2)}) collective-permute-start(bf16[272,1280]{1,0:T(8,128)(2,1)S(1)} %copy-done.3), channel_id=1, source_target_pairs={{0,2},{2,0},{1,3},{3,1},{4,6},{6,4},{5,7},{7,5},{8,10},{10,8},{9,1... | collective-permute-start | bytes 2088968 | tf_op jit(solution)/shard_map/ppermute | solution.py:286
  15.3 0.0 copy-done.1
  15.3 1.9 %collective-permute-start.4 = (bf16[256,1280]{1,0:T(8,128)(2,1)S(1)}, bf16[256,1280]{1,0:T(8,128)(2,1)S(1)}, u32[]{:S(2)}, u32[]{:S(2)}) collective-permute-start(bf16[256,1280]{1,0:T(8,128)(2,1)S(1)} %copy-done.1), channel_id=1, source_target_pairs={{0,2},{2,0},{1,3},{3,1},{4,6},{6,4},{5,7},{7,5},{8,10},{10,8},{9,1... | collective-permute-start | bytes 1966088 | tf_op jit(solution)/shard_map/ppermute | solution.py:286
  17.2 7.3 %collective-permute-start = (bf16[272,1280]{1,0:T(8,128)(2,1)S(1)}, bf16[272,1280]{1,0:T(8,128)(2,1)S(1)}, u32[]{:S(2)}, u32[]{:S(2)}) collective-permute-start(bf16[272,1280]{1,0:T(8,128)(2,1)S(1)} %copy-done.3), channel_id=1, source_target_pairs={{0,1},{1,0},{2,3},{3,2},{4,5},{5,4},{6,7},{7,6},{8,9},{9,8},{10,11... | collective-permute-start | bytes 2088968 | tf_op jit(solution)/shard_map/ppermute | solution.py:283
  24.6 2.5 %collective-permute-done.1.x2_ref = bf16[272,1280]{1,0:T(8,128)(2,1)S(1)} collective-permute-done((bf16[272,1280]{1,0:T(8,128)(2,1)S(1)}, bf16[272,1280]{1,0:T(8,128)(2,1)S(1)}, u32[]{:S(2)}, u32[]{:S(2)}) %collective-permute-start.1) | collective-permute-done | bytes 696352 | tf_op jit(solution)/shard_map/ppermute | solution.py:286
  27.1 0.0 copy-start.4
  27.1 12.1 %collective-permute-start.2 = (bf16[272,1280]{1,0:T(8,128)(2,1)S(1)}, bf16[272,1280]{1,0:T(8,128)(2,1)}, u32[]{:S(2)}, u32[]{:S(2)}) collective-permute-start(bf16[272,1280]{1,0:T(8,128)(2,1)S(1)} %collective-permute-done.1.x2_ref), channel_id=1, source_target_pairs={{0,1},{1,0},{2,3},{3,2},{4,5},{5,4},{6,7},{7,6},{8,9},{9,8},{10,11... | collective-permute-start | bytes 2088968 | tf_op jit(solution)/shard_map/ppermute | solution.py:283
  39.1 1.9 %collective-permute-start.3 = (bf16[256,1280]{1,0:T(8,128)(2,1)S(1)}, bf16[256,1280]{1,0:T(8,128)(2,1)S(1)}, u32[]{:S(2)}, u32[]{:S(2)}) collective-permute-start(bf16[256,1280]{1,0:T(8,128)(2,1)S(1)} %copy-done.1), channel_id=1, source_target_pairs={{0,1},{1,0},{2,3},{3,2},{4,5},{5,4},{6,7},{7,6},{8,9},{9,8},{10,11... | collective-permute-start | bytes 1966088 | tf_op jit(solution)/shard_map/ppermute | solution.py:283
  41.1 0.0 collective-permute-done.4.c2_ref
  41.1 0.0 copy-start.6
  41.1 6.7 %collective-permute-start.5 = (bf16[256,1280]{1,0:T(8,128)(2,1)S(1)}, bf16[256,1280]{1,0:T(8,128)(2,1)S(1)}, u32[]{:S(2)}, u32[]{:S(2)}) collective-permute-start(bf16[256,1280]{1,0:T(8,128)(2,1)S(1)} %collective-permute-done.4.c2_ref), channel_id=1, source_target_pairs={{0,1},{1,0},{2,3},{3,2},{4,5},{5,4},{6,7},{7,6},{8,9},{9,8},{10,11... | collective-permute-start | bytes 1966088 | tf_op jit(solution)/shard_map/ppermute | solution.py:283
  47.8 0.0 collective-permute-done.3.c1_ref
  47.8 0.0 collective-permute-done.x1_ref
  47.8 0.0 copy-done.6
  47.8 0.0 copy-start.5
  47.8 1.7 %collective-permute-done.5.c3_ref = bf16[256,1280]{1,0:T(8,128)(2,1)S(1)} collective-permute-done((bf16[256,1280]{1,0:T(8,128)(2,1)S(1)}, bf16[256,1280]{1,0:T(8,128)(2,1)S(1)}, u32[]{:S(2)}, u32[]{:S(2)}) %collective-permute-start.5) | collective-permute-done | bytes 655392 | tf_op jit(solution)/shard_map/ppermute | solution.py:283
  49.5 0.0 copy-start.7
  49.5 0.8 copy-done.7
  50.3 0.0 collective-permute-done.2.x3_ref
  50.3 0.0 all-to-all-done
  50.3 0.0 copy-done.5
  50.3 0.0 copy-done.4
  50.3 0.0 copy-done
  50.4 10.4 %shard_map.105 = (bf16[320,1024]{1,0:T(8,128)(2,1)S(1)}, bf16[320,1280]{1,0:T(8,128)(2,1)}) custom-call(s32[1]{0:T(128)} %bitcast.place_ref, s32[32]{0:T(128)S(1)} %copy-done, bf16[272,1280]{1,0:T(8,128)(2,1)} %get-tuple-element.16.x0_ref, bf16[272,1280]{1,0:T(8,128)(2,1)} %copy-done.5, bf16[272,1280]{1,0:T(8,128)(2,1)} %copy-done.4, ...), custom_call_target="tpu_custom_call" | custom-call | flops 3892314112 | bytes 12582912 | tf_op jit(solution)/shard_map/pallas_call | solution.py:321
  60.8 5.2 %all-to-all-start.1 = ((bf16[8,40,1280]{2,1,0:T(8,128)(2,1)}), bf16[8,40,1280]{2,1,0:T(8,128)(2,1)S(1)}, u32[]{:S(2)}, u32[]{:S(2)}) async-start(bf16[8,40,1280]{2,1,0:T(8,128)(2,1)} %bitcast.31), calls=%async_computation.1 | async-start | bytes 1638400 | tf_op jit(solution)/shard_map/all_to_all | solution.py:371
  65.9 4.4 %shard_map.106 = (bf16[2,256,1280]{2,1,0:T(8,128)(2,1)S(1)}, bf16[2,256,1280]{2,1,0:T(8,128)(2,1)}) custom-call(s32[1]{0:T(128)} %bitcast.place_ref, s32[32]{0:T(128)S(1)} %copy-done, bf16[320,1024]{1,0:T(8,128)(2,1)S(1)} %get-tuple-element.19.from_ref, bf16[16,80,1280]{2,1,0:T(8,128)(2,1)} %bitcast.4.blocks_ref), custom_call_target="tpu_custom_call" | custom-call | flops 838860800 | bytes 6291456 | tf_op jit(solution)/shard_map/pallas_call | solution.py:353
  70.3 2.6 %collective-permute-start.6 = (bf16[2,256,1280]{2,1,0:T(8,128)(2,1)}, bf16[2,256,1280]{2,1,0:T(8,128)(2,1)}, u32[]{:S(2)}, u32[]{:S(2)}) collective-permute-start(bf16[2,256,1280]{2,1,0:T(8,128)(2,1)} %get-tuple-element.22), channel_id=1, source_target_pairs={{0,1},{1,0},{2,3},{3,2},{4,5},{5,4},{6,7},{7,6},{8,9},{9,8},{10,11... | collective-permute-start | bytes 3932168 | tf_op jit(solution)/shard_map/ppermute | solution.py:283
  72.8 5.3 %all-to-all-done.1.terms_ref = bf16[8,40,1280]{2,1,0:T(8,128)(2,1)S(1)} async-done(((bf16[8,40,1280]{2,1,0:T(8,128)(2,1)}), bf16[8,40,1280]{2,1,0:T(8,128)(2,1)S(1)}, u32[]{:S(2)}, u32[]{:S(2)}) %all-to-all-start.1) | async-done | bytes 819232 | tf_op jit(solution)/shard_map/all_to_all | solution.py:371
  78.2 0.9 shard_map.107
  79.0 9.4 %all-to-all-start.2 = ((bf16[4,40,1280]{2,1,0:T(8,128)(2,1)}), bf16[4,40,1280]{2,1,0:T(8,128)(2,1)S(1)}, u32[]{:S(2)}, u32[]{:S(2)}) async-start(bf16[4,40,1280]{2,1,0:T(8,128)(2,1)} %shard_map.107), calls=%async_computation.2 | async-start | bytes 819200 | tf_op jit(solution)/shard_map/all_to_all | solution.py:376
  88.4 0.0 collective-permute-done.6
  88.4 2.1 %fusion.3 = bf16[256,1280]{1,0:T(8,128)(2,1)} fusion(bf16[2,256,1280]{2,1,0:T(8,128)(2,1)} %collective-permute-done.6, bf16[2,256,1280]{2,1,0:T(8,128)(2,1)S(1)} %get-tuple-element.25), kind=kLoop, calls=%fused_computation.5 | loop fusion | flops 1310720 | bytes 1966080 | tf_op jit(solution)/shard_map/convert_element_type | solution.py:375
  90.5 0.0 copy-start.2
  90.5 3.2 %collective-permute-start.7 = (bf16[256,1280]{1,0:T(8,128)(2,1)}, bf16[256,1280]{1,0:T(8,128)(2,1)S(1)}, u32[]{:S(2)}, u32[]{:S(2)}) collective-permute-start(bf16[256,1280]{1,0:T(8,128)(2,1)} %fusion.3), channel_id=1, source_target_pairs={{0,2},{2,0},{1,3},{3,1},{4,6},{6,4},{5,7},{7,5},{8,10},{10,8},{9,1... | collective-permute-start | bytes 1966088 | tf_op jit(solution)/shard_map/ppermute | solution.py:286
  93.7 4.5 %all-to-all-done.2.terms_ref = bf16[4,40,1280]{2,1,0:T(8,128)(2,1)S(1)} async-done(((bf16[4,40,1280]{2,1,0:T(8,128)(2,1)}), bf16[4,40,1280]{2,1,0:T(8,128)(2,1)S(1)}, u32[]{:S(2)}, u32[]{:S(2)}) %all-to-all-start.2) | async-done | bytes 409632 | tf_op jit(solution)/shard_map/all_to_all | solution.py:376
  98.2 0.8 shard_map.108
  99.0 6.0 %all-to-all-start.3 = ((bf16[4,40,1280]{2,1,0:T(8,128)(2,1)}), bf16[4,40,1280]{2,1,0:T(8,128)(2,1)S(1)}, u32[]{:S(2)}, u32[]{:S(2)}) async-start(bf16[4,40,1280]{2,1,0:T(8,128)(2,1)} %shard_map.108), calls=%async_computation.3 | async-start | bytes 819200 | tf_op jit(solution)/shard_map/all_to_all | solution.py:380
  105.0 0.1 broadcast_in_dim.66
  105.1 0.1 broadcast_in_dim.67
  105.2 7.4 %collective-permute-done.7 = bf16[256,1280]{1,0:T(8,128)(2,1)S(1)} collective-permute-done((bf16[256,1280]{1,0:T(8,128)(2,1)}, bf16[256,1280]{1,0:T(8,128)(2,1)S(1)}, u32[]{:S(2)}, u32[]{:S(2)}) %collective-permute-start.7) | collective-permute-done | bytes 655392 | tf_op jit(solution)/shard_map/ppermute | solution.py:286
  112.5 2.3 %all-to-all-done.3.terms_ref = bf16[4,40,1280]{2,1,0:T(8,128)(2,1)S(1)} async-done(((bf16[4,40,1280]{2,1,0:T(8,128)(2,1)}), bf16[4,40,1280]{2,1,0:T(8,128)(2,1)S(1)}, u32[]{:S(2)}, u32[]{:S(2)}) %all-to-all-start.3) | async-done | bytes 409632 | tf_op jit(solution)/shard_map/all_to_all | solution.py:380
  114.8 0.1 shard_map.109
  114.9 1.9 %collective-permute-start.9 = (bf16[40,1280]{1,0:T(8,128)(2,1)S(1)}, bf16[40,1280]{1,0:T(8,128)(2,1)S(1)}, u32[]{:S(2)}, u32[]{:S(2)}) collective-permute-start(bf16[40,1280]{1,0:T(8,128)(2,1)S(1)} %bitcast.28), channel_id=1, source_target_pairs={{0,64},{2,0},{64,66},{66,2},{128,130},{130,194},{192,128},{194,192... | collective-permute-start | bytes 307208 | tf_op jit(solution)/shard_map/ppermute | solution.py:384
  116.8 8.3 %collective-permute-start.8 = (bf16[40,1280]{1,0:T(8,128)(2,1)S(1)}, bf16[40,1280]{1,0:T(8,128)(2,1)S(1)}, u32[]{:S(2)}, u32[]{:S(2)}) collective-permute-start(bf16[40,1280]{1,0:T(8,128)(2,1)S(1)} %bitcast.29), channel_id=1, source_target_pairs={{0,66},{66,0},{130,192},{192,130},{1,67},{67,1},{131,193},{193,131... | collective-permute-start | bytes 307208 | tf_op jit(solution)/shard_map/ppermute | solution.py:385
  125.1 0.0 copy-done.2
  125.2 2.3 %fusion.2 = bf16[256,1280]{1,0:T(8,128)(2,1)} fusion(bf16[256,1280]{1,0:T(8,128)(2,1)S(1)} %collective-permute-done.7, bf16[256,1280]{1,0:T(8,128)(2,1)S(1)} %copy-done.2, bf16[2,256,1280]{2,1,0:T(8,128)(2,1)} %collective-permute-done.6, bf16[2,256,1280]{2,1,0:T(8,128)(2,1)S(1)} %get-tuple-element.25, pred[256]{0:T(512)(128)(4,1)S(1)} %iota_compare_fusion), kind=kLoop, calls=%fused_computation.3 | loop fusion | flops 2949120 | bytes 3277056 | tf_op jit(solution)/shard_map/convert_element_type | solution.py:388
  127.5 0.0 collective-permute-done.8
  127.5 0.0 collective-permute-done.9
  127.5 0.1 bitcast_select_fusion.1
  127.6 7.7 %collective-permute-start.10 = (bf16[80,1280]{1,0:T(8,128)(2,1)S(1)}, bf16[80,1280]{1,0:T(8,128)(2,1)S(1)}, u32[]{:S(2)}, u32[]{:S(2)}) collective-permute-start(bf16[80,1280]{1,0:T(8,128)(2,1)S(1)} %bitcast_select_fusion.1), channel_id=1, source_target_pairs={{0,1},{1,0},{2,3},{3,2},{4,5},{5,4},{6,7},{7,6},{8,9},{9,8},{10,11... | collective-permute-start | bytes 614408 | tf_op jit(solution)/shard_map/ppermute | solution.py:283
  135.4 0.1 broadcast_in_dim.63
  135.4 0.1 broadcast_in_dim.64
  135.5 0.9 collective-permute-done.10
  136.4 0.9 bitcast_select_fusion
  (4 shorter events, 0.0 us)
Async XLA Ops:
  5.2 6.0 %copy-start.3 = (bf16[272,1280]{1,0:T(8,128)(2,1)S(1)}, bf16[272,1280]{1,0:T(8,128)(2,1)}, u32[]{:S(2)}) copy-start(bf16[272,1280]{1,0:T(8,128)(2,1)} %get-tuple-element.16.x0_ref) | copy-start | bytes 2088964
  5.3 10.0 %copy-start.1 = (bf16[256,1280]{1,0:T(8,128)(2,1)S(1)}, bf16[256,1280]{1,0:T(8,128)(2,1)}, u32[]{:S(2)}) copy-start(bf16[256,1280]{1,0:T(8,128)(2,1)} %c0_ref.1) | copy-start | bytes 1966084
  5.3 45.1 %copy-start = (s32[32]{0:T(128)S(1)}, s32[32]{0:T(128)}, u32[]{:S(2)}) copy-start(s32[32]{0:T(128)} %constant.58.clone.order_ref) | copy-start | bytes 388
  5.3 45.1 %all-to-all-start = ((bf16[8,2,80,1280]{3,2,1,0:T(8,128)(2,1)}), bf16[8,2,80,1280]{3,2,1,0:T(8,128)(2,1)}, u32[]{:S(2)}, u32[]{:S(2)}) async-start(bf16[8,2,80,1280]{3,2,1,0:T(8,128)(2,1)} %get-tuple-element.17), calls=%async_computation | async-start | bytes 6553600 | tf_op jit(solution)/shard_map/all_to_all | solution.py:312
  11.3 15.8 %collective-permute-start.1 = (bf16[272,1280]{1,0:T(8,128)(2,1)S(1)}, bf16[272,1280]{1,0:T(8,128)(2,1)S(1)}, u32[]{:S(2)}, u32[]{:S(2)}) collective-permute-start(bf16[272,1280]{1,0:T(8,128)(2,1)S(1)} %copy-done.3), channel_id=1, source_target_pairs={{0,2},{2,0},{1,3},{3,1},{4,6},{6,4},{5,7},{7,5},{8,10},{10,8},{9,1... | collective-permute-start | bytes 2088968 | tf_op jit(solution)/shard_map/ppermute | solution.py:286
  15.3 25.8 %collective-permute-start.4 = (bf16[256,1280]{1,0:T(8,128)(2,1)S(1)}, bf16[256,1280]{1,0:T(8,128)(2,1)S(1)}, u32[]{:S(2)}, u32[]{:S(2)}) collective-permute-start(bf16[256,1280]{1,0:T(8,128)(2,1)S(1)} %copy-done.1), channel_id=1, source_target_pairs={{0,2},{2,0},{1,3},{3,1},{4,6},{6,4},{5,7},{7,5},{8,10},{10,8},{9,1... | collective-permute-start | bytes 1966088 | tf_op jit(solution)/shard_map/ppermute | solution.py:286
  17.2 30.6 %collective-permute-start = (bf16[272,1280]{1,0:T(8,128)(2,1)S(1)}, bf16[272,1280]{1,0:T(8,128)(2,1)S(1)}, u32[]{:S(2)}, u32[]{:S(2)}) collective-permute-start(bf16[272,1280]{1,0:T(8,128)(2,1)S(1)} %copy-done.3), channel_id=1, source_target_pairs={{0,1},{1,0},{2,3},{3,2},{4,5},{5,4},{6,7},{7,6},{8,9},{9,8},{10,11... | collective-permute-start | bytes 2088968 | tf_op jit(solution)/shard_map/ppermute | solution.py:283
  27.1 23.3 %copy-start.4 = (bf16[272,1280]{1,0:T(8,128)(2,1)}, bf16[272,1280]{1,0:T(8,128)(2,1)S(1)}, u32[]{:S(2)}) copy-start(bf16[272,1280]{1,0:T(8,128)(2,1)S(1)} %collective-permute-done.1.x2_ref) | copy-start | bytes 2088964
  27.1 23.3 %collective-permute-start.2 = (bf16[272,1280]{1,0:T(8,128)(2,1)S(1)}, bf16[272,1280]{1,0:T(8,128)(2,1)}, u32[]{:S(2)}, u32[]{:S(2)}) collective-permute-start(bf16[272,1280]{1,0:T(8,128)(2,1)S(1)} %collective-permute-done.1.x2_ref), channel_id=1, source_target_pairs={{0,1},{1,0},{2,3},{3,2},{4,5},{5,4},{6,7},{7,6},{8,9},{9,8},{10,11... | collective-permute-start | bytes 2088968 | tf_op jit(solution)/shard_map/ppermute | solution.py:283
  39.1 8.7 %collective-permute-start.3 = (bf16[256,1280]{1,0:T(8,128)(2,1)S(1)}, bf16[256,1280]{1,0:T(8,128)(2,1)S(1)}, u32[]{:S(2)}, u32[]{:S(2)}) collective-permute-start(bf16[256,1280]{1,0:T(8,128)(2,1)S(1)} %copy-done.1), channel_id=1, source_target_pairs={{0,1},{1,0},{2,3},{3,2},{4,5},{5,4},{6,7},{7,6},{8,9},{9,8},{10,11... | collective-permute-start | bytes 1966088 | tf_op jit(solution)/shard_map/ppermute | solution.py:283
  41.1 6.7 %copy-start.6 = (bf16[256,1280]{1,0:T(8,128)(2,1)}, bf16[256,1280]{1,0:T(8,128)(2,1)S(1)}, u32[]{:S(2)}) copy-start(bf16[256,1280]{1,0:T(8,128)(2,1)S(1)} %collective-permute-done.4.c2_ref) | copy-start | bytes 1966084
  41.1 8.4 %collective-permute-start.5 = (bf16[256,1280]{1,0:T(8,128)(2,1)S(1)}, bf16[256,1280]{1,0:T(8,128)(2,1)S(1)}, u32[]{:S(2)}, u32[]{:S(2)}) collective-permute-start(bf16[256,1280]{1,0:T(8,128)(2,1)S(1)} %collective-permute-done.4.c2_ref), channel_id=1, source_target_pairs={{0,1},{1,0},{2,3},{3,2},{4,5},{5,4},{6,7},{7,6},{8,9},{9,8},{10,11... | collective-permute-start | bytes 1966088 | tf_op jit(solution)/shard_map/ppermute | solution.py:283
  47.8 2.5 %copy-start.5 = (bf16[272,1280]{1,0:T(8,128)(2,1)}, bf16[272,1280]{1,0:T(8,128)(2,1)S(1)}, u32[]{:S(2)}) copy-start(bf16[272,1280]{1,0:T(8,128)(2,1)S(1)} %collective-permute-done.x1_ref) | copy-start | bytes 2088964
  49.5 0.8 copy-start.7
  60.8 17.4 %all-to-all-start.1 = ((bf16[8,40,1280]{2,1,0:T(8,128)(2,1)}), bf16[8,40,1280]{2,1,0:T(8,128)(2,1)S(1)}, u32[]{:S(2)}, u32[]{:S(2)}) async-start(bf16[8,40,1280]{2,1,0:T(8,128)(2,1)} %bitcast.31), calls=%async_computation.1 | async-start | bytes 1638400 | tf_op jit(solution)/shard_map/all_to_all | solution.py:371
  70.3 18.1 %collective-permute-start.6 = (bf16[2,256,1280]{2,1,0:T(8,128)(2,1)}, bf16[2,256,1280]{2,1,0:T(8,128)(2,1)}, u32[]{:S(2)}, u32[]{:S(2)}) collective-permute-start(bf16[2,256,1280]{2,1,0:T(8,128)(2,1)} %get-tuple-element.22), channel_id=1, source_target_pairs={{0,1},{1,0},{2,3},{3,2},{4,5},{5,4},{6,7},{7,6},{8,9},{9,8},{10,11... | collective-permute-start | bytes 3932168 | tf_op jit(solution)/shard_map/ppermute | solution.py:283
  79.0 19.2 %all-to-all-start.2 = ((bf16[4,40,1280]{2,1,0:T(8,128)(2,1)}), bf16[4,40,1280]{2,1,0:T(8,128)(2,1)S(1)}, u32[]{:S(2)}, u32[]{:S(2)}) async-start(bf16[4,40,1280]{2,1,0:T(8,128)(2,1)} %shard_map.107), calls=%async_computation.2 | async-start | bytes 819200 | tf_op jit(solution)/shard_map/all_to_all | solution.py:376
  90.5 34.6 %copy-start.2 = (bf16[256,1280]{1,0:T(8,128)(2,1)S(1)}, bf16[256,1280]{1,0:T(8,128)(2,1)}, u32[]{:S(2)}) copy-start(bf16[256,1280]{1,0:T(8,128)(2,1)} %patches_ref.1) | copy-start | bytes 1966084
  90.5 22.0 %collective-permute-start.7 = (bf16[256,1280]{1,0:T(8,128)(2,1)}, bf16[256,1280]{1,0:T(8,128)(2,1)S(1)}, u32[]{:S(2)}, u32[]{:S(2)}) collective-permute-start(bf16[256,1280]{1,0:T(8,128)(2,1)} %fusion.3), channel_id=1, source_target_pairs={{0,2},{2,0},{1,3},{3,1},{4,6},{6,4},{5,7},{7,5},{8,10},{10,8},{9,1... | collective-permute-start | bytes 1966088 | tf_op jit(solution)/shard_map/ppermute | solution.py:286
  99.0 15.8 %all-to-all-start.3 = ((bf16[4,40,1280]{2,1,0:T(8,128)(2,1)}), bf16[4,40,1280]{2,1,0:T(8,128)(2,1)S(1)}, u32[]{:S(2)}, u32[]{:S(2)}) async-start(bf16[4,40,1280]{2,1,0:T(8,128)(2,1)} %shard_map.108), calls=%async_computation.3 | async-start | bytes 819200 | tf_op jit(solution)/shard_map/all_to_all | solution.py:380
  114.9 12.6 %collective-permute-start.9 = (bf16[40,1280]{1,0:T(8,128)(2,1)S(1)}, bf16[40,1280]{1,0:T(8,128)(2,1)S(1)}, u32[]{:S(2)}, u32[]{:S(2)}) collective-permute-start(bf16[40,1280]{1,0:T(8,128)(2,1)S(1)} %bitcast.28), channel_id=1, source_target_pairs={{0,64},{2,0},{64,66},{66,2},{128,130},{130,194},{192,128},{194,192... | collective-permute-start | bytes 307208 | tf_op jit(solution)/shard_map/ppermute | solution.py:384
  116.8 10.7 %collective-permute-start.8 = (bf16[40,1280]{1,0:T(8,128)(2,1)S(1)}, bf16[40,1280]{1,0:T(8,128)(2,1)S(1)}, u32[]{:S(2)}, u32[]{:S(2)}) collective-permute-start(bf16[40,1280]{1,0:T(8,128)(2,1)S(1)} %bitcast.29), channel_id=1, source_target_pairs={{0,66},{66,0},{130,192},{192,130},{1,67},{67,1},{131,193},{193,131... | collective-permute-start | bytes 307208 | tf_op jit(solution)/shard_map/ppermute | solution.py:385
  127.6 8.8 %collective-permute-start.10 = (bf16[80,1280]{1,0:T(8,128)(2,1)S(1)}, bf16[80,1280]{1,0:T(8,128)(2,1)S(1)}, u32[]{:S(2)}, u32[]{:S(2)}) collective-permute-start(bf16[80,1280]{1,0:T(8,128)(2,1)S(1)} %bitcast_select_fusion.1), channel_id=1, source_target_pairs={{0,1},{1,0},{2,3},{3,2},{4,5},{5,4},{6,7},{7,6},{8,9},{9,8},{10,11... | collective-permute-start | bytes 614408 | tf_op jit(solution)/shard_map/ppermute | solution.py:283

commit v5 on v4

--- a/solution.py
+++ b/solution.py
@@ -57,6 +57,14 @@
     (2 * x + half, 2 * x + (1 - half) if owns(x, half) else 2 * (x ^ 1) + half) for x in range(4) for half in range(2)
 ]
 ACROSS = [(2 * x + half, 2 * (x ^ 1) + (1 - half)) for x in range(4) for half in range(2) if not owns(x, half)]
+
+
+def cross_groups(first):
+    def place(y, z, core):
+        return (y * Z_QUAD + z) * CORES + core
+
+    along_z = [[place(y, z, first) for z in range(Z_QUAD)] for y in range(Y_HI)]
+    return along_z + [[place(y, z, 1 - first) for y in range(Y_HI)] for z in range(Z_QUAD)]
 
 
 def half_of(place_ref):
@@ -373,11 +381,11 @@
     grad = sum_of(grad, Z_QUAD)
     from_core = to_core(send_out)
     for_pair = (keep_out[1].astype(F32) + from_core[1].astype(F32)).astype(BF16)
-    grad = lax.all_to_all(grad, "z_quad", 0, 0)
+    grad = lax.all_to_all(grad, ("y_hi", "z_quad", "core"), 0, 0, axis_index_groups=cross_groups(0))
     grad, from_core_late = lax.optimization_barrier((grad, from_core))
     grad = sum_of(grad, Y_HI)
     from_pair = to_pair(for_pair)
-    grad = lax.all_to_all(grad, "y_hi", 0, 0)
+    grad = lax.all_to_all(grad, ("y_hi", "z_quad", "core"), 0, 0, axis_index_groups=cross_groups(1))
     grad, from_pair = lax.optimization_barrier((grad, from_pair))
     grad = sum_of(grad, 1)[0]
 

time: 138 us -> 135 us (0.978)
  starting transfers between devices: 84.2 us -> 74.2 us
  waiting for transfers between devices: 24.6 us -> 31.4 us
    all_to_all x2, waiting for transfers between devices: 6.8 us -> 14.9 us  [shards(): lax.all_to_all(grad, ('y_hi', 'z_quad', 'core'), 0, 0, axis_index_groups=...]
    ppermute x1, starting transfers between devices: 8.32 us -> 2 us  [shards(): second = lax.ppermute(grad, ('x', 'z_pair'), ACROSS)]
    ppermute x6, starting transfers between devices: 38.3 us -> 33 us  [to_core(): return lax.ppermute(value, 'core', CORE_SWAP)]
    ppermute x3, waiting for transfers between devices: 9.87 us -> 5.35 us  [to_pair(): return lax.ppermute(value, 'z_pair', PAIR_SWAP)]
    ppermute x1, waiting for transfers between devices: 0.01 us -> 3.27 us  [shards(): second = lax.ppermute(grad, ('x', 'z_pair'), ACROSS)]
  transfers between devices with their start and end apart: 15 -> 15, of which waited for: 7 -> 8; matrix products, arithmetic and copies ran while one was open for 3% -> 4% of each run, Pallas kernels for 4% -> 4%
where the time goes in v5:
time: 135 us; the launch traced here: 134 us
  starting transfers between devices  74.2 us (55%)
  waiting for transfers between devices  31.4 us (23%)
  Pallas kernels  20.4 us (15%)
  other arithmetic  5.37 us (4%)
  between operations  1.54 us (1%)
    ppermute x6, starting transfers between devices, to_core(): return lax.ppermute(value, 'core', CORE_SWAP)  33 us
    all_to_all x2, starting transfers between devices, shards(): lax.all_to_all(grad, ('y_hi', 'z_quad', 'core'), 0, 0, axis_index_groups=...  15.5 us
    all_to_all x2, waiting for transfers between devices, shards(): lax.all_to_all(grad, ('y_hi', 'z_quad', 'core'), 0, 0, axis_index_groups=...  14.9 us
    pallas_call x1, Pallas kernels, shards(): call(attention_kernel, (array(4 * HEAD, 4 * ROWS), array(4 * HEAD, WIDTH)...  10.4 us
    ppermute x3, starting transfers between devices, to_pair(): return lax.ppermute(value, 'z_pair', PAIR_SWAP)  9.37 us
    all_to_all x1, starting transfers between devices, shards(): blocks = lax.all_to_all(own, FSDP, 0, 0).reshape(16, HEAD, WIDTH)  6.01 us
    ppermute x3, waiting for transfers between devices, to_pair(): return lax.ppermute(value, 'z_pair', PAIR_SWAP)  5.35 us
    all_to_all x1, waiting for transfers between devices, shards(): grad = lax.all_to_all(grad.reshape(8, 40, WIDTH), FSDP, 0, 0)  5.33 us
  transfers between devices with their start and end apart: 15, of which 8 were waited for; matrix products, arithmetic and copies ran while one was open for 4% of the time, Pallas kernels for 4%

profile of v5, /device:TPU:1, one launch (start us, length us, event | category | flops | bytes accessed | tf_op | source)
XLA Modules:
  0.0 134.1 jit_solution(1946362193028305180)
XLA Ops:
  1.3 3.9 %shard_map.104 = (bf16[272,1280]{1,0:T(8,128)(2,1)}, bf16[8,2,80,1280]{3,2,1,0:T(8,128)(2,1)}) custom-call(s32[1]{0:T(128)} %bitcast.place_ref, s32[32]{0:T(128)} %constant.57.clone.sends_ref, s32[1]{0:T(128)S(6)} %copy.11.count_ref, bf16[256,1280]{1,0:T(8,128)(2,1)} %patches_ref.1, f32[1280]{0:T(1024)} %gain_ref.1, s32[256]{0:T(256)} %images_ref.1, ...), custom_call_target="tpu_custom_call" | custom-call | bytes 6291456 | tf_op jit(solution)/shard_map/pallas_call | solution.py:296
  5.2 0.0 copy-start.3
  5.3 0.0 copy-start.1
  5.3 0.0 copy-start
  5.3 6.0 %all-to-all-start = ((bf16[8,2,80,1280]{3,2,1,0:T(8,128)(2,1)}), bf16[8,2,80,1280]{3,2,1,0:T(8,128)(2,1)}, u32[]{:S(2)}, u32[]{:S(2)}) async-start(bf16[8,2,80,1280]{3,2,1,0:T(8,128)(2,1)} %get-tuple-element.17), calls=%async_computation | async-start | bytes 6553600 | tf_op jit(solution)/shard_map/all_to_all | solution.py:320
  11.3 0.0 copy-done.3
  11.3 4.0 %collective-permute-start.1 = (bf16[272,1280]{1,0:T(8,128)(2,1)S(1)}, bf16[272,1280]{1,0:T(8,128)(2,1)S(1)}, u32[]{:S(2)}, u32[]{:S(2)}) collective-permute-start(bf16[272,1280]{1,0:T(8,128)(2,1)S(1)} %copy-done.3), channel_id=1, source_target_pairs={{0,2},{2,0},{1,3},{3,1},{4,6},{6,4},{5,7},{7,5},{8,10},{10,8},{9,1... | collective-permute-start | bytes 2088968 | tf_op jit(solution)/shard_map/ppermute | solution.py:294
  15.3 0.0 copy-done.1
  15.3 1.9 %collective-permute-start.4 = (bf16[256,1280]{1,0:T(8,128)(2,1)S(1)}, bf16[256,1280]{1,0:T(8,128)(2,1)S(1)}, u32[]{:S(2)}, u32[]{:S(2)}) collective-permute-start(bf16[256,1280]{1,0:T(8,128)(2,1)S(1)} %copy-done.1), channel_id=1, source_target_pairs={{0,2},{2,0},{1,3},{3,1},{4,6},{6,4},{5,7},{7,5},{8,10},{10,8},{9,1... | collective-permute-start | bytes 1966088 | tf_op jit(solution)/shard_map/ppermute | solution.py:294
  17.2 7.3 %collective-permute-start = (bf16[272,1280]{1,0:T(8,128)(2,1)S(1)}, bf16[272,1280]{1,0:T(8,128)(2,1)S(1)}, u32[]{:S(2)}, u32[]{:S(2)}) collective-permute-start(bf16[272,1280]{1,0:T(8,128)(2,1)S(1)} %copy-done.3), channel_id=1, source_target_pairs={{0,1},{1,0},{2,3},{3,2},{4,5},{5,4},{6,7},{7,6},{8,9},{9,8},{10,11... | collective-permute-start | bytes 2088968 | tf_op jit(solution)/shard_map/ppermute | solution.py:291
  24.6 2.5 %collective-permute-done.1.x2_ref = bf16[272,1280]{1,0:T(8,128)(2,1)S(1)} collective-permute-done((bf16[272,1280]{1,0:T(8,128)(2,1)S(1)}, bf16[272,1280]{1,0:T(8,128)(2,1)S(1)}, u32[]{:S(2)}, u32[]{:S(2)}) %collective-permute-start.1) | collective-permute-done | bytes 696352 | tf_op jit(solution)/shard_map/ppermute | solution.py:294
  27.1 0.0 copy-start.4
  27.1 12.1 %collective-permute-start.2 = (bf16[272,1280]{1,0:T(8,128)(2,1)S(1)}, bf16[272,1280]{1,0:T(8,128)(2,1)}, u32[]{:S(2)}, u32[]{:S(2)}) collective-permute-start(bf16[272,1280]{1,0:T(8,128)(2,1)S(1)} %collective-permute-done.1.x2_ref), channel_id=1, source_target_pairs={{0,1},{1,0},{2,3},{3,2},{4,5},{5,4},{6,7},{7,6},{8,9},{9,8},{10,11... | collective-permute-start | bytes 2088968 | tf_op jit(solution)/shard_map/ppermute | solution.py:291
  39.1 1.9 %collective-permute-start.3 = (bf16[256,1280]{1,0:T(8,128)(2,1)S(1)}, bf16[256,1280]{1,0:T(8,128)(2,1)S(1)}, u32[]{:S(2)}, u32[]{:S(2)}) collective-permute-start(bf16[256,1280]{1,0:T(8,128)(2,1)S(1)} %copy-done.1), channel_id=1, source_target_pairs={{0,1},{1,0},{2,3},{3,2},{4,5},{5,4},{6,7},{7,6},{8,9},{9,8},{10,11... | collective-permute-start | bytes 1966088 | tf_op jit(solution)/shard_map/ppermute | solution.py:291
  41.1 0.0 collective-permute-done.4.c2_ref
  41.1 0.0 copy-start.6
  41.1 6.7 %collective-permute-start.5 = (bf16[256,1280]{1,0:T(8,128)(2,1)S(1)}, bf16[256,1280]{1,0:T(8,128)(2,1)S(1)}, u32[]{:S(2)}, u32[]{:S(2)}) collective-permute-start(bf16[256,1280]{1,0:T(8,128)(2,1)S(1)} %collective-permute-done.4.c2_ref), channel_id=1, source_target_pairs={{0,1},{1,0},{2,3},{3,2},{4,5},{5,4},{6,7},{7,6},{8,9},{9,8},{10,11... | collective-permute-start | bytes 1966088 | tf_op jit(solution)/shard_map/ppermute | solution.py:291
  47.8 0.0 collective-permute-done.3.c1_ref
  47.8 0.0 collective-permute-done.x1_ref
  47.8 0.0 copy-done.6
  47.8 0.0 copy-start.5
  47.8 1.7 %collective-permute-done.5.c3_ref = bf16[256,1280]{1,0:T(8,128)(2,1)S(1)} collective-permute-done((bf16[256,1280]{1,0:T(8,128)(2,1)S(1)}, bf16[256,1280]{1,0:T(8,128)(2,1)S(1)}, u32[]{:S(2)}, u32[]{:S(2)}) %collective-permute-start.5) | collective-permute-done | bytes 655392 | tf_op jit(solution)/shard_map/ppermute | solution.py:291
  49.5 0.0 copy-start.7
  49.5 0.8 copy-done.7
  50.3 0.0 collective-permute-done.2.x3_ref
  50.3 0.0 all-to-all-done
  50.3 0.0 copy-done.5
  50.3 0.0 copy-done.4
  50.3 0.0 copy-done
  50.4 10.4 %shard_map.105 = (bf16[320,1024]{1,0:T(8,128)(2,1)S(1)}, bf16[320,1280]{1,0:T(8,128)(2,1)}) custom-call(s32[1]{0:T(128)} %bitcast.place_ref, s32[32]{0:T(128)S(1)} %copy-done, bf16[272,1280]{1,0:T(8,128)(2,1)} %get-tuple-element.16.x0_ref, bf16[272,1280]{1,0:T(8,128)(2,1)} %copy-done.5, bf16[272,1280]{1,0:T(8,128)(2,1)} %copy-done.4, ...), custom_call_target="tpu_custom_call" | custom-call | flops 3892314112 | bytes 12582912 | tf_op jit(solution)/shard_map/pallas_call | solution.py:329
  60.8 5.2 %all-to-all-start.1 = ((bf16[8,40,1280]{2,1,0:T(8,128)(2,1)}), bf16[8,40,1280]{2,1,0:T(8,128)(2,1)S(1)}, u32[]{:S(2)}, u32[]{:S(2)}) async-start(bf16[8,40,1280]{2,1,0:T(8,128)(2,1)} %bitcast.31), calls=%async_computation.1 | async-start | bytes 1638400 | tf_op jit(solution)/shard_map/all_to_all | solution.py:379
  65.9 4.4 %shard_map.106 = (bf16[2,256,1280]{2,1,0:T(8,128)(2,1)S(1)}, bf16[2,256,1280]{2,1,0:T(8,128)(2,1)}) custom-call(s32[1]{0:T(128)} %bitcast.place_ref, s32[32]{0:T(128)S(1)} %copy-done, bf16[320,1024]{1,0:T(8,128)(2,1)S(1)} %get-tuple-element.19.from_ref, bf16[16,80,1280]{2,1,0:T(8,128)(2,1)} %bitcast.4.blocks_ref), custom_call_target="tpu_custom_call" | custom-call | flops 838860800 | bytes 6291456 | tf_op jit(solution)/shard_map/pallas_call | solution.py:361
  70.3 2.6 %collective-permute-start.6 = (bf16[2,256,1280]{2,1,0:T(8,128)(2,1)}, bf16[2,256,1280]{2,1,0:T(8,128)(2,1)}, u32[]{:S(2)}, u32[]{:S(2)}) collective-permute-start(bf16[2,256,1280]{2,1,0:T(8,128)(2,1)} %get-tuple-element.22), channel_id=1, source_target_pairs={{0,1},{1,0},{2,3},{3,2},{4,5},{5,4},{6,7},{7,6},{8,9},{9,8},{10,11... | collective-permute-start | bytes 3932168 | tf_op jit(solution)/shard_map/ppermute | solution.py:291
  72.8 5.3 %all-to-all-done.1.terms_ref = bf16[8,40,1280]{2,1,0:T(8,128)(2,1)S(1)} async-done(((bf16[8,40,1280]{2,1,0:T(8,128)(2,1)}), bf16[8,40,1280]{2,1,0:T(8,128)(2,1)S(1)}, u32[]{:S(2)}, u32[]{:S(2)}) %all-to-all-start.1) | async-done | bytes 819232 | tf_op jit(solution)/shard_map/all_to_all | solution.py:379
  78.2 0.9 shard_map.107
  79.0 6.1 %all-to-all-start.2 = ((bf16[4,40,1280]{2,1,0:T(8,128)(2,1)}), bf16[4,40,1280]{2,1,0:T(8,128)(2,1)S(1)}, u32[]{:S(2)}, u32[]{:S(2)}) async-start(bf16[4,40,1280]{2,1,0:T(8,128)(2,1)} %shard_map.107), calls=%async_computation.2 | async-start | bytes 819200 | tf_op jit(solution)/shard_map/all_to_all | solution.py:384
  85.2 0.0 collective-permute-done.6
  85.2 2.1 %fusion.3 = bf16[256,1280]{1,0:T(8,128)(2,1)} fusion(bf16[2,256,1280]{2,1,0:T(8,128)(2,1)} %collective-permute-done.6, bf16[2,256,1280]{2,1,0:T(8,128)(2,1)S(1)} %get-tuple-element.25), kind=kLoop, calls=%fused_computation.5 | loop fusion | flops 1310720 | bytes 1966080 | tf_op jit(solution)/shard_map/convert_element_type | solution.py:383
  87.3 0.0 copy-start.2
  87.3 3.4 %collective-permute-start.7 = (bf16[256,1280]{1,0:T(8,128)(2,1)}, bf16[256,1280]{1,0:T(8,128)(2,1)S(1)}, u32[]{:S(2)}, u32[]{:S(2)}) collective-permute-start(bf16[256,1280]{1,0:T(8,128)(2,1)} %fusion.3), channel_id=1, source_target_pairs={{0,2},{2,0},{1,3},{3,1},{4,6},{6,4},{5,7},{7,5},{8,10},{10,8},{9,1... | collective-permute-start | bytes 1966088 | tf_op jit(solution)/shard_map/ppermute | solution.py:294
  90.7 4.3 %all-to-all-done.2.terms_ref = bf16[4,40,1280]{2,1,0:T(8,128)(2,1)S(1)} async-done(((bf16[4,40,1280]{2,1,0:T(8,128)(2,1)}), bf16[4,40,1280]{2,1,0:T(8,128)(2,1)S(1)}, u32[]{:S(2)}, u32[]{:S(2)}) %all-to-all-start.2) | async-done | bytes 409632 | tf_op jit(solution)/shard_map/all_to_all | solution.py:384
  95.0 0.8 shard_map.108
  95.8 9.3 %all-to-all-start.3 = ((bf16[4,40,1280]{2,1,0:T(8,128)(2,1)}), bf16[4,40,1280]{2,1,0:T(8,128)(2,1)S(1)}, u32[]{:S(2)}, u32[]{:S(2)}) async-start(bf16[4,40,1280]{2,1,0:T(8,128)(2,1)} %shard_map.108), calls=%async_computation.3 | async-start | bytes 819200 | tf_op jit(solution)/shard_map/all_to_all | solution.py:388
  105.2 0.1 broadcast_in_dim.66
  105.2 0.1 broadcast_in_dim.67
  105.3 2.8 %collective-permute-done.7 = bf16[256,1280]{1,0:T(8,128)(2,1)S(1)} collective-permute-done((bf16[256,1280]{1,0:T(8,128)(2,1)}, bf16[256,1280]{1,0:T(8,128)(2,1)S(1)}, u32[]{:S(2)}, u32[]{:S(2)}) %collective-permute-start.7) | collective-permute-done | bytes 655392 | tf_op jit(solution)/shard_map/ppermute | solution.py:294
  108.2 10.6 %all-to-all-done.3.terms_ref = bf16[4,40,1280]{2,1,0:T(8,128)(2,1)S(1)} async-done(((bf16[4,40,1280]{2,1,0:T(8,128)(2,1)}), bf16[4,40,1280]{2,1,0:T(8,128)(2,1)S(1)}, u32[]{:S(2)}, u32[]{:S(2)}) %all-to-all-start.3) | async-done | bytes 409632 | tf_op jit(solution)/shard_map/all_to_all | solution.py:388
  118.8 0.1 shard_map.109
  118.9 3.2 %collective-permute-start.9 = (bf16[40,1280]{1,0:T(8,128)(2,1)S(1)}, bf16[40,1280]{1,0:T(8,128)(2,1)S(1)}, u32[]{:S(2)}, u32[]{:S(2)}) collective-permute-start(bf16[40,1280]{1,0:T(8,128)(2,1)S(1)} %bitcast.28), channel_id=1, source_target_pairs={{0,64},{2,0},{64,66},{66,2},{128,130},{130,194},{192,128},{194,192... | collective-permute-start | bytes 307208 | tf_op jit(solution)/shard_map/ppermute | solution.py:392
  122.1 2.0 %collective-permute-start.8 = (bf16[40,1280]{1,0:T(8,128)(2,1)S(1)}, bf16[40,1280]{1,0:T(8,128)(2,1)S(1)}, u32[]{:S(2)}, u32[]{:S(2)}) collective-permute-start(bf16[40,1280]{1,0:T(8,128)(2,1)S(1)} %bitcast.29), channel_id=1, source_target_pairs={{0,66},{66,0},{130,192},{192,130},{1,67},{67,1},{131,193},{193,131... | collective-permute-start | bytes 307208 | tf_op jit(solution)/shard_map/ppermute | solution.py:393
  124.1 0.0 copy-done.2
  124.1 2.3 %fusion.2 = bf16[256,1280]{1,0:T(8,128)(2,1)} fusion(bf16[256,1280]{1,0:T(8,128)(2,1)S(1)} %collective-permute-done.7, bf16[256,1280]{1,0:T(8,128)(2,1)S(1)} %copy-done.2, bf16[2,256,1280]{2,1,0:T(8,128)(2,1)} %collective-permute-done.6, bf16[2,256,1280]{2,1,0:T(8,128)(2,1)S(1)} %get-tuple-element.25, pred[256]{0:T(512)(128)(4,1)S(1)} %iota_compare_fusion), kind=kLoop, calls=%fused_computation.3 | loop fusion | flops 2949120 | bytes 3277056 | tf_op jit(solution)/shard_map/convert_element_type | solution.py:396
  126.4 3.3 %collective-permute-done.8 = bf16[40,1280]{1,0:T(8,128)(2,1)S(1)} collective-permute-done((bf16[40,1280]{1,0:T(8,128)(2,1)S(1)}, bf16[40,1280]{1,0:T(8,128)(2,1)S(1)}, u32[]{:S(2)}, u32[]{:S(2)}) %collective-permute-start.8) | collective-permute-done | bytes 102432 | tf_op jit(solution)/shard_map/ppermute | solution.py:393
  129.7 0.0 collective-permute-done.9
  129.7 0.1 bitcast_select_fusion.1
  129.8 2.4 %collective-permute-start.10 = (bf16[80,1280]{1,0:T(8,128)(2,1)S(1)}, bf16[80,1280]{1,0:T(8,128)(2,1)S(1)}, u32[]{:S(2)}, u32[]{:S(2)}) collective-permute-start(bf16[80,1280]{1,0:T(8,128)(2,1)S(1)} %bitcast_select_fusion.1), channel_id=1, source_target_pairs={{0,1},{1,0},{2,3},{3,2},{4,5},{5,4},{6,7},{7,6},{8,9},{9,8},{10,11... | collective-permute-start | bytes 614408 | tf_op jit(solution)/shard_map/ppermute | solution.py:291
  132.2 0.1 broadcast_in_dim.63
  132.3 0.1 broadcast_in_dim.64
  132.4 0.9 collective-permute-done.10
  133.3 0.9 bitcast_select_fusion
  (4 shorter events, 0.0 us)
Async XLA Ops:
  5.2 6.0 %copy-start.3 = (bf16[272,1280]{1,0:T(8,128)(2,1)S(1)}, bf16[272,1280]{1,0:T(8,128)(2,1)}, u32[]{:S(2)}) copy-start(bf16[272,1280]{1,0:T(8,128)(2,1)} %get-tuple-element.16.x0_ref) | copy-start | bytes 2088964
  5.3 10.0 %copy-start.1 = (bf16[256,1280]{1,0:T(8,128)(2,1)S(1)}, bf16[256,1280]{1,0:T(8,128)(2,1)}, u32[]{:S(2)}) copy-start(bf16[256,1280]{1,0:T(8,128)(2,1)} %c0_ref.1) | copy-start | bytes 1966084
  5.3 45.1 %copy-start = (s32[32]{0:T(128)S(1)}, s32[32]{0:T(128)}, u32[]{:S(2)}) copy-start(s32[32]{0:T(128)} %constant.58.clone.order_ref) | copy-start | bytes 388
  5.3 45.1 %all-to-all-start = ((bf16[8,2,80,1280]{3,2,1,0:T(8,128)(2,1)}), bf16[8,2,80,1280]{3,2,1,0:T(8,128)(2,1)}, u32[]{:S(2)}, u32[]{:S(2)}) async-start(bf16[8,2,80,1280]{3,2,1,0:T(8,128)(2,1)} %get-tuple-element.17), calls=%async_computation | async-start | bytes 6553600 | tf_op jit(solution)/shard_map/all_to_all | solution.py:320
  11.3 15.8 %collective-permute-start.1 = (bf16[272,1280]{1,0:T(8,128)(2,1)S(1)}, bf16[272,1280]{1,0:T(8,128)(2,1)S(1)}, u32[]{:S(2)}, u32[]{:S(2)}) collective-permute-start(bf16[272,1280]{1,0:T(8,128)(2,1)S(1)} %copy-done.3), channel_id=1, source_target_pairs={{0,2},{2,0},{1,3},{3,1},{4,6},{6,4},{5,7},{7,5},{8,10},{10,8},{9,1... | collective-permute-start | bytes 2088968 | tf_op jit(solution)/shard_map/ppermute | solution.py:294
  15.3 25.8 %collective-permute-start.4 = (bf16[256,1280]{1,0:T(8,128)(2,1)S(1)}, bf16[256,1280]{1,0:T(8,128)(2,1)S(1)}, u32[]{:S(2)}, u32[]{:S(2)}) collective-permute-start(bf16[256,1280]{1,0:T(8,128)(2,1)S(1)} %copy-done.1), channel_id=1, source_target_pairs={{0,2},{2,0},{1,3},{3,1},{4,6},{6,4},{5,7},{7,5},{8,10},{10,8},{9,1... | collective-permute-start | bytes 1966088 | tf_op jit(solution)/shard_map/ppermute | solution.py:294
  17.2 30.6 %collective-permute-start = (bf16[272,1280]{1,0:T(8,128)(2,1)S(1)}, bf16[272,1280]{1,0:T(8,128)(2,1)S(1)}, u32[]{:S(2)}, u32[]{:S(2)}) collective-permute-start(bf16[272,1280]{1,0:T(8,128)(2,1)S(1)} %copy-done.3), channel_id=1, source_target_pairs={{0,1},{1,0},{2,3},{3,2},{4,5},{5,4},{6,7},{7,6},{8,9},{9,8},{10,11... | collective-permute-start | bytes 2088968 | tf_op jit(solution)/shard_map/ppermute | solution.py:291
  27.1 23.3 %copy-start.4 = (bf16[272,1280]{1,0:T(8,128)(2,1)}, bf16[272,1280]{1,0:T(8,128)(2,1)S(1)}, u32[]{:S(2)}) copy-start(bf16[272,1280]{1,0:T(8,128)(2,1)S(1)} %collective-permute-done.1.x2_ref) | copy-start | bytes 2088964
  27.1 23.3 %collective-permute-start.2 = (bf16[272,1280]{1,0:T(8,128)(2,1)S(1)}, bf16[272,1280]{1,0:T(8,128)(2,1)}, u32[]{:S(2)}, u32[]{:S(2)}) collective-permute-start(bf16[272,1280]{1,0:T(8,128)(2,1)S(1)} %collective-permute-done.1.x2_ref), channel_id=1, source_target_pairs={{0,1},{1,0},{2,3},{3,2},{4,5},{5,4},{6,7},{7,6},{8,9},{9,8},{10,11... | collective-permute-start | bytes 2088968 | tf_op jit(solution)/shard_map/ppermute | solution.py:291
  39.1 8.7 %collective-permute-start.3 = (bf16[256,1280]{1,0:T(8,128)(2,1)S(1)}, bf16[256,1280]{1,0:T(8,128)(2,1)S(1)}, u32[]{:S(2)}, u32[]{:S(2)}) collective-permute-start(bf16[256,1280]{1,0:T(8,128)(2,1)S(1)} %copy-done.1), channel_id=1, source_target_pairs={{0,1},{1,0},{2,3},{3,2},{4,5},{5,4},{6,7},{7,6},{8,9},{9,8},{10,11... | collective-permute-start | bytes 1966088 | tf_op jit(solution)/shard_map/ppermute | solution.py:291
  41.1 6.7 %copy-start.6 = (bf16[256,1280]{1,0:T(8,128)(2,1)}, bf16[256,1280]{1,0:T(8,128)(2,1)S(1)}, u32[]{:S(2)}) copy-start(bf16[256,1280]{1,0:T(8,128)(2,1)S(1)} %collective-permute-done.4.c2_ref) | copy-start | bytes 1966084
  41.1 8.4 %collective-permute-start.5 = (bf16[256,1280]{1,0:T(8,128)(2,1)S(1)}, bf16[256,1280]{1,0:T(8,128)(2,1)S(1)}, u32[]{:S(2)}, u32[]{:S(2)}) collective-permute-start(bf16[256,1280]{1,0:T(8,128)(2,1)S(1)} %collective-permute-done.4.c2_ref), channel_id=1, source_target_pairs={{0,1},{1,0},{2,3},{3,2},{4,5},{5,4},{6,7},{7,6},{8,9},{9,8},{10,11... | collective-permute-start | bytes 1966088 | tf_op jit(solution)/shard_map/ppermute | solution.py:291
  47.8 2.5 %copy-start.5 = (bf16[272,1280]{1,0:T(8,128)(2,1)}, bf16[272,1280]{1,0:T(8,128)(2,1)S(1)}, u32[]{:S(2)}) copy-start(bf16[272,1280]{1,0:T(8,128)(2,1)S(1)} %collective-permute-done.x1_ref) | copy-start | bytes 2088964
  49.5 0.8 copy-start.7
  60.8 17.4 %all-to-all-start.1 = ((bf16[8,40,1280]{2,1,0:T(8,128)(2,1)}), bf16[8,40,1280]{2,1,0:T(8,128)(2,1)S(1)}, u32[]{:S(2)}, u32[]{:S(2)}) async-start(bf16[8,40,1280]{2,1,0:T(8,128)(2,1)} %bitcast.31), calls=%async_computation.1 | async-start | bytes 1638400 | tf_op jit(solution)/shard_map/all_to_all | solution.py:379
  70.3 14.9 %collective-permute-start.6 = (bf16[2,256,1280]{2,1,0:T(8,128)(2,1)}, bf16[2,256,1280]{2,1,0:T(8,128)(2,1)}, u32[]{:S(2)}, u32[]{:S(2)}) collective-permute-start(bf16[2,256,1280]{2,1,0:T(8,128)(2,1)} %get-tuple-element.22), channel_id=1, source_target_pairs={{0,1},{1,0},{2,3},{3,2},{4,5},{5,4},{6,7},{7,6},{8,9},{9,8},{10,11... | collective-permute-start | bytes 3932168 | tf_op jit(solution)/shard_map/ppermute | solution.py:291
  79.0 16.0 %all-to-all-start.2 = ((bf16[4,40,1280]{2,1,0:T(8,128)(2,1)}), bf16[4,40,1280]{2,1,0:T(8,128)(2,1)S(1)}, u32[]{:S(2)}, u32[]{:S(2)}) async-start(bf16[4,40,1280]{2,1,0:T(8,128)(2,1)} %shard_map.107), calls=%async_computation.2 | async-start | bytes 819200 | tf_op jit(solution)/shard_map/all_to_all | solution.py:384
  87.3 36.8 %copy-start.2 = (bf16[256,1280]{1,0:T(8,128)(2,1)S(1)}, bf16[256,1280]{1,0:T(8,128)(2,1)}, u32[]{:S(2)}) copy-start(bf16[256,1280]{1,0:T(8,128)(2,1)} %patches_ref.1) | copy-start | bytes 1966084
  87.3 20.9 %collective-permute-start.7 = (bf16[256,1280]{1,0:T(8,128)(2,1)}, bf16[256,1280]{1,0:T(8,128)(2,1)S(1)}, u32[]{:S(2)}, u32[]{:S(2)}) collective-permute-start(bf16[256,1280]{1,0:T(8,128)(2,1)} %fusion.3), channel_id=1, source_target_pairs={{0,2},{2,0},{1,3},{3,1},{4,6},{6,4},{5,7},{7,5},{8,10},{10,8},{9,1... | collective-permute-start | bytes 1966088 | tf_op jit(solution)/shard_map/ppermute | solution.py:294
  95.8 23.0 %all-to-all-start.3 = ((bf16[4,40,1280]{2,1,0:T(8,128)(2,1)}), bf16[4,40,1280]{2,1,0:T(8,128)(2,1)S(1)}, u32[]{:S(2)}, u32[]{:S(2)}) async-start(bf16[4,40,1280]{2,1,0:T(8,128)(2,1)} %shard_map.108), calls=%async_computation.3 | async-start | bytes 819200 | tf_op jit(solution)/shard_map/all_to_all | solution.py:388
  118.9 10.8 %collective-permute-start.9 = (bf16[40,1280]{1,0:T(8,128)(2,1)S(1)}, bf16[40,1280]{1,0:T(8,128)(2,1)S(1)}, u32[]{:S(2)}, u32[]{:S(2)}) collective-permute-start(bf16[40,1280]{1,0:T(8,128)(2,1)S(1)} %bitcast.28), channel_id=1, source_target_pairs={{0,64},{2,0},{64,66},{66,2},{128,130},{130,194},{192,128},{194,192... | collective-permute-start | bytes 307208 | tf_op jit(solution)/shard_map/ppermute | solution.py:392
  122.1 7.6 %collective-permute-start.8 = (bf16[40,1280]{1,0:T(8,128)(2,1)S(1)}, bf16[40,1280]{1,0:T(8,128)(2,1)S(1)}, u32[]{:S(2)}, u32[]{:S(2)}) collective-permute-start(bf16[40,1280]{1,0:T(8,128)(2,1)S(1)} %bitcast.29), channel_id=1, source_target_pairs={{0,66},{66,0},{130,192},{192,130},{1,67},{67,1},{131,193},{193,131... | collective-permute-start | bytes 307208 | tf_op jit(solution)/shard_map/ppermute | solution.py:393
  129.8 3.5 %collective-permute-start.10 = (bf16[80,1280]{1,0:T(8,128)(2,1)S(1)}, bf16[80,1280]{1,0:T(8,128)(2,1)S(1)}, u32[]{:S(2)}, u32[]{:S(2)}) collective-permute-start(bf16[80,1280]{1,0:T(8,128)(2,1)S(1)} %bitcast_select_fusion.1), channel_id=1, source_target_pairs={{0,1},{1,0},{2,3},{3,2},{4,5},{5,4},{6,7},{7,6},{8,9},{9,8},{10,11... | collective-permute-start | bytes 614408 | tf_op jit(solution)/shard_map/ppermute | solution.py:291

commit v6 on v4

--- a/solution.py
+++ b/solution.py
@@ -57,6 +57,22 @@
     (2 * x + half, 2 * x + (1 - half) if owns(x, half) else 2 * (x ^ 1) + half) for x in range(4) for half in range(2)
 ]
 ACROSS = [(2 * x + half, 2 * (x ^ 1) + (1 - half)) for x in range(4) for half in range(2) if not owns(x, half)]
+
+
+CROSS = ("y_lo", "y_hi", "z_quad", "z_pair", "core")
+
+
+def cross_groups(first):
+    def place(y_lo, y, z, half, core):
+        return (((y_lo * Y_HI + y % Y_HI) * Z_QUAD + z % Z_QUAD) * Z_PAIR + half) * CORES + core
+
+    groups = []
+    for y_lo in range(2):
+        for half in range(Z_PAIR):
+            for other in range(4):
+                groups.append([place(y_lo, other, z + 2 * half, half, first) for z in range(Z_QUAD)])
+                groups.append([place(y_lo, y + 2 * y_lo, other, half, 1 - first) for y in range(Y_HI)])
+    return groups
 
 
 def half_of(place_ref):
@@ -373,11 +389,11 @@
     grad = sum_of(grad, Z_QUAD)
     from_core = to_core(send_out)
     for_pair = (keep_out[1].astype(F32) + from_core[1].astype(F32)).astype(BF16)
-    grad = lax.all_to_all(grad, "z_quad", 0, 0)
+    grad = lax.all_to_all(grad, CROSS, 0, 0, axis_index_groups=cross_groups(0))
     grad, from_core_late = lax.optimization_barrier((grad, from_core))
     grad = sum_of(grad, Y_HI)
     from_pair = to_pair(for_pair)
-    grad = lax.all_to_all(grad, "y_hi", 0, 0)
+    grad = lax.all_to_all(grad, CROSS, 0, 0, axis_index_groups=cross_groups(1))
     grad, from_pair = lax.optimization_barrier((grad, from_pair))
     grad = sum_of(grad, 1)[0]
 

time: 138 us -> 134 us (0.971)
  starting transfers between devices: 84.2 us -> 74.6 us
  waiting for transfers between devices: 24.6 us -> 30.1 us
    all_to_all x2, waiting for transfers between devices: 6.8 us -> 15.4 us  [the longest x1 12.1 us: shards(): grad = lax.all_to_all(grad, CROSS, 0, 0, axis_index_groups=cross_groups(1))]
    ppermute x1, starting transfers between devices: 8.32 us -> 1.92 us  [shards(): second = lax.ppermute(grad, ('x', 'z_pair'), ACROSS)]
    ppermute x3, waiting for transfers between devices: 9.87 us -> 4.33 us  [to_pair(): return lax.ppermute(value, 'z_pair', PAIR_SWAP)]
    ppermute x6, starting transfers between devices: 38.3 us -> 33.8 us  [to_core(): return lax.ppermute(value, 'core', CORE_SWAP)]
    ppermute x1, waiting for transfers between devices: 0.01 us -> 2.51 us  [shards(): second = lax.ppermute(grad, ('x', 'z_pair'), ACROSS)]
  transfers between devices with their start and end apart: 15 -> 15, of which waited for: 7 -> 8; matrix products, arithmetic and copies ran while one was open for 3% -> 4% of each run, Pallas kernels for 4% -> 5%
where the time goes in v6:
time: 134 us; the launch traced here: 133 us
  starting transfers between devices  74.6 us (56%)
  waiting for transfers between devices  30.1 us (22%)
  Pallas kernels  20.4 us (15%)
  other arithmetic  5.37 us (4%)
  between operations  1.54 us (1%)
    ppermute x6, starting transfers between devices, to_core(): return lax.ppermute(value, 'core', CORE_SWAP)  33.8 us
    all_to_all x1, waiting for transfers between devices, shards(): grad = lax.all_to_all(grad, CROSS, 0, 0, axis_index_groups=cross_groups(1))  12.1 us
    pallas_call x1, Pallas kernels, shards(): call(attention_kernel, (array(4 * HEAD, 4 * ROWS), array(4 * HEAD, WIDTH)...  10.4 us
    all_to_all x1, starting transfers between devices, shards(): grad = lax.all_to_all(grad, CROSS, 0, 0, axis_index_groups=cross_groups(1))  9.64 us
    ppermute x3, starting transfers between devices, to_pair(): return lax.ppermute(value, 'z_pair', PAIR_SWAP)  9.37 us
    all_to_all x1, starting transfers between devices, shards(): grad = lax.all_to_all(grad, CROSS, 0, 0, axis_index_groups=cross_groups(0))  6.15 us
    all_to_all x1, starting transfers between devices, shards(): blocks = lax.all_to_all(own, FSDP, 0, 0).reshape(16, HEAD, WIDTH)  6.01 us
    all_to_all x1, waiting for transfers between devices, shards(): grad = lax.all_to_all(grad.reshape(8, 40, WIDTH), FSDP, 0, 0)  5.33 us
  transfers between devices with their start and end apart: 15, of which 8 were waited for; matrix products, arithmetic and copies ran while one was open for 4% of the time, Pallas kernels for 5%

profile of v6, /device:TPU:1, one launch (start us, length us, event | category | flops | bytes accessed | tf_op | source)
XLA Modules:
  0.0 133.2 jit_solution(441989331994329738)
XLA Ops:
  1.3 3.9 %shard_map.104 = (bf16[272,1280]{1,0:T(8,128)(2,1)}, bf16[8,2,80,1280]{3,2,1,0:T(8,128)(2,1)}) custom-call(s32[1]{0:T(128)} %bitcast.place_ref, s32[32]{0:T(128)} %constant.57.clone.sends_ref, s32[1]{0:T(128)S(6)} %copy.11.count_ref, bf16[256,1280]{1,0:T(8,128)(2,1)} %patches_ref.1, f32[1280]{0:T(1024)} %gain_ref.1, s32[256]{0:T(256)} %images_ref.1, ...), custom_call_target="tpu_custom_call" | custom-call | bytes 6291456 | tf_op jit(solution)/shard_map/pallas_call | solution.py:304
  5.2 0.0 copy-start.3
  5.3 0.0 copy-start.1
  5.3 0.0 copy-start
  5.3 6.0 %all-to-all-start = ((bf16[8,2,80,1280]{3,2,1,0:T(8,128)(2,1)}), bf16[8,2,80,1280]{3,2,1,0:T(8,128)(2,1)}, u32[]{:S(2)}, u32[]{:S(2)}) async-start(bf16[8,2,80,1280]{3,2,1,0:T(8,128)(2,1)} %get-tuple-element.17), calls=%async_computation | async-start | bytes 6553600 | tf_op jit(solution)/shard_map/all_to_all | solution.py:328
  11.3 0.0 copy-done.3
  11.3 4.0 %collective-permute-start.1 = (bf16[272,1280]{1,0:T(8,128)(2,1)S(1)}, bf16[272,1280]{1,0:T(8,128)(2,1)S(1)}, u32[]{:S(2)}, u32[]{:S(2)}) collective-permute-start(bf16[272,1280]{1,0:T(8,128)(2,1)S(1)} %copy-done.3), channel_id=1, source_target_pairs={{0,2},{2,0},{1,3},{3,1},{4,6},{6,4},{5,7},{7,5},{8,10},{10,8},{9,1... | collective-permute-start | bytes 2088968 | tf_op jit(solution)/shard_map/ppermute | solution.py:302
  15.3 0.0 copy-done.1
  15.3 1.9 %collective-permute-start.4 = (bf16[256,1280]{1,0:T(8,128)(2,1)S(1)}, bf16[256,1280]{1,0:T(8,128)(2,1)S(1)}, u32[]{:S(2)}, u32[]{:S(2)}) collective-permute-start(bf16[256,1280]{1,0:T(8,128)(2,1)S(1)} %copy-done.1), channel_id=1, source_target_pairs={{0,2},{2,0},{1,3},{3,1},{4,6},{6,4},{5,7},{7,5},{8,10},{10,8},{9,1... | collective-permute-start | bytes 1966088 | tf_op jit(solution)/shard_map/ppermute | solution.py:302
  17.2 7.3 %collective-permute-start = (bf16[272,1280]{1,0:T(8,128)(2,1)S(1)}, bf16[272,1280]{1,0:T(8,128)(2,1)S(1)}, u32[]{:S(2)}, u32[]{:S(2)}) collective-permute-start(bf16[272,1280]{1,0:T(8,128)(2,1)S(1)} %copy-done.3), channel_id=1, source_target_pairs={{0,1},{1,0},{2,3},{3,2},{4,5},{5,4},{6,7},{7,6},{8,9},{9,8},{10,11... | collective-permute-start | bytes 2088968 | tf_op jit(solution)/shard_map/ppermute | solution.py:299
  24.6 2.5 %collective-permute-done.1.x2_ref = bf16[272,1280]{1,0:T(8,128)(2,1)S(1)} collective-permute-done((bf16[272,1280]{1,0:T(8,128)(2,1)S(1)}, bf16[272,1280]{1,0:T(8,128)(2,1)S(1)}, u32[]{:S(2)}, u32[]{:S(2)}) %collective-permute-start.1) | collective-permute-done | bytes 696352 | tf_op jit(solution)/shard_map/ppermute | solution.py:302
  27.1 0.0 copy-start.4
  27.1 12.1 %collective-permute-start.2 = (bf16[272,1280]{1,0:T(8,128)(2,1)S(1)}, bf16[272,1280]{1,0:T(8,128)(2,1)}, u32[]{:S(2)}, u32[]{:S(2)}) collective-permute-start(bf16[272,1280]{1,0:T(8,128)(2,1)S(1)} %collective-permute-done.1.x2_ref), channel_id=1, source_target_pairs={{0,1},{1,0},{2,3},{3,2},{4,5},{5,4},{6,7},{7,6},{8,9},{9,8},{10,11... | collective-permute-start | bytes 2088968 | tf_op jit(solution)/shard_map/ppermute | solution.py:299
  39.1 1.9 %collective-permute-start.3 = (bf16[256,1280]{1,0:T(8,128)(2,1)S(1)}, bf16[256,1280]{1,0:T(8,128)(2,1)S(1)}, u32[]{:S(2)}, u32[]{:S(2)}) collective-permute-start(bf16[256,1280]{1,0:T(8,128)(2,1)S(1)} %copy-done.1), channel_id=1, source_target_pairs={{0,1},{1,0},{2,3},{3,2},{4,5},{5,4},{6,7},{7,6},{8,9},{9,8},{10,11... | collective-permute-start | bytes 1966088 | tf_op jit(solution)/shard_map/ppermute | solution.py:299
  41.1 0.0 collective-permute-done.4.c2_ref
  41.1 0.0 copy-start.6
  41.1 6.7 %collective-permute-start.5 = (bf16[256,1280]{1,0:T(8,128)(2,1)S(1)}, bf16[256,1280]{1,0:T(8,128)(2,1)S(1)}, u32[]{:S(2)}, u32[]{:S(2)}) collective-permute-start(bf16[256,1280]{1,0:T(8,128)(2,1)S(1)} %collective-permute-done.4.c2_ref), channel_id=1, source_target_pairs={{0,1},{1,0},{2,3},{3,2},{4,5},{5,4},{6,7},{7,6},{8,9},{9,8},{10,11... | collective-permute-start | bytes 1966088 | tf_op jit(solution)/shard_map/ppermute | solution.py:299
  47.8 0.0 collective-permute-done.3.c1_ref
  47.8 0.0 collective-permute-done.x1_ref
  47.8 0.0 copy-done.6
  47.8 0.0 copy-start.5
  47.8 1.7 %collective-permute-done.5.c3_ref = bf16[256,1280]{1,0:T(8,128)(2,1)S(1)} collective-permute-done((bf16[256,1280]{1,0:T(8,128)(2,1)S(1)}, bf16[256,1280]{1,0:T(8,128)(2,1)S(1)}, u32[]{:S(2)}, u32[]{:S(2)}) %collective-permute-start.5) | collective-permute-done | bytes 655392 | tf_op jit(solution)/shard_map/ppermute | solution.py:299
  49.5 0.0 copy-start.7
  49.5 0.8 copy-done.7
  50.3 0.0 collective-permute-done.2.x3_ref
  50.3 0.0 all-to-all-done
  50.3 0.0 copy-done.5
  50.3 0.0 copy-done.4
  50.3 0.0 copy-done
  50.4 10.4 %shard_map.105 = (bf16[320,1024]{1,0:T(8,128)(2,1)S(1)}, bf16[320,1280]{1,0:T(8,128)(2,1)}) custom-call(s32[1]{0:T(128)} %bitcast.place_ref, s32[32]{0:T(128)S(1)} %copy-done, bf16[272,1280]{1,0:T(8,128)(2,1)} %get-tuple-element.16.x0_ref, bf16[272,1280]{1,0:T(8,128)(2,1)} %copy-done.5, bf16[272,1280]{1,0:T(8,128)(2,1)} %copy-done.4, ...), custom_call_target="tpu_custom_call" | custom-call | flops 3892314112 | bytes 12582912 | tf_op jit(solution)/shard_map/pallas_call | solution.py:337
  60.8 5.2 %all-to-all-start.1 = ((bf16[8,40,1280]{2,1,0:T(8,128)(2,1)}), bf16[8,40,1280]{2,1,0:T(8,128)(2,1)S(1)}, u32[]{:S(2)}, u32[]{:S(2)}) async-start(bf16[8,40,1280]{2,1,0:T(8,128)(2,1)} %bitcast.31), calls=%async_computation.1 | async-start | bytes 1638400 | tf_op jit(solution)/shard_map/all_to_all | solution.py:387
  65.9 4.4 %shard_map.106 = (bf16[2,256,1280]{2,1,0:T(8,128)(2,1)S(1)}, bf16[2,256,1280]{2,1,0:T(8,128)(2,1)}) custom-call(s32[1]{0:T(128)} %bitcast.place_ref, s32[32]{0:T(128)S(1)} %copy-done, bf16[320,1024]{1,0:T(8,128)(2,1)S(1)} %get-tuple-element.19.from_ref, bf16[16,80,1280]{2,1,0:T(8,128)(2,1)} %bitcast.4.blocks_ref), custom_call_target="tpu_custom_call" | custom-call | flops 838860800 | bytes 6291456 | tf_op jit(solution)/shard_map/pallas_call | solution.py:369
  70.3 2.6 %collective-permute-start.6 = (bf16[2,256,1280]{2,1,0:T(8,128)(2,1)}, bf16[2,256,1280]{2,1,0:T(8,128)(2,1)}, u32[]{:S(2)}, u32[]{:S(2)}) collective-permute-start(bf16[2,256,1280]{2,1,0:T(8,128)(2,1)} %get-tuple-element.22), channel_id=1, source_target_pairs={{0,1},{1,0},{2,3},{3,2},{4,5},{5,4},{6,7},{7,6},{8,9},{9,8},{10,11... | collective-permute-start | bytes 3932168 | tf_op jit(solution)/shard_map/ppermute | solution.py:299
  72.8 5.3 %all-to-all-done.1.terms_ref = bf16[8,40,1280]{2,1,0:T(8,128)(2,1)S(1)} async-done(((bf16[8,40,1280]{2,1,0:T(8,128)(2,1)}), bf16[8,40,1280]{2,1,0:T(8,128)(2,1)S(1)}, u32[]{:S(2)}, u32[]{:S(2)}) %all-to-all-start.1) | async-done | bytes 819232 | tf_op jit(solution)/shard_map/all_to_all | solution.py:387
  78.2 0.9 shard_map.107
  79.0 6.1 %all-to-all-start.2 = ((bf16[4,40,1280]{2,1,0:T(8,128)(2,1)}), bf16[4,40,1280]{2,1,0:T(8,128)(2,1)S(1)}, u32[]{:S(2)}, u32[]{:S(2)}) async-start(bf16[4,40,1280]{2,1,0:T(8,128)(2,1)} %shard_map.107), calls=%async_computation.2 | async-start | bytes 819200 | tf_op jit(solution)/shard_map/all_to_all | solution.py:392
  85.2 0.0 collective-permute-done.6
  85.2 2.1 %fusion.3 = bf16[256,1280]{1,0:T(8,128)(2,1)} fusion(bf16[2,256,1280]{2,1,0:T(8,128)(2,1)} %collective-permute-done.6, bf16[2,256,1280]{2,1,0:T(8,128)(2,1)S(1)} %get-tuple-element.25), kind=kLoop, calls=%fused_computation.5 | loop fusion | flops 1310720 | bytes 1966080 | tf_op jit(solution)/shard_map/convert_element_type | solution.py:391
  87.3 0.0 copy-start.2
  87.3 3.4 %collective-permute-start.7 = (bf16[256,1280]{1,0:T(8,128)(2,1)}, bf16[256,1280]{1,0:T(8,128)(2,1)S(1)}, u32[]{:S(2)}, u32[]{:S(2)}) collective-permute-start(bf16[256,1280]{1,0:T(8,128)(2,1)} %fusion.3), channel_id=1, source_target_pairs={{0,2},{2,0},{1,3},{3,1},{4,6},{6,4},{5,7},{7,5},{8,10},{10,8},{9,1... | collective-permute-start | bytes 1966088 | tf_op jit(solution)/shard_map/ppermute | solution.py:302
  90.7 3.3 %all-to-all-done.2.terms_ref = bf16[4,40,1280]{2,1,0:T(8,128)(2,1)S(1)} async-done(((bf16[4,40,1280]{2,1,0:T(8,128)(2,1)}), bf16[4,40,1280]{2,1,0:T(8,128)(2,1)S(1)}, u32[]{:S(2)}, u32[]{:S(2)}) %all-to-all-start.2) | async-done | bytes 409632 | tf_op jit(solution)/shard_map/all_to_all | solution.py:392
  94.0 0.8 shard_map.108
  94.8 9.6 %all-to-all-start.3 = ((bf16[4,40,1280]{2,1,0:T(8,128)(2,1)}), bf16[4,40,1280]{2,1,0:T(8,128)(2,1)S(1)}, u32[]{:S(2)}, u32[]{:S(2)}) async-start(bf16[4,40,1280]{2,1,0:T(8,128)(2,1)} %shard_map.108), calls=%async_computation.3 | async-start | bytes 819200 | tf_op jit(solution)/shard_map/all_to_all | solution.py:396
  104.5 0.1 broadcast_in_dim.66
  104.5 0.1 broadcast_in_dim.67
  104.6 1.8 %collective-permute-done.7 = bf16[256,1280]{1,0:T(8,128)(2,1)S(1)} collective-permute-done((bf16[256,1280]{1,0:T(8,128)(2,1)}, bf16[256,1280]{1,0:T(8,128)(2,1)S(1)}, u32[]{:S(2)}, u32[]{:S(2)}) %collective-permute-start.7) | collective-permute-done | bytes 655392 | tf_op jit(solution)/shard_map/ppermute | solution.py:302
  106.5 12.1 %all-to-all-done.3.terms_ref = bf16[4,40,1280]{2,1,0:T(8,128)(2,1)S(1)} async-done(((bf16[4,40,1280]{2,1,0:T(8,128)(2,1)}), bf16[4,40,1280]{2,1,0:T(8,128)(2,1)S(1)}, u32[]{:S(2)}, u32[]{:S(2)}) %all-to-all-start.3) | async-done | bytes 409632 | tf_op jit(solution)/shard_map/all_to_all | solution.py:396
  118.5 0.1 shard_map.109
  118.6 2.5 %collective-permute-start.9 = (bf16[40,1280]{1,0:T(8,128)(2,1)S(1)}, bf16[40,1280]{1,0:T(8,128)(2,1)S(1)}, u32[]{:S(2)}, u32[]{:S(2)}) collective-permute-start(bf16[40,1280]{1,0:T(8,128)(2,1)S(1)} %bitcast.28), channel_id=1, source_target_pairs={{0,64},{2,0},{64,66},{66,2},{128,130},{130,194},{192,128},{194,192... | collective-permute-start | bytes 307208 | tf_op jit(solution)/shard_map/ppermute | solution.py:400
  121.1 1.9 %collective-permute-start.8 = (bf16[40,1280]{1,0:T(8,128)(2,1)S(1)}, bf16[40,1280]{1,0:T(8,128)(2,1)S(1)}, u32[]{:S(2)}, u32[]{:S(2)}) collective-permute-start(bf16[40,1280]{1,0:T(8,128)(2,1)S(1)} %bitcast.29), channel_id=1, source_target_pairs={{0,66},{66,0},{130,192},{192,130},{1,67},{67,1},{131,193},{193,131... | collective-permute-start | bytes 307208 | tf_op jit(solution)/shard_map/ppermute | solution.py:401
  123.0 0.0 copy-done.2
  123.1 2.3 %fusion.2 = bf16[256,1280]{1,0:T(8,128)(2,1)} fusion(bf16[256,1280]{1,0:T(8,128)(2,1)S(1)} %collective-permute-done.7, bf16[256,1280]{1,0:T(8,128)(2,1)S(1)} %copy-done.2, bf16[2,256,1280]{2,1,0:T(8,128)(2,1)} %collective-permute-done.6, bf16[2,256,1280]{2,1,0:T(8,128)(2,1)S(1)} %get-tuple-element.25, pred[256]{0:T(512)(128)(4,1)S(1)} %iota_compare_fusion), kind=kLoop, calls=%fused_computation.3 | loop fusion | flops 2949120 | bytes 3277056 | tf_op jit(solution)/shard_map/convert_element_type | solution.py:404
  125.4 2.5 %collective-permute-done.8 = bf16[40,1280]{1,0:T(8,128)(2,1)S(1)} collective-permute-done((bf16[40,1280]{1,0:T(8,128)(2,1)S(1)}, bf16[40,1280]{1,0:T(8,128)(2,1)S(1)}, u32[]{:S(2)}, u32[]{:S(2)}) %collective-permute-start.8) | collective-permute-done | bytes 102432 | tf_op jit(solution)/shard_map/ppermute | solution.py:401
  127.9 0.0 collective-permute-done.9
  127.9 0.1 bitcast_select_fusion.1
  128.0 3.2 %collective-permute-start.10 = (bf16[80,1280]{1,0:T(8,128)(2,1)S(1)}, bf16[80,1280]{1,0:T(8,128)(2,1)S(1)}, u32[]{:S(2)}, u32[]{:S(2)}) collective-permute-start(bf16[80,1280]{1,0:T(8,128)(2,1)S(1)} %bitcast_select_fusion.1), channel_id=1, source_target_pairs={{0,1},{1,0},{2,3},{3,2},{4,5},{5,4},{6,7},{7,6},{8,9},{9,8},{10,11... | collective-permute-start | bytes 614408 | tf_op jit(solution)/shard_map/ppermute | solution.py:299
  131.3 0.1 broadcast_in_dim.63
  131.3 0.1 broadcast_in_dim.64
  131.4 0.9 collective-permute-done.10
  132.3 0.9 bitcast_select_fusion
  (4 shorter events, 0.0 us)
Async XLA Ops:
  5.2 6.0 %copy-start.3 = (bf16[272,1280]{1,0:T(8,128)(2,1)S(1)}, bf16[272,1280]{1,0:T(8,128)(2,1)}, u32[]{:S(2)}) copy-start(bf16[272,1280]{1,0:T(8,128)(2,1)} %get-tuple-element.16.x0_ref) | copy-start | bytes 2088964
  5.3 10.0 %copy-start.1 = (bf16[256,1280]{1,0:T(8,128)(2,1)S(1)}, bf16[256,1280]{1,0:T(8,128)(2,1)}, u32[]{:S(2)}) copy-start(bf16[256,1280]{1,0:T(8,128)(2,1)} %c0_ref.1) | copy-start | bytes 1966084
  5.3 45.1 %copy-start = (s32[32]{0:T(128)S(1)}, s32[32]{0:T(128)}, u32[]{:S(2)}) copy-start(s32[32]{0:T(128)} %constant.58.clone.order_ref) | copy-start | bytes 388
  5.3 45.1 %all-to-all-start = ((bf16[8,2,80,1280]{3,2,1,0:T(8,128)(2,1)}), bf16[8,2,80,1280]{3,2,1,0:T(8,128)(2,1)}, u32[]{:S(2)}, u32[]{:S(2)}) async-start(bf16[8,2,80,1280]{3,2,1,0:T(8,128)(2,1)} %get-tuple-element.17), calls=%async_computation | async-start | bytes 6553600 | tf_op jit(solution)/shard_map/all_to_all | solution.py:328
  11.3 15.8 %collective-permute-start.1 = (bf16[272,1280]{1,0:T(8,128)(2,1)S(1)}, bf16[272,1280]{1,0:T(8,128)(2,1)S(1)}, u32[]{:S(2)}, u32[]{:S(2)}) collective-permute-start(bf16[272,1280]{1,0:T(8,128)(2,1)S(1)} %copy-done.3), channel_id=1, source_target_pairs={{0,2},{2,0},{1,3},{3,1},{4,6},{6,4},{5,7},{7,5},{8,10},{10,8},{9,1... | collective-permute-start | bytes 2088968 | tf_op jit(solution)/shard_map/ppermute | solution.py:302
  15.3 25.8 %collective-permute-start.4 = (bf16[256,1280]{1,0:T(8,128)(2,1)S(1)}, bf16[256,1280]{1,0:T(8,128)(2,1)S(1)}, u32[]{:S(2)}, u32[]{:S(2)}) collective-permute-start(bf16[256,1280]{1,0:T(8,128)(2,1)S(1)} %copy-done.1), channel_id=1, source_target_pairs={{0,2},{2,0},{1,3},{3,1},{4,6},{6,4},{5,7},{7,5},{8,10},{10,8},{9,1... | collective-permute-start | bytes 1966088 | tf_op jit(solution)/shard_map/ppermute | solution.py:302
  17.2 30.6 %collective-permute-start = (bf16[272,1280]{1,0:T(8,128)(2,1)S(1)}, bf16[272,1280]{1,0:T(8,128)(2,1)S(1)}, u32[]{:S(2)}, u32[]{:S(2)}) collective-permute-start(bf16[272,1280]{1,0:T(8,128)(2,1)S(1)} %copy-done.3), channel_id=1, source_target_pairs={{0,1},{1,0},{2,3},{3,2},{4,5},{5,4},{6,7},{7,6},{8,9},{9,8},{10,11... | collective-permute-start | bytes 2088968 | tf_op jit(solution)/shard_map/ppermute | solution.py:299
  27.1 23.3 %copy-start.4 = (bf16[272,1280]{1,0:T(8,128)(2,1)}, bf16[272,1280]{1,0:T(8,128)(2,1)S(1)}, u32[]{:S(2)}) copy-start(bf16[272,1280]{1,0:T(8,128)(2,1)S(1)} %collective-permute-done.1.x2_ref) | copy-start | bytes 2088964
  27.1 23.3 %collective-permute-start.2 = (bf16[272,1280]{1,0:T(8,128)(2,1)S(1)}, bf16[272,1280]{1,0:T(8,128)(2,1)}, u32[]{:S(2)}, u32[]{:S(2)}) collective-permute-start(bf16[272,1280]{1,0:T(8,128)(2,1)S(1)} %collective-permute-done.1.x2_ref), channel_id=1, source_target_pairs={{0,1},{1,0},{2,3},{3,2},{4,5},{5,4},{6,7},{7,6},{8,9},{9,8},{10,11... | collective-permute-start | bytes 2088968 | tf_op jit(solution)/shard_map/ppermute | solution.py:299
  39.1 8.7 %collective-permute-start.3 = (bf16[256,1280]{1,0:T(8,128)(2,1)S(1)}, bf16[256,1280]{1,0:T(8,128)(2,1)S(1)}, u32[]{:S(2)}, u32[]{:S(2)}) collective-permute-start(bf16[256,1280]{1,0:T(8,128)(2,1)S(1)} %copy-done.1), channel_id=1, source_target_pairs={{0,1},{1,0},{2,3},{3,2},{4,5},{5,4},{6,7},{7,6},{8,9},{9,8},{10,11... | collective-permute-start | bytes 1966088 | tf_op jit(solution)/shard_map/ppermute | solution.py:299
  41.1 6.7 %copy-start.6 = (bf16[256,1280]{1,0:T(8,128)(2,1)}, bf16[256,1280]{1,0:T(8,128)(2,1)S(1)}, u32[]{:S(2)}) copy-start(bf16[256,1280]{1,0:T(8,128)(2,1)S(1)} %collective-permute-done.4.c2_ref) | copy-start | bytes 1966084
  41.1 8.4 %collective-permute-start.5 = (bf16[256,1280]{1,0:T(8,128)(2,1)S(1)}, bf16[256,1280]{1,0:T(8,128)(2,1)S(1)}, u32[]{:S(2)}, u32[]{:S(2)}) collective-permute-start(bf16[256,1280]{1,0:T(8,128)(2,1)S(1)} %collective-permute-done.4.c2_ref), channel_id=1, source_target_pairs={{0,1},{1,0},{2,3},{3,2},{4,5},{5,4},{6,7},{7,6},{8,9},{9,8},{10,11... | collective-permute-start | bytes 1966088 | tf_op jit(solution)/shard_map/ppermute | solution.py:299
  47.8 2.5 %copy-start.5 = (bf16[272,1280]{1,0:T(8,128)(2,1)}, bf16[272,1280]{1,0:T(8,128)(2,1)S(1)}, u32[]{:S(2)}) copy-start(bf16[272,1280]{1,0:T(8,128)(2,1)S(1)} %collective-permute-done.x1_ref) | copy-start | bytes 2088964
  49.5 0.8 copy-start.7
  60.8 17.4 %all-to-all-start.1 = ((bf16[8,40,1280]{2,1,0:T(8,128)(2,1)}), bf16[8,40,1280]{2,1,0:T(8,128)(2,1)S(1)}, u32[]{:S(2)}, u32[]{:S(2)}) async-start(bf16[8,40,1280]{2,1,0:T(8,128)(2,1)} %bitcast.31), calls=%async_computation.1 | async-start | bytes 1638400 | tf_op jit(solution)/shard_map/all_to_all | solution.py:387
  70.3 14.9 %collective-permute-start.6 = (bf16[2,256,1280]{2,1,0:T(8,128)(2,1)}, bf16[2,256,1280]{2,1,0:T(8,128)(2,1)}, u32[]{:S(2)}, u32[]{:S(2)}) collective-permute-start(bf16[2,256,1280]{2,1,0:T(8,128)(2,1)} %get-tuple-element.22), channel_id=1, source_target_pairs={{0,1},{1,0},{2,3},{3,2},{4,5},{5,4},{6,7},{7,6},{8,9},{9,8},{10,11... | collective-permute-start | bytes 3932168 | tf_op jit(solution)/shard_map/ppermute | solution.py:299
  79.0 15.0 %all-to-all-start.2 = ((bf16[4,40,1280]{2,1,0:T(8,128)(2,1)}), bf16[4,40,1280]{2,1,0:T(8,128)(2,1)S(1)}, u32[]{:S(2)}, u32[]{:S(2)}) async-start(bf16[4,40,1280]{2,1,0:T(8,128)(2,1)} %shard_map.107), calls=%async_computation.2 | async-start | bytes 819200 | tf_op jit(solution)/shard_map/all_to_all | solution.py:392
  87.3 35.8 %copy-start.2 = (bf16[256,1280]{1,0:T(8,128)(2,1)S(1)}, bf16[256,1280]{1,0:T(8,128)(2,1)}, u32[]{:S(2)}) copy-start(bf16[256,1280]{1,0:T(8,128)(2,1)} %patches_ref.1) | copy-start | bytes 1966084
  87.3 19.2 %collective-permute-start.7 = (bf16[256,1280]{1,0:T(8,128)(2,1)}, bf16[256,1280]{1,0:T(8,128)(2,1)S(1)}, u32[]{:S(2)}, u32[]{:S(2)}) collective-permute-start(bf16[256,1280]{1,0:T(8,128)(2,1)} %fusion.3), channel_id=1, source_target_pairs={{0,2},{2,0},{1,3},{3,1},{4,6},{6,4},{5,7},{7,5},{8,10},{10,8},{9,1... | collective-permute-start | bytes 1966088 | tf_op jit(solution)/shard_map/ppermute | solution.py:302
  94.8 23.7 %all-to-all-start.3 = ((bf16[4,40,1280]{2,1,0:T(8,128)(2,1)}), bf16[4,40,1280]{2,1,0:T(8,128)(2,1)S(1)}, u32[]{:S(2)}, u32[]{:S(2)}) async-start(bf16[4,40,1280]{2,1,0:T(8,128)(2,1)} %shard_map.108), calls=%async_computation.3 | async-start | bytes 819200 | tf_op jit(solution)/shard_map/all_to_all | solution.py:396
  118.6 9.3 %collective-permute-start.9 = (bf16[40,1280]{1,0:T(8,128)(2,1)S(1)}, bf16[40,1280]{1,0:T(8,128)(2,1)S(1)}, u32[]{:S(2)}, u32[]{:S(2)}) collective-permute-start(bf16[40,1280]{1,0:T(8,128)(2,1)S(1)} %bitcast.28), channel_id=1, source_target_pairs={{0,64},{2,0},{64,66},{66,2},{128,130},{130,194},{192,128},{194,192... | collective-permute-start | bytes 307208 | tf_op jit(solution)/shard_map/ppermute | solution.py:400
  121.1 6.8 %collective-permute-start.8 = (bf16[40,1280]{1,0:T(8,128)(2,1)S(1)}, bf16[40,1280]{1,0:T(8,128)(2,1)S(1)}, u32[]{:S(2)}, u32[]{:S(2)}) collective-permute-start(bf16[40,1280]{1,0:T(8,128)(2,1)S(1)} %bitcast.29), channel_id=1, source_target_pairs={{0,66},{66,0},{130,192},{192,130},{1,67},{67,1},{131,193},{193,131... | collective-permute-start | bytes 307208 | tf_op jit(solution)/shard_map/ppermute | solution.py:401
  128.0 4.3 %collective-permute-start.10 = (bf16[80,1280]{1,0:T(8,128)(2,1)S(1)}, bf16[80,1280]{1,0:T(8,128)(2,1)S(1)}, u32[]{:S(2)}, u32[]{:S(2)}) collective-permute-start(bf16[80,1280]{1,0:T(8,128)(2,1)S(1)} %bitcast_select_fusion.1), channel_id=1, source_target_pairs={{0,1},{1,0},{2,3},{3,2},{4,5},{5,4},{6,7},{7,6},{8,9},{9,8},{10,11... | collective-permute-start | bytes 614408 | tf_op jit(solution)/shard_map/ppermute | solution.py:299

commit v7 on v6

--- a/solution.py
+++ b/solution.py
@@ -26,21 +26,23 @@
 HEAD_SETS = ((1, 2, 5, 6), (0, 3, 4, 7))
 
 
+def rank_of(shard, core):
+    return 2 * (3 - shard // 2) + shard % 2 if core else shard
+
+
 def block_tables():
     sends = np.zeros((8, 2, 2), np.int32)
-    orders = np.zeros((2, 16), np.int32)
+    orders = np.zeros((2, 2, 16), np.int32)
     for half, heads in enumerate(HEAD_SETS):
         for shard in range(8):
             picked = [k for k in range(3) if (3 * shard + k) % 8 in heads] + ([3] if shard in heads else [])
             assert len(picked) == 2
             for place, k in enumerate(picked):
                 sends[shard, half, place] = k
-                if k == 3:
-                    slot = 12 + heads.index(shard)
-                else:
-                    kind, m = divmod(3 * shard + k, 8)
-                    slot = 4 * kind + heads.index(m)
-                orders[half, slot] = 2 * shard + place
+                kind, m = (3, shard) if k == 3 else divmod(3 * shard + k, 8)
+                for core in range(2):
+                    listed = heads[::-1] if core else heads
+                    orders[half, core, 4 * kind + listed.index(m)] = 2 * rank_of(shard, core) + place
     return sends.reshape(-1), orders.reshape(-1)
 
 
@@ -59,6 +61,8 @@
 ACROSS = [(2 * x + half, 2 * (x ^ 1) + (1 - half)) for x in range(4) for half in range(2) if not owns(x, half)]
 
 
+SHARDS = ("y_lo", "x", "core")
+SHARD_GROUPS = [[rank_of(rank, core) * CORES + core for rank in range(8)] for core in range(CORES)]
 CROSS = ("y_lo", "y_hi", "z_quad", "z_pair", "core")
 
 
@@ -162,7 +166,7 @@
     hidden = -1e30 * HEAD**0.5
     copies = []
     for slot in range(12):
-        source = blocks_ref.at[order_ref[16 * half_of(place_ref) + slot]]
+        source = blocks_ref.at[order_ref[16 * (place_ref[0] % 4) + slot]]
         copies.append(pltpu.make_async_copy(source, weight_ref.at[slot * HEAD : (slot + 1) * HEAD], sems.at[slot]))
     arrivals = [
         pltpu.make_async_copy(ref, x_ref.at[part], x_sems.at[part])
@@ -224,7 +228,7 @@
     copies = [pltpu.make_async_copy(from_ref, context_ref, sem)]
     copies[0].start()
     for slot in range(4):
-        source = blocks_ref.at[order_ref[16 * half_of(place_ref) + 12 + slot]]
+        source = blocks_ref.at[order_ref[16 * (place_ref[0] % 4) + 12 + slot]]
         copies.append(pltpu.make_async_copy(source, weight_ref.at[slot * HEAD : (slot + 1) * HEAD], sems.at[slot]))
         copies[-1].start()
     for copy in copies:
@@ -325,7 +329,7 @@
         qkv_weight.T.reshape(6, HEAD, WIDTH),
         proj_weight.reshape(2, HEAD, WIDTH),
     )
-    blocks = lax.all_to_all(own, FSDP, 0, 0).reshape(16, HEAD, WIDTH)
+    blocks = lax.all_to_all(own, SHARDS, 0, 0, axis_index_groups=SHARD_GROUPS).reshape(16, HEAD, WIDTH)
 
     message_pair = to_pair(message)
     cotangent_pair = to_pair(out_cotangent)
@@ -384,7 +388,7 @@
         read=6 << 20,
     )(place, orders, context, blocks)
 
-    grad = lax.all_to_all(grad.reshape(8, 40, WIDTH), FSDP, 0, 0)
+    grad = lax.all_to_all(grad.reshape(8, 40, WIDTH), SHARDS, 0, 0, axis_index_groups=SHARD_GROUPS)
     grad, keep_late = lax.optimization_barrier((grad, keep_out))
     grad = sum_of(grad, Z_QUAD)
     from_core = to_core(send_out)

time: 134 us -> 133 us (level)
  starting transfers between devices: 74.6 us -> 63.5 us
  waiting for transfers between devices: 30.1 us -> 40.7 us
    ppermute x6, starting transfers between devices: 33.8 us -> 19.6 us  [to_core(): return lax.ppermute(value, 'core', CORE_SWAP)]
    ppermute x3, waiting for transfers between devices: 4.33 us -> 17.4 us  [to_pair(): return lax.ppermute(value, 'z_pair', PAIR_SWAP)]
    all_to_all x2, starting transfers between devices: 11.2 us -> 14.3 us  [the longest x1 9.1 us: shards(): lax.all_to_all(own, SHARDS, 0, 0, axis_index_groups=SHARD_GROUPS)]
  transfers between devices with their start and end apart: 15 -> 15, of which waited for: 8 -> 9; matrix products, arithmetic and copies ran while one was open for 4% -> 4% of each run, Pallas kernels for 5% -> 5%
where the time goes in v7:
time: 133 us
  starting transfers between devices  63.5 us (48%)
  waiting for transfers between devices  40.7 us (31%)
  Pallas kernels  20.4 us (15%)
  other arithmetic  5.37 us (4%)
  between operations  1.53 us (1%)
    ppermute x6, starting transfers between devices, to_core(): return lax.ppermute(value, 'core', CORE_SWAP)  19.6 us
    ppermute x3, waiting for transfers between devices, to_pair(): return lax.ppermute(value, 'z_pair', PAIR_SWAP)  17.4 us
    all_to_all x1, waiting for transfers between devices, shards(): grad = lax.all_to_all(grad, CROSS, 0, 0, axis_index_groups=cross_groups(1))  11.2 us
    pallas_call x1, Pallas kernels, shards(): call(attention_kernel, (array(4 * HEAD, 4 * ROWS), array(4 * HEAD, WIDTH)...  10.4 us
    all_to_all x1, starting transfers between devices, shards(): grad = lax.all_to_all(grad, CROSS, 0, 0, axis_index_groups=cross_groups(1))  10.1 us
    ppermute x3, starting transfers between devices, to_pair(): return lax.ppermute(value, 'z_pair', PAIR_SWAP)  9.77 us
    all_to_all x1, starting transfers between devices, shards(): lax.all_to_all(own, SHARDS, 0, 0, axis_index_groups=SHARD_GROUPS)  9.1 us
    all_to_all x1, starting transfers between devices, shards(): grad = lax.all_to_all(grad, CROSS, 0, 0, axis_index_groups=cross_groups(0))  5.57 us
  transfers between devices with their start and end apart: 15, of which 9 were waited for; matrix products, arithmetic and copies ran while one was open for 4% of the time, Pallas kernels for 5%

profile of v7, /device:TPU:1, one launch (start us, length us, event | category | flops | bytes accessed | tf_op | source)
XLA Modules:
  0.0 132.6 jit_solution(5305023654406437586)
XLA Ops:
  1.3 3.9 %shard_map.104 = (bf16[272,1280]{1,0:T(8,128)(2,1)}, bf16[8,2,80,1280]{3,2,1,0:T(8,128)(2,1)}) custom-call(s32[1]{0:T(128)} %bitcast.place_ref, s32[32]{0:T(128)} %constant.57.clone.sends_ref, s32[1]{0:T(128)S(6)} %copy.11.count_ref, bf16[256,1280]{1,0:T(8,128)(2,1)} %patches_ref.1, f32[1280]{0:T(1024)} %gain_ref.1, s32[256]{0:T(256)} %images_ref.1, ...), custom_call_target="tpu_custom_call" | custom-call | bytes 6291456 | tf_op jit(solution)/shard_map/pallas_call | solution.py:308
  5.2 0.0 copy-start.3
  5.3 0.0 copy-start.1
  5.3 0.0 copy-start
  5.3 9.1 %all-to-all-start = ((bf16[8,2,80,1280]{3,2,1,0:T(8,128)(2,1)}), bf16[8,2,80,1280]{3,2,1,0:T(8,128)(2,1)}, u32[]{:S(2)}, u32[]{:S(2)}) async-start(bf16[8,2,80,1280]{3,2,1,0:T(8,128)(2,1)} %get-tuple-element.17), calls=%async_computation | async-start | bytes 6553600 | tf_op jit(solution)/shard_map/all_to_all | solution.py:332
  14.4 0.0 copy-done.3
  14.4 4.0 %collective-permute-start.1 = (bf16[272,1280]{1,0:T(8,128)(2,1)S(1)}, bf16[272,1280]{1,0:T(8,128)(2,1)S(1)}, u32[]{:S(2)}, u32[]{:S(2)}) collective-permute-start(bf16[272,1280]{1,0:T(8,128)(2,1)S(1)} %copy-done.3), channel_id=1, source_target_pairs={{0,2},{2,0},{1,3},{3,1},{4,6},{6,4},{5,7},{7,5},{8,10},{10,8},{9,1... | collective-permute-start | bytes 2088968 | tf_op jit(solution)/shard_map/ppermute | solution.py:306
  18.4 0.0 copy-done.1
  18.4 1.9 %collective-permute-start.4 = (bf16[256,1280]{1,0:T(8,128)(2,1)S(1)}, bf16[256,1280]{1,0:T(8,128)(2,1)S(1)}, u32[]{:S(2)}, u32[]{:S(2)}) collective-permute-start(bf16[256,1280]{1,0:T(8,128)(2,1)S(1)} %copy-done.1), channel_id=1, source_target_pairs={{0,2},{2,0},{1,3},{3,1},{4,6},{6,4},{5,7},{7,5},{8,10},{10,8},{9,1... | collective-permute-start | bytes 1966088 | tf_op jit(solution)/shard_map/ppermute | solution.py:306
  20.3 4.2 %collective-permute-start = (bf16[272,1280]{1,0:T(8,128)(2,1)S(1)}, bf16[272,1280]{1,0:T(8,128)(2,1)S(1)}, u32[]{:S(2)}, u32[]{:S(2)}) collective-permute-start(bf16[272,1280]{1,0:T(8,128)(2,1)S(1)} %copy-done.3), channel_id=1, source_target_pairs={{0,1},{1,0},{2,3},{3,2},{4,5},{5,4},{6,7},{7,6},{8,9},{9,8},{10,11... | collective-permute-start | bytes 2088968 | tf_op jit(solution)/shard_map/ppermute | solution.py:303
  24.6 8.8 %collective-permute-done.1.x2_ref = bf16[272,1280]{1,0:T(8,128)(2,1)S(1)} collective-permute-done((bf16[272,1280]{1,0:T(8,128)(2,1)S(1)}, bf16[272,1280]{1,0:T(8,128)(2,1)S(1)}, u32[]{:S(2)}, u32[]{:S(2)}) %collective-permute-start.1) | collective-permute-done | bytes 696352 | tf_op jit(solution)/shard_map/ppermute | solution.py:306
  33.4 0.0 copy-start.4
  33.4 5.8 %collective-permute-start.2 = (bf16[272,1280]{1,0:T(8,128)(2,1)S(1)}, bf16[272,1280]{1,0:T(8,128)(2,1)}, u32[]{:S(2)}, u32[]{:S(2)}) collective-permute-start(bf16[272,1280]{1,0:T(8,128)(2,1)S(1)} %collective-permute-done.1.x2_ref), channel_id=1, source_target_pairs={{0,1},{1,0},{2,3},{3,2},{4,5},{5,4},{6,7},{7,6},{8,9},{9,8},{10,11... | collective-permute-start | bytes 2088968 | tf_op jit(solution)/shard_map/ppermute | solution.py:303
  39.1 1.9 %collective-permute-start.3 = (bf16[256,1280]{1,0:T(8,128)(2,1)S(1)}, bf16[256,1280]{1,0:T(8,128)(2,1)S(1)}, u32[]{:S(2)}, u32[]{:S(2)}) collective-permute-start(bf16[256,1280]{1,0:T(8,128)(2,1)S(1)} %copy-done.1), channel_id=1, source_target_pairs={{0,1},{1,0},{2,3},{3,2},{4,5},{5,4},{6,7},{7,6},{8,9},{9,8},{10,11... | collective-permute-start | bytes 1966088 | tf_op jit(solution)/shard_map/ppermute | solution.py:303
  41.1 6.3 %collective-permute-done.4.c2_ref = bf16[256,1280]{1,0:T(8,128)(2,1)S(1)} collective-permute-done((bf16[256,1280]{1,0:T(8,128)(2,1)S(1)}, bf16[256,1280]{1,0:T(8,128)(2,1)S(1)}, u32[]{:S(2)}, u32[]{:S(2)}) %collective-permute-start.4) | collective-permute-done | bytes 655392 | tf_op jit(solution)/shard_map/ppermute | solution.py:306
  47.4 0.0 copy-start.6
  47.4 3.5 %collective-permute-start.5 = (bf16[256,1280]{1,0:T(8,128)(2,1)S(1)}, bf16[256,1280]{1,0:T(8,128)(2,1)S(1)}, u32[]{:S(2)}, u32[]{:S(2)}) collective-permute-start(bf16[256,1280]{1,0:T(8,128)(2,1)S(1)} %collective-permute-done.4.c2_ref), channel_id=1, source_target_pairs={{0,1},{1,0},{2,3},{3,2},{4,5},{5,4},{6,7},{7,6},{8,9},{9,8},{10,11... | collective-permute-start | bytes 1966088 | tf_op jit(solution)/shard_map/ppermute | solution.py:303
  50.9 0.0 collective-permute-done.3.c1_ref
  50.9 0.0 collective-permute-done.x1_ref
  50.9 0.0 copy-done.6
  50.9 0.0 copy-start.5
  50.9 1.7 %collective-permute-done.5.c3_ref = bf16[256,1280]{1,0:T(8,128)(2,1)S(1)} collective-permute-done((bf16[256,1280]{1,0:T(8,128)(2,1)S(1)}, bf16[256,1280]{1,0:T(8,128)(2,1)S(1)}, u32[]{:S(2)}, u32[]{:S(2)}) %collective-permute-start.5) | collective-permute-done | bytes 655392 | tf_op jit(solution)/shard_map/ppermute | solution.py:303
  52.6 0.0 copy-start.7
  52.6 0.8 copy-done.7
  53.4 0.0 collective-permute-done.2.x3_ref
  53.4 0.0 all-to-all-done
  53.4 0.0 copy-done.5
  53.4 0.0 copy-done.4
  53.4 0.0 copy-done
  53.4 10.4 %shard_map.105 = (bf16[320,1024]{1,0:T(8,128)(2,1)S(1)}, bf16[320,1280]{1,0:T(8,128)(2,1)}) custom-call(s32[1]{0:T(128)} %bitcast.place_ref, s32[64]{0:T(128)S(1)} %copy-done, bf16[272,1280]{1,0:T(8,128)(2,1)} %get-tuple-element.16.x0_ref, bf16[272,1280]{1,0:T(8,128)(2,1)} %copy-done.5, bf16[272,1280]{1,0:T(8,128)(2,1)} %copy-done.4, ...), custom_call_target="tpu_custom_call" | custom-call | flops 3892314112 | bytes 12582912 | tf_op jit(solution)/shard_map/pallas_call | solution.py:341
  63.8 5.2 %all-to-all-start.1 = ((bf16[8,40,1280]{2,1,0:T(8,128)(2,1)}), bf16[8,40,1280]{2,1,0:T(8,128)(2,1)S(1)}, u32[]{:S(2)}, u32[]{:S(2)}) async-start(bf16[8,40,1280]{2,1,0:T(8,128)(2,1)} %bitcast.31), calls=%async_computation.1 | async-start | bytes 1638400 | tf_op jit(solution)/shard_map/all_to_all | solution.py:391
  69.0 4.4 %shard_map.106 = (bf16[2,256,1280]{2,1,0:T(8,128)(2,1)S(1)}, bf16[2,256,1280]{2,1,0:T(8,128)(2,1)}) custom-call(s32[1]{0:T(128)} %bitcast.place_ref, s32[64]{0:T(128)S(1)} %copy-done, bf16[320,1024]{1,0:T(8,128)(2,1)S(1)} %get-tuple-element.19.from_ref, bf16[16,80,1280]{2,1,0:T(8,128)(2,1)} %bitcast.4.blocks_ref), custom_call_target="tpu_custom_call" | custom-call | flops 838860800 | bytes 6291456 | tf_op jit(solution)/shard_map/pallas_call | solution.py:373
  73.3 1.9 %collective-permute-start.6 = (bf16[2,256,1280]{2,1,0:T(8,128)(2,1)}, bf16[2,256,1280]{2,1,0:T(8,128)(2,1)}, u32[]{:S(2)}, u32[]{:S(2)}) collective-permute-start(bf16[2,256,1280]{2,1,0:T(8,128)(2,1)} %get-tuple-element.22), channel_id=1, source_target_pairs={{0,1},{1,0},{2,3},{3,2},{4,5},{5,4},{6,7},{7,6},{8,9},{9,8},{10,11... | collective-permute-start | bytes 3932168 | tf_op jit(solution)/shard_map/ppermute | solution.py:303
  75.3 4.1 %all-to-all-done.1.terms_ref = bf16[8,40,1280]{2,1,0:T(8,128)(2,1)S(1)} async-done(((bf16[8,40,1280]{2,1,0:T(8,128)(2,1)}), bf16[8,40,1280]{2,1,0:T(8,128)(2,1)S(1)}, u32[]{:S(2)}, u32[]{:S(2)}) %all-to-all-start.1) | async-done | bytes 819232 | tf_op jit(solution)/shard_map/all_to_all | solution.py:391
  79.4 0.9 shard_map.107
  80.3 5.6 %all-to-all-start.2 = ((bf16[4,40,1280]{2,1,0:T(8,128)(2,1)}), bf16[4,40,1280]{2,1,0:T(8,128)(2,1)S(1)}, u32[]{:S(2)}, u32[]{:S(2)}) async-start(bf16[4,40,1280]{2,1,0:T(8,128)(2,1)} %shard_map.107), calls=%async_computation.2 | async-start | bytes 819200 | tf_op jit(solution)/shard_map/all_to_all | solution.py:396
  85.8 0.0 collective-permute-done.6
  85.8 2.1 %fusion.3 = bf16[256,1280]{1,0:T(8,128)(2,1)} fusion(bf16[2,256,1280]{2,1,0:T(8,128)(2,1)} %collective-permute-done.6, bf16[2,256,1280]{2,1,0:T(8,128)(2,1)S(1)} %get-tuple-element.25), kind=kLoop, calls=%fused_computation.5 | loop fusion | flops 1310720 | bytes 1966080 | tf_op jit(solution)/shard_map/convert_element_type | solution.py:395
  87.9 0.0 copy-start.2
  87.9 3.9 %collective-permute-start.7 = (bf16[256,1280]{1,0:T(8,128)(2,1)}, bf16[256,1280]{1,0:T(8,128)(2,1)S(1)}, u32[]{:S(2)}, u32[]{:S(2)}) collective-permute-start(bf16[256,1280]{1,0:T(8,128)(2,1)} %fusion.3), channel_id=1, source_target_pairs={{0,2},{2,0},{1,3},{3,1},{4,6},{6,4},{5,7},{7,5},{8,10},{10,8},{9,1... | collective-permute-start | bytes 1966088 | tf_op jit(solution)/shard_map/ppermute | solution.py:306
  91.8 2.8 %all-to-all-done.2.terms_ref = bf16[4,40,1280]{2,1,0:T(8,128)(2,1)S(1)} async-done(((bf16[4,40,1280]{2,1,0:T(8,128)(2,1)}), bf16[4,40,1280]{2,1,0:T(8,128)(2,1)S(1)}, u32[]{:S(2)}, u32[]{:S(2)}) %all-to-all-start.2) | async-done | bytes 409632 | tf_op jit(solution)/shard_map/all_to_all | solution.py:396
  94.5 0.8 shard_map.108
  95.3 10.1 %all-to-all-start.3 = ((bf16[4,40,1280]{2,1,0:T(8,128)(2,1)}), bf16[4,40,1280]{2,1,0:T(8,128)(2,1)S(1)}, u32[]{:S(2)}, u32[]{:S(2)}) async-start(bf16[4,40,1280]{2,1,0:T(8,128)(2,1)} %shard_map.108), calls=%async_computation.3 | async-start | bytes 819200 | tf_op jit(solution)/shard_map/all_to_all | solution.py:400
  105.4 0.1 broadcast_in_dim.66
  105.5 0.1 broadcast_in_dim.67
  105.6 2.3 %collective-permute-done.7 = bf16[256,1280]{1,0:T(8,128)(2,1)S(1)} collective-permute-done((bf16[256,1280]{1,0:T(8,128)(2,1)}, bf16[256,1280]{1,0:T(8,128)(2,1)S(1)}, u32[]{:S(2)}, u32[]{:S(2)}) %collective-permute-start.7) | collective-permute-done | bytes 655392 | tf_op jit(solution)/shard_map/ppermute | solution.py:306
  107.9 11.2 %all-to-all-done.3.terms_ref = bf16[4,40,1280]{2,1,0:T(8,128)(2,1)S(1)} async-done(((bf16[4,40,1280]{2,1,0:T(8,128)(2,1)}), bf16[4,40,1280]{2,1,0:T(8,128)(2,1)S(1)}, u32[]{:S(2)}, u32[]{:S(2)}) %all-to-all-start.3) | async-done | bytes 409632 | tf_op jit(solution)/shard_map/all_to_all | solution.py:400
  119.1 0.1 shard_map.109
  119.2 1.9 %collective-permute-start.9 = (bf16[40,1280]{1,0:T(8,128)(2,1)S(1)}, bf16[40,1280]{1,0:T(8,128)(2,1)S(1)}, u32[]{:S(2)}, u32[]{:S(2)}) collective-permute-start(bf16[40,1280]{1,0:T(8,128)(2,1)S(1)} %bitcast.28), channel_id=1, source_target_pairs={{0,64},{2,0},{64,66},{66,2},{128,130},{130,194},{192,128},{194,192... | collective-permute-start | bytes 307208 | tf_op jit(solution)/shard_map/ppermute | solution.py:404
  121.1 2.3 %collective-permute-start.8 = (bf16[40,1280]{1,0:T(8,128)(2,1)S(1)}, bf16[40,1280]{1,0:T(8,128)(2,1)S(1)}, u32[]{:S(2)}, u32[]{:S(2)}) collective-permute-start(bf16[40,1280]{1,0:T(8,128)(2,1)S(1)} %bitcast.29), channel_id=1, source_target_pairs={{0,66},{66,0},{130,192},{192,130},{1,67},{67,1},{131,193},{193,131... | collective-permute-start | bytes 307208 | tf_op jit(solution)/shard_map/ppermute | solution.py:405
  123.4 0.0 copy-done.2
  123.4 2.3 %fusion.2 = bf16[256,1280]{1,0:T(8,128)(2,1)} fusion(bf16[256,1280]{1,0:T(8,128)(2,1)S(1)} %collective-permute-done.7, bf16[256,1280]{1,0:T(8,128)(2,1)S(1)} %copy-done.2, bf16[2,256,1280]{2,1,0:T(8,128)(2,1)} %collective-permute-done.6, bf16[2,256,1280]{2,1,0:T(8,128)(2,1)S(1)} %get-tuple-element.25, pred[256]{0:T(512)(128)(4,1)S(1)} %iota_compare_fusion), kind=kLoop, calls=%fused_computation.3 | loop fusion | flops 2949120 | bytes 3277056 | tf_op jit(solution)/shard_map/convert_element_type | solution.py:408
  125.7 2.5 %collective-permute-done.8 = bf16[40,1280]{1,0:T(8,128)(2,1)S(1)} collective-permute-done((bf16[40,1280]{1,0:T(8,128)(2,1)S(1)}, bf16[40,1280]{1,0:T(8,128)(2,1)S(1)}, u32[]{:S(2)}, u32[]{:S(2)}) %collective-permute-start.8) | collective-permute-done | bytes 102432 | tf_op jit(solution)/shard_map/ppermute | solution.py:405
  128.3 0.0 collective-permute-done.9
  128.3 0.1 bitcast_select_fusion.1
  128.4 2.3 %collective-permute-start.10 = (bf16[80,1280]{1,0:T(8,128)(2,1)S(1)}, bf16[80,1280]{1,0:T(8,128)(2,1)S(1)}, u32[]{:S(2)}, u32[]{:S(2)}) collective-permute-start(bf16[80,1280]{1,0:T(8,128)(2,1)S(1)} %bitcast_select_fusion.1), channel_id=1, source_target_pairs={{0,1},{1,0},{2,3},{3,2},{4,5},{5,4},{6,7},{7,6},{8,9},{9,8},{10,11... | collective-permute-start | bytes 614408 | tf_op jit(solution)/shard_map/ppermute | solution.py:303
  130.7 0.1 broadcast_in_dim.63
  130.8 0.1 broadcast_in_dim.64
  130.9 0.9 collective-permute-done.10
  131.7 0.9 bitcast_select_fusion
  (4 shorter events, 0.0 us)
Async XLA Ops:
  5.2 9.1 %copy-start.3 = (bf16[272,1280]{1,0:T(8,128)(2,1)S(1)}, bf16[272,1280]{1,0:T(8,128)(2,1)}, u32[]{:S(2)}) copy-start(bf16[272,1280]{1,0:T(8,128)(2,1)} %get-tuple-element.16.x0_ref) | copy-start | bytes 2088964
  5.3 13.1 %copy-start.1 = (bf16[256,1280]{1,0:T(8,128)(2,1)S(1)}, bf16[256,1280]{1,0:T(8,128)(2,1)}, u32[]{:S(2)}) copy-start(bf16[256,1280]{1,0:T(8,128)(2,1)} %c0_ref.1) | copy-start | bytes 1966084
  5.3 48.2 %copy-start = (s32[64]{0:T(128)S(1)}, s32[64]{0:T(128)}, u32[]{:S(2)}) copy-start(s32[64]{0:T(128)} %constant.58.clone.order_ref) | copy-start | bytes 772
  5.3 48.1 %all-to-all-start = ((bf16[8,2,80,1280]{3,2,1,0:T(8,128)(2,1)}), bf16[8,2,80,1280]{3,2,1,0:T(8,128)(2,1)}, u32[]{:S(2)}, u32[]{:S(2)}) async-start(bf16[8,2,80,1280]{3,2,1,0:T(8,128)(2,1)} %get-tuple-element.17), calls=%async_computation | async-start | bytes 6553600 | tf_op jit(solution)/shard_map/all_to_all | solution.py:332
  14.4 19.0 %collective-permute-start.1 = (bf16[272,1280]{1,0:T(8,128)(2,1)S(1)}, bf16[272,1280]{1,0:T(8,128)(2,1)S(1)}, u32[]{:S(2)}, u32[]{:S(2)}) collective-permute-start(bf16[272,1280]{1,0:T(8,128)(2,1)S(1)} %copy-done.3), channel_id=1, source_target_pairs={{0,2},{2,0},{1,3},{3,1},{4,6},{6,4},{5,7},{7,5},{8,10},{10,8},{9,1... | collective-permute-start | bytes 2088968 | tf_op jit(solution)/shard_map/ppermute | solution.py:306
  18.4 29.0 %collective-permute-start.4 = (bf16[256,1280]{1,0:T(8,128)(2,1)S(1)}, bf16[256,1280]{1,0:T(8,128)(2,1)S(1)}, u32[]{:S(2)}, u32[]{:S(2)}) collective-permute-start(bf16[256,1280]{1,0:T(8,128)(2,1)S(1)} %copy-done.1), channel_id=1, source_target_pairs={{0,2},{2,0},{1,3},{3,1},{4,6},{6,4},{5,7},{7,5},{8,10},{10,8},{9,1... | collective-permute-start | bytes 1966088 | tf_op jit(solution)/shard_map/ppermute | solution.py:306
  20.3 30.6 %collective-permute-start = (bf16[272,1280]{1,0:T(8,128)(2,1)S(1)}, bf16[272,1280]{1,0:T(8,128)(2,1)S(1)}, u32[]{:S(2)}, u32[]{:S(2)}) collective-permute-start(bf16[272,1280]{1,0:T(8,128)(2,1)S(1)} %copy-done.3), channel_id=1, source_target_pairs={{0,1},{1,0},{2,3},{3,2},{4,5},{5,4},{6,7},{7,6},{8,9},{9,8},{10,11... | collective-permute-start | bytes 2088968 | tf_op jit(solution)/shard_map/ppermute | solution.py:303
  33.4 20.1 %copy-start.4 = (bf16[272,1280]{1,0:T(8,128)(2,1)}, bf16[272,1280]{1,0:T(8,128)(2,1)S(1)}, u32[]{:S(2)}) copy-start(bf16[272,1280]{1,0:T(8,128)(2,1)S(1)} %collective-permute-done.1.x2_ref) | copy-start | bytes 2088964
  33.4 20.1 %collective-permute-start.2 = (bf16[272,1280]{1,0:T(8,128)(2,1)S(1)}, bf16[272,1280]{1,0:T(8,128)(2,1)}, u32[]{:S(2)}, u32[]{:S(2)}) collective-permute-start(bf16[272,1280]{1,0:T(8,128)(2,1)S(1)} %collective-permute-done.1.x2_ref), channel_id=1, source_target_pairs={{0,1},{1,0},{2,3},{3,2},{4,5},{5,4},{6,7},{7,6},{8,9},{9,8},{10,11... | collective-permute-start | bytes 2088968 | tf_op jit(solution)/shard_map/ppermute | solution.py:303
  39.1 11.8 %collective-permute-start.3 = (bf16[256,1280]{1,0:T(8,128)(2,1)S(1)}, bf16[256,1280]{1,0:T(8,128)(2,1)S(1)}, u32[]{:S(2)}, u32[]{:S(2)}) collective-permute-start(bf16[256,1280]{1,0:T(8,128)(2,1)S(1)} %copy-done.1), channel_id=1, source_target_pairs={{0,1},{1,0},{2,3},{3,2},{4,5},{5,4},{6,7},{7,6},{8,9},{9,8},{10,11... | collective-permute-start | bytes 1966088 | tf_op jit(solution)/shard_map/ppermute | solution.py:303
  47.4 3.5 %copy-start.6 = (bf16[256,1280]{1,0:T(8,128)(2,1)}, bf16[256,1280]{1,0:T(8,128)(2,1)S(1)}, u32[]{:S(2)}) copy-start(bf16[256,1280]{1,0:T(8,128)(2,1)S(1)} %collective-permute-done.4.c2_ref) | copy-start | bytes 1966084
  47.4 5.2 %collective-permute-start.5 = (bf16[256,1280]{1,0:T(8,128)(2,1)S(1)}, bf16[256,1280]{1,0:T(8,128)(2,1)S(1)}, u32[]{:S(2)}, u32[]{:S(2)}) collective-permute-start(bf16[256,1280]{1,0:T(8,128)(2,1)S(1)} %collective-permute-done.4.c2_ref), channel_id=1, source_target_pairs={{0,1},{1,0},{2,3},{3,2},{4,5},{5,4},{6,7},{7,6},{8,9},{9,8},{10,11... | collective-permute-start | bytes 1966088 | tf_op jit(solution)/shard_map/ppermute | solution.py:303
  50.9 2.5 %copy-start.5 = (bf16[272,1280]{1,0:T(8,128)(2,1)}, bf16[272,1280]{1,0:T(8,128)(2,1)S(1)}, u32[]{:S(2)}) copy-start(bf16[272,1280]{1,0:T(8,128)(2,1)S(1)} %collective-permute-done.x1_ref) | copy-start | bytes 2088964
  52.6 0.8 copy-start.7
  63.8 15.6 %all-to-all-start.1 = ((bf16[8,40,1280]{2,1,0:T(8,128)(2,1)}), bf16[8,40,1280]{2,1,0:T(8,128)(2,1)S(1)}, u32[]{:S(2)}, u32[]{:S(2)}) async-start(bf16[8,40,1280]{2,1,0:T(8,128)(2,1)} %bitcast.31), calls=%async_computation.1 | async-start | bytes 1638400 | tf_op jit(solution)/shard_map/all_to_all | solution.py:391
  73.3 12.5 %collective-permute-start.6 = (bf16[2,256,1280]{2,1,0:T(8,128)(2,1)}, bf16[2,256,1280]{2,1,0:T(8,128)(2,1)}, u32[]{:S(2)}, u32[]{:S(2)}) collective-permute-start(bf16[2,256,1280]{2,1,0:T(8,128)(2,1)} %get-tuple-element.22), channel_id=1, source_target_pairs={{0,1},{1,0},{2,3},{3,2},{4,5},{5,4},{6,7},{7,6},{8,9},{9,8},{10,11... | collective-permute-start | bytes 3932168 | tf_op jit(solution)/shard_map/ppermute | solution.py:303
  80.3 14.3 %all-to-all-start.2 = ((bf16[4,40,1280]{2,1,0:T(8,128)(2,1)}), bf16[4,40,1280]{2,1,0:T(8,128)(2,1)S(1)}, u32[]{:S(2)}, u32[]{:S(2)}) async-start(bf16[4,40,1280]{2,1,0:T(8,128)(2,1)} %shard_map.107), calls=%async_computation.2 | async-start | bytes 819200 | tf_op jit(solution)/shard_map/all_to_all | solution.py:396
  87.9 35.5 %copy-start.2 = (bf16[256,1280]{1,0:T(8,128)(2,1)S(1)}, bf16[256,1280]{1,0:T(8,128)(2,1)}, u32[]{:S(2)}) copy-start(bf16[256,1280]{1,0:T(8,128)(2,1)} %patches_ref.1) | copy-start | bytes 1966084
  87.9 20.0 %collective-permute-start.7 = (bf16[256,1280]{1,0:T(8,128)(2,1)}, bf16[256,1280]{1,0:T(8,128)(2,1)S(1)}, u32[]{:S(2)}, u32[]{:S(2)}) collective-permute-start(bf16[256,1280]{1,0:T(8,128)(2,1)} %fusion.3), channel_id=1, source_target_pairs={{0,2},{2,0},{1,3},{3,1},{4,6},{6,4},{5,7},{7,5},{8,10},{10,8},{9,1... | collective-permute-start | bytes 1966088 | tf_op jit(solution)/shard_map/ppermute | solution.py:306
  95.3 23.8 %all-to-all-start.3 = ((bf16[4,40,1280]{2,1,0:T(8,128)(2,1)}), bf16[4,40,1280]{2,1,0:T(8,128)(2,1)S(1)}, u32[]{:S(2)}, u32[]{:S(2)}) async-start(bf16[4,40,1280]{2,1,0:T(8,128)(2,1)} %shard_map.108), calls=%async_computation.3 | async-start | bytes 819200 | tf_op jit(solution)/shard_map/all_to_all | solution.py:400
  119.2 9.1 %collective-permute-start.9 = (bf16[40,1280]{1,0:T(8,128)(2,1)S(1)}, bf16[40,1280]{1,0:T(8,128)(2,1)S(1)}, u32[]{:S(2)}, u32[]{:S(2)}) collective-permute-start(bf16[40,1280]{1,0:T(8,128)(2,1)S(1)} %bitcast.28), channel_id=1, source_target_pairs={{0,64},{2,0},{64,66},{66,2},{128,130},{130,194},{192,128},{194,192... | collective-permute-start | bytes 307208 | tf_op jit(solution)/shard_map/ppermute | solution.py:404
  121.1 7.1 %collective-permute-start.8 = (bf16[40,1280]{1,0:T(8,128)(2,1)S(1)}, bf16[40,1280]{1,0:T(8,128)(2,1)S(1)}, u32[]{:S(2)}, u32[]{:S(2)}) collective-permute-start(bf16[40,1280]{1,0:T(8,128)(2,1)S(1)} %bitcast.29), channel_id=1, source_target_pairs={{0,66},{66,0},{130,192},{192,130},{1,67},{67,1},{131,193},{193,131... | collective-permute-start | bytes 307208 | tf_op jit(solution)/shard_map/ppermute | solution.py:405
  128.4 3.4 %collective-permute-start.10 = (bf16[80,1280]{1,0:T(8,128)(2,1)S(1)}, bf16[80,1280]{1,0:T(8,128)(2,1)S(1)}, u32[]{:S(2)}, u32[]{:S(2)}) collective-permute-start(bf16[80,1280]{1,0:T(8,128)(2,1)S(1)} %bitcast_select_fusion.1), channel_id=1, source_target_pairs={{0,1},{1,0},{2,3},{3,2},{4,5},{5,4},{6,7},{7,6},{8,9},{9,8},{10,11... | collective-permute-start | bytes 614408 | tf_op jit(solution)/shard_map/ppermute | solution.py:303

commit v8 on v7

--- a/solution.py
+++ b/solution.py
@@ -186,19 +186,24 @@
         ).astype(BF16)
         for part in range(4)
     ]
+    def piece(part, kind, head):
+        return everything[part][(4 * kind + head) * HEAD : (4 * kind + head + 1) * HEAD, :]
+
+    def products(part):
+        return [
+            lax.dot_general(
+                piece(part, 1, head), piece(part, 0, head), (((0,), (0,)), ((), ())), preferred_element_type=F32
+            )
+            for head in range(4)
+        ]
+
+    scores = products(0)
     for part in range(4):
-        mixed = everything[part]
+        following = products(part + 1) if part < 3 else None
         code = x_ref[part, ROWS:, :ROWS].astype(F32)[0:1, :]
         square = jnp.broadcast_to(code, (ROWS, ROWS))
         allowed = square == square.T
         alive = code < 64.0
-        def piece(kind, head):
-            return mixed[(4 * kind + head) * HEAD : (4 * kind + head + 1) * HEAD, :]
-
-        scores = [
-            lax.dot_general(piece(1, head), piece(0, head), (((0,), (0,)), ((), ())), preferred_element_type=F32)
-            for head in range(4)
-        ]
         weights, totals = [], []
         for head in range(4):
             masked = jnp.where(allowed, scores[head], hidden)
@@ -207,9 +212,10 @@
             totals.append(jnp.sum(weight, axis=0, keepdims=True))
             weights.append(weight.astype(BF16))
         for head in range(4):
-            context = jnp.dot(piece(2, head), weights[head], preferred_element_type=F32)
+            context = jnp.dot(piece(part, 2, head), weights[head], preferred_element_type=F32)
             context = jnp.where(alive, context / totals[head], 0.0)
             context_ref[head * HEAD : (head + 1) * HEAD, part * ROWS : (part + 1) * ROWS] = context.astype(BF16)
+        scores = following
     store = pltpu.make_async_copy(context_ref, out_ref, out_sem)
     store.start()
     for copy in cotangents:

time: 133 us -> 133 us (level)
  no operation moved by 1% of the time
where the time goes in v8:
time: 133 us; the launch traced here: 132 us
  starting transfers between devices  63.5 us (48%)
  waiting for transfers between devices  40.7 us (31%)
  Pallas kernels  19.9 us (15%)
  other arithmetic  5.37 us (4%)
  between operations  1.53 us (1%)
    ppermute x6, starting transfers between devices, to_core(): return lax.ppermute(value, 'core', CORE_SWAP)  19.6 us
    ppermute x3, waiting for transfers between devices, to_pair(): return lax.ppermute(value, 'z_pair', PAIR_SWAP)  17.4 us
    all_to_all x1, waiting for transfers between devices, shards(): grad = lax.all_to_all(grad, CROSS, 0, 0, axis_index_groups=cross_groups(1))  11.2 us
    all_to_all x1, starting transfers between devices, shards(): grad = lax.all_to_all(grad, CROSS, 0, 0, axis_index_groups=cross_groups(1))  10 us
    pallas_call x1, Pallas kernels, shards(): call(attention_kernel, (array(4 * HEAD, 4 * ROWS), array(4 * HEAD, WIDTH)...  9.91 us
    ppermute x3, starting transfers between devices, to_pair(): return lax.ppermute(value, 'z_pair', PAIR_SWAP)  9.76 us
    all_to_all x1, starting transfers between devices, shards(): lax.all_to_all(own, SHARDS, 0, 0, axis_index_groups=SHARD_GROUPS)  9.1 us
    all_to_all x1, starting transfers between devices, shards(): grad = lax.all_to_all(grad, CROSS, 0, 0, axis_index_groups=cross_groups(0))  5.58 us
  transfers between devices with their start and end apart: 15, of which 9 were waited for; matrix products, arithmetic and copies ran while one was open for 4% of the time, Pallas kernels for 5%

profile of v8, /device:TPU:1, one launch (start us, length us, event | category | flops | bytes accessed | tf_op | source)
XLA Modules:
  0.0 132.2 jit_solution(4251409250794430846)
XLA Ops:
  1.3 3.9 %shard_map.104 = (bf16[272,1280]{1,0:T(8,128)(2,1)}, bf16[8,2,80,1280]{3,2,1,0:T(8,128)(2,1)}) custom-call(s32[1]{0:T(128)} %bitcast.place_ref, s32[32]{0:T(128)} %constant.57.clone.sends_ref, s32[1]{0:T(128)S(6)} %copy.11.count_ref, bf16[256,1280]{1,0:T(8,128)(2,1)} %patches_ref.1, f32[1280]{0:T(1024)} %gain_ref.1, s32[256]{0:T(256)} %images_ref.1, ...), custom_call_target="tpu_custom_call" | custom-call | bytes 6291456 | tf_op jit(solution)/shard_map/pallas_call | solution.py:314
  5.2 0.0 copy-start.3
  5.3 0.0 copy-start.1
  5.3 0.0 copy-start
  5.3 9.1 %all-to-all-start = ((bf16[8,2,80,1280]{3,2,1,0:T(8,128)(2,1)}), bf16[8,2,80,1280]{3,2,1,0:T(8,128)(2,1)}, u32[]{:S(2)}, u32[]{:S(2)}) async-start(bf16[8,2,80,1280]{3,2,1,0:T(8,128)(2,1)} %get-tuple-element.17), calls=%async_computation | async-start | bytes 6553600 | tf_op jit(solution)/shard_map/all_to_all | solution.py:338
  14.4 0.0 copy-done.3
  14.4 4.0 %collective-permute-start.1 = (bf16[272,1280]{1,0:T(8,128)(2,1)S(1)}, bf16[272,1280]{1,0:T(8,128)(2,1)S(1)}, u32[]{:S(2)}, u32[]{:S(2)}) collective-permute-start(bf16[272,1280]{1,0:T(8,128)(2,1)S(1)} %copy-done.3), channel_id=1, source_target_pairs={{0,2},{2,0},{1,3},{3,1},{4,6},{6,4},{5,7},{7,5},{8,10},{10,8},{9,1... | collective-permute-start | bytes 2088968 | tf_op jit(solution)/shard_map/ppermute | solution.py:312
  18.4 0.0 copy-done.1
  18.4 1.9 %collective-permute-start.4 = (bf16[256,1280]{1,0:T(8,128)(2,1)S(1)}, bf16[256,1280]{1,0:T(8,128)(2,1)S(1)}, u32[]{:S(2)}, u32[]{:S(2)}) collective-permute-start(bf16[256,1280]{1,0:T(8,128)(2,1)S(1)} %copy-done.1), channel_id=1, source_target_pairs={{0,2},{2,0},{1,3},{3,1},{4,6},{6,4},{5,7},{7,5},{8,10},{10,8},{9,1... | collective-permute-start | bytes 1966088 | tf_op jit(solution)/shard_map/ppermute | solution.py:312
  20.3 4.2 %collective-permute-start = (bf16[272,1280]{1,0:T(8,128)(2,1)S(1)}, bf16[272,1280]{1,0:T(8,128)(2,1)S(1)}, u32[]{:S(2)}, u32[]{:S(2)}) collective-permute-start(bf16[272,1280]{1,0:T(8,128)(2,1)S(1)} %copy-done.3), channel_id=1, source_target_pairs={{0,1},{1,0},{2,3},{3,2},{4,5},{5,4},{6,7},{7,6},{8,9},{9,8},{10,11... | collective-permute-start | bytes 2088968 | tf_op jit(solution)/shard_map/ppermute | solution.py:309
  24.6 8.8 %collective-permute-done.1.x2_ref = bf16[272,1280]{1,0:T(8,128)(2,1)S(1)} collective-permute-done((bf16[272,1280]{1,0:T(8,128)(2,1)S(1)}, bf16[272,1280]{1,0:T(8,128)(2,1)S(1)}, u32[]{:S(2)}, u32[]{:S(2)}) %collective-permute-start.1) | collective-permute-done | bytes 696352 | tf_op jit(solution)/shard_map/ppermute | solution.py:312
  33.4 0.0 copy-start.4
  33.4 5.8 %collective-permute-start.2 = (bf16[272,1280]{1,0:T(8,128)(2,1)S(1)}, bf16[272,1280]{1,0:T(8,128)(2,1)}, u32[]{:S(2)}, u32[]{:S(2)}) collective-permute-start(bf16[272,1280]{1,0:T(8,128)(2,1)S(1)} %collective-permute-done.1.x2_ref), channel_id=1, source_target_pairs={{0,1},{1,0},{2,3},{3,2},{4,5},{5,4},{6,7},{7,6},{8,9},{9,8},{10,11... | collective-permute-start | bytes 2088968 | tf_op jit(solution)/shard_map/ppermute | solution.py:309
  39.1 1.9 %collective-permute-start.3 = (bf16[256,1280]{1,0:T(8,128)(2,1)S(1)}, bf16[256,1280]{1,0:T(8,128)(2,1)S(1)}, u32[]{:S(2)}, u32[]{:S(2)}) collective-permute-start(bf16[256,1280]{1,0:T(8,128)(2,1)S(1)} %copy-done.1), channel_id=1, source_target_pairs={{0,1},{1,0},{2,3},{3,2},{4,5},{5,4},{6,7},{7,6},{8,9},{9,8},{10,11... | collective-permute-start | bytes 1966088 | tf_op jit(solution)/shard_map/ppermute | solution.py:309
  41.1 6.3 %collective-permute-done.4.c2_ref = bf16[256,1280]{1,0:T(8,128)(2,1)S(1)} collective-permute-done((bf16[256,1280]{1,0:T(8,128)(2,1)S(1)}, bf16[256,1280]{1,0:T(8,128)(2,1)S(1)}, u32[]{:S(2)}, u32[]{:S(2)}) %collective-permute-start.4) | collective-permute-done | bytes 655392 | tf_op jit(solution)/shard_map/ppermute | solution.py:312
  47.4 0.0 copy-start.6
  47.4 3.5 %collective-permute-start.5 = (bf16[256,1280]{1,0:T(8,128)(2,1)S(1)}, bf16[256,1280]{1,0:T(8,128)(2,1)S(1)}, u32[]{:S(2)}, u32[]{:S(2)}) collective-permute-start(bf16[256,1280]{1,0:T(8,128)(2,1)S(1)} %collective-permute-done.4.c2_ref), channel_id=1, source_target_pairs={{0,1},{1,0},{2,3},{3,2},{4,5},{5,4},{6,7},{7,6},{8,9},{9,8},{10,11... | collective-permute-start | bytes 1966088 | tf_op jit(solution)/shard_map/ppermute | solution.py:309
  50.9 0.0 collective-permute-done.3.c1_ref
  50.9 0.0 collective-permute-done.x1_ref
  50.9 0.0 copy-done.6
  50.9 0.0 copy-start.5
  50.9 1.7 %collective-permute-done.5.c3_ref = bf16[256,1280]{1,0:T(8,128)(2,1)S(1)} collective-permute-done((bf16[256,1280]{1,0:T(8,128)(2,1)S(1)}, bf16[256,1280]{1,0:T(8,128)(2,1)S(1)}, u32[]{:S(2)}, u32[]{:S(2)}) %collective-permute-start.5) | collective-permute-done | bytes 655392 | tf_op jit(solution)/shard_map/ppermute | solution.py:309
  52.6 0.0 copy-start.7
  52.6 0.8 copy-done.7
  53.4 0.0 collective-permute-done.2.x3_ref
  53.4 0.0 all-to-all-done
  53.4 0.0 copy-done.5
  53.4 0.0 copy-done.4
  53.4 0.0 copy-done
  53.4 9.9 %shard_map.105 = (bf16[320,1024]{1,0:T(8,128)(2,1)S(1)}, bf16[320,1280]{1,0:T(8,128)(2,1)}) custom-call(s32[1]{0:T(128)} %bitcast.place_ref, s32[64]{0:T(128)S(1)} %copy-done, bf16[272,1280]{1,0:T(8,128)(2,1)} %get-tuple-element.16.x0_ref, bf16[272,1280]{1,0:T(8,128)(2,1)} %copy-done.5, bf16[272,1280]{1,0:T(8,128)(2,1)} %copy-done.4, ...), custom_call_target="tpu_custom_call" | custom-call | flops 3892314112 | bytes 12582912 | tf_op jit(solution)/shard_map/pallas_call | solution.py:347
  63.4 5.2 %all-to-all-start.1 = ((bf16[8,40,1280]{2,1,0:T(8,128)(2,1)}), bf16[8,40,1280]{2,1,0:T(8,128)(2,1)S(1)}, u32[]{:S(2)}, u32[]{:S(2)}) async-start(bf16[8,40,1280]{2,1,0:T(8,128)(2,1)} %bitcast.31), calls=%async_computation.1 | async-start | bytes 1638400 | tf_op jit(solution)/shard_map/all_to_all | solution.py:397
  68.5 4.4 %shard_map.106 = (bf16[2,256,1280]{2,1,0:T(8,128)(2,1)S(1)}, bf16[2,256,1280]{2,1,0:T(8,128)(2,1)}) custom-call(s32[1]{0:T(128)} %bitcast.place_ref, s32[64]{0:T(128)S(1)} %copy-done, bf16[320,1024]{1,0:T(8,128)(2,1)S(1)} %get-tuple-element.19.from_ref, bf16[16,80,1280]{2,1,0:T(8,128)(2,1)} %bitcast.4.blocks_ref), custom_call_target="tpu_custom_call" | custom-call | flops 838860800 | bytes 6291456 | tf_op jit(solution)/shard_map/pallas_call | solution.py:379
  72.9 1.9 %collective-permute-start.6 = (bf16[2,256,1280]{2,1,0:T(8,128)(2,1)}, bf16[2,256,1280]{2,1,0:T(8,128)(2,1)}, u32[]{:S(2)}, u32[]{:S(2)}) collective-permute-start(bf16[2,256,1280]{2,1,0:T(8,128)(2,1)} %get-tuple-element.22), channel_id=1, source_target_pairs={{0,1},{1,0},{2,3},{3,2},{4,5},{5,4},{6,7},{7,6},{8,9},{9,8},{10,11... | collective-permute-start | bytes 3932168 | tf_op jit(solution)/shard_map/ppermute | solution.py:309
  74.8 4.1 %all-to-all-done.1.terms_ref = bf16[8,40,1280]{2,1,0:T(8,128)(2,1)S(1)} async-done(((bf16[8,40,1280]{2,1,0:T(8,128)(2,1)}), bf16[8,40,1280]{2,1,0:T(8,128)(2,1)S(1)}, u32[]{:S(2)}, u32[]{:S(2)}) %all-to-all-start.1) | async-done | bytes 819232 | tf_op jit(solution)/shard_map/all_to_all | solution.py:397
  78.9 0.9 shard_map.107
  79.8 5.6 %all-to-all-start.2 = ((bf16[4,40,1280]{2,1,0:T(8,128)(2,1)}), bf16[4,40,1280]{2,1,0:T(8,128)(2,1)S(1)}, u32[]{:S(2)}, u32[]{:S(2)}) async-start(bf16[4,40,1280]{2,1,0:T(8,128)(2,1)} %shard_map.107), calls=%async_computation.2 | async-start | bytes 819200 | tf_op jit(solution)/shard_map/all_to_all | solution.py:402
  85.4 0.0 collective-permute-done.6
  85.4 2.1 %fusion.3 = bf16[256,1280]{1,0:T(8,128)(2,1)} fusion(bf16[2,256,1280]{2,1,0:T(8,128)(2,1)} %collective-permute-done.6, bf16[2,256,1280]{2,1,0:T(8,128)(2,1)S(1)} %get-tuple-element.25), kind=kLoop, calls=%fused_computation.5 | loop fusion | flops 1310720 | bytes 1966080 | tf_op jit(solution)/shard_map/convert_element_type | solution.py:401
  87.4 0.0 copy-start.2
  87.4 3.8 %collective-permute-start.7 = (bf16[256,1280]{1,0:T(8,128)(2,1)}, bf16[256,1280]{1,0:T(8,128)(2,1)S(1)}, u32[]{:S(2)}, u32[]{:S(2)}) collective-permute-start(bf16[256,1280]{1,0:T(8,128)(2,1)} %fusion.3), channel_id=1, source_target_pairs={{0,2},{2,0},{1,3},{3,1},{4,6},{6,4},{5,7},{7,5},{8,10},{10,8},{9,1... | collective-permute-start | bytes 1966088 | tf_op jit(solution)/shard_map/ppermute | solution.py:312
  91.3 2.8 %all-to-all-done.2.terms_ref = bf16[4,40,1280]{2,1,0:T(8,128)(2,1)S(1)} async-done(((bf16[4,40,1280]{2,1,0:T(8,128)(2,1)}), bf16[4,40,1280]{2,1,0:T(8,128)(2,1)S(1)}, u32[]{:S(2)}, u32[]{:S(2)}) %all-to-all-start.2) | async-done | bytes 409632 | tf_op jit(solution)/shard_map/all_to_all | solution.py:402
  94.1 0.8 shard_map.108
  94.9 10.0 %all-to-all-start.3 = ((bf16[4,40,1280]{2,1,0:T(8,128)(2,1)}), bf16[4,40,1280]{2,1,0:T(8,128)(2,1)S(1)}, u32[]{:S(2)}, u32[]{:S(2)}) async-start(bf16[4,40,1280]{2,1,0:T(8,128)(2,1)} %shard_map.108), calls=%async_computation.3 | async-start | bytes 819200 | tf_op jit(solution)/shard_map/all_to_all | solution.py:406
  104.9 0.1 broadcast_in_dim.66
  105.0 0.1 broadcast_in_dim.67
  105.1 2.3 %collective-permute-done.7 = bf16[256,1280]{1,0:T(8,128)(2,1)S(1)} collective-permute-done((bf16[256,1280]{1,0:T(8,128)(2,1)}, bf16[256,1280]{1,0:T(8,128)(2,1)S(1)}, u32[]{:S(2)}, u32[]{:S(2)}) %collective-permute-start.7) | collective-permute-done | bytes 655392 | tf_op jit(solution)/shard_map/ppermute | solution.py:312
  107.4 11.2 %all-to-all-done.3.terms_ref = bf16[4,40,1280]{2,1,0:T(8,128)(2,1)S(1)} async-done(((bf16[4,40,1280]{2,1,0:T(8,128)(2,1)}), bf16[4,40,1280]{2,1,0:T(8,128)(2,1)S(1)}, u32[]{:S(2)}, u32[]{:S(2)}) %all-to-all-start.3) | async-done | bytes 409632 | tf_op jit(solution)/shard_map/all_to_all | solution.py:406
  118.7 0.1 shard_map.109
  118.7 1.9 %collective-permute-start.9 = (bf16[40,1280]{1,0:T(8,128)(2,1)S(1)}, bf16[40,1280]{1,0:T(8,128)(2,1)S(1)}, u32[]{:S(2)}, u32[]{:S(2)}) collective-permute-start(bf16[40,1280]{1,0:T(8,128)(2,1)S(1)} %bitcast.28), channel_id=1, source_target_pairs={{0,64},{2,0},{64,66},{66,2},{128,130},{130,194},{192,128},{194,192... | collective-permute-start | bytes 307208 | tf_op jit(solution)/shard_map/ppermute | solution.py:410
  120.7 2.3 %collective-permute-start.8 = (bf16[40,1280]{1,0:T(8,128)(2,1)S(1)}, bf16[40,1280]{1,0:T(8,128)(2,1)S(1)}, u32[]{:S(2)}, u32[]{:S(2)}) collective-permute-start(bf16[40,1280]{1,0:T(8,128)(2,1)S(1)} %bitcast.29), channel_id=1, source_target_pairs={{0,66},{66,0},{130,192},{192,130},{1,67},{67,1},{131,193},{193,131... | collective-permute-start | bytes 307208 | tf_op jit(solution)/shard_map/ppermute | solution.py:411
  122.9 0.0 copy-done.2
  122.9 2.3 %fusion.2 = bf16[256,1280]{1,0:T(8,128)(2,1)} fusion(bf16[256,1280]{1,0:T(8,128)(2,1)S(1)} %collective-permute-done.7, bf16[256,1280]{1,0:T(8,128)(2,1)S(1)} %copy-done.2, bf16[2,256,1280]{2,1,0:T(8,128)(2,1)} %collective-permute-done.6, bf16[2,256,1280]{2,1,0:T(8,128)(2,1)S(1)} %get-tuple-element.25, pred[256]{0:T(512)(128)(4,1)S(1)} %iota_compare_fusion), kind=kLoop, calls=%fused_computation.3 | loop fusion | flops 2949120 | bytes 3277056 | tf_op jit(solution)/shard_map/convert_element_type | solution.py:414
  125.2 2.6 %collective-permute-done.8 = bf16[40,1280]{1,0:T(8,128)(2,1)S(1)} collective-permute-done((bf16[40,1280]{1,0:T(8,128)(2,1)S(1)}, bf16[40,1280]{1,0:T(8,128)(2,1)S(1)}, u32[]{:S(2)}, u32[]{:S(2)}) %collective-permute-start.8) | collective-permute-done | bytes 102432 | tf_op jit(solution)/shard_map/ppermute | solution.py:411
  127.8 0.0 collective-permute-done.9
  127.8 0.1 bitcast_select_fusion.1
  127.9 2.3 %collective-permute-start.10 = (bf16[80,1280]{1,0:T(8,128)(2,1)S(1)}, bf16[80,1280]{1,0:T(8,128)(2,1)S(1)}, u32[]{:S(2)}, u32[]{:S(2)}) collective-permute-start(bf16[80,1280]{1,0:T(8,128)(2,1)S(1)} %bitcast_select_fusion.1), channel_id=1, source_target_pairs={{0,1},{1,0},{2,3},{3,2},{4,5},{5,4},{6,7},{7,6},{8,9},{9,8},{10,11... | collective-permute-start | bytes 614408 | tf_op jit(solution)/shard_map/ppermute | solution.py:309
  130.3 0.1 broadcast_in_dim.63
  130.3 0.1 broadcast_in_dim.64
  130.4 0.9 collective-permute-done.10
  131.3 0.9 bitcast_select_fusion
  (4 shorter events, 0.0 us)
Async XLA Ops:
  5.2 9.1 %copy-start.3 = (bf16[272,1280]{1,0:T(8,128)(2,1)S(1)}, bf16[272,1280]{1,0:T(8,128)(2,1)}, u32[]{:S(2)}) copy-start(bf16[272,1280]{1,0:T(8,128)(2,1)} %get-tuple-element.16.x0_ref) | copy-start | bytes 2088964
  5.3 13.1 %copy-start.1 = (bf16[256,1280]{1,0:T(8,128)(2,1)S(1)}, bf16[256,1280]{1,0:T(8,128)(2,1)}, u32[]{:S(2)}) copy-start(bf16[256,1280]{1,0:T(8,128)(2,1)} %c0_ref.1) | copy-start | bytes 1966084
  5.3 48.2 %copy-start = (s32[64]{0:T(128)S(1)}, s32[64]{0:T(128)}, u32[]{:S(2)}) copy-start(s32[64]{0:T(128)} %constant.58.clone.order_ref) | copy-start | bytes 772
  5.3 48.1 %all-to-all-start = ((bf16[8,2,80,1280]{3,2,1,0:T(8,128)(2,1)}), bf16[8,2,80,1280]{3,2,1,0:T(8,128)(2,1)}, u32[]{:S(2)}, u32[]{:S(2)}) async-start(bf16[8,2,80,1280]{3,2,1,0:T(8,128)(2,1)} %get-tuple-element.17), calls=%async_computation | async-start | bytes 6553600 | tf_op jit(solution)/shard_map/all_to_all | solution.py:338
  14.4 19.0 %collective-permute-start.1 = (bf16[272,1280]{1,0:T(8,128)(2,1)S(1)}, bf16[272,1280]{1,0:T(8,128)(2,1)S(1)}, u32[]{:S(2)}, u32[]{:S(2)}) collective-permute-start(bf16[272,1280]{1,0:T(8,128)(2,1)S(1)} %copy-done.3), channel_id=1, source_target_pairs={{0,2},{2,0},{1,3},{3,1},{4,6},{6,4},{5,7},{7,5},{8,10},{10,8},{9,1... | collective-permute-start | bytes 2088968 | tf_op jit(solution)/shard_map/ppermute | solution.py:312
  18.4 29.0 %collective-permute-start.4 = (bf16[256,1280]{1,0:T(8,128)(2,1)S(1)}, bf16[256,1280]{1,0:T(8,128)(2,1)S(1)}, u32[]{:S(2)}, u32[]{:S(2)}) collective-permute-start(bf16[256,1280]{1,0:T(8,128)(2,1)S(1)} %copy-done.1), channel_id=1, source_target_pairs={{0,2},{2,0},{1,3},{3,1},{4,6},{6,4},{5,7},{7,5},{8,10},{10,8},{9,1... | collective-permute-start | bytes 1966088 | tf_op jit(solution)/shard_map/ppermute | solution.py:312
  20.3 30.6 %collective-permute-start = (bf16[272,1280]{1,0:T(8,128)(2,1)S(1)}, bf16[272,1280]{1,0:T(8,128)(2,1)S(1)}, u32[]{:S(2)}, u32[]{:S(2)}) collective-permute-start(bf16[272,1280]{1,0:T(8,128)(2,1)S(1)} %copy-done.3), channel_id=1, source_target_pairs={{0,1},{1,0},{2,3},{3,2},{4,5},{5,4},{6,7},{7,6},{8,9},{9,8},{10,11... | collective-permute-start | bytes 2088968 | tf_op jit(solution)/shard_map/ppermute | solution.py:309
  33.4 20.1 %copy-start.4 = (bf16[272,1280]{1,0:T(8,128)(2,1)}, bf16[272,1280]{1,0:T(8,128)(2,1)S(1)}, u32[]{:S(2)}) copy-start(bf16[272,1280]{1,0:T(8,128)(2,1)S(1)} %collective-permute-done.1.x2_ref) | copy-start | bytes 2088964
  33.4 20.1 %collective-permute-start.2 = (bf16[272,1280]{1,0:T(8,128)(2,1)S(1)}, bf16[272,1280]{1,0:T(8,128)(2,1)}, u32[]{:S(2)}, u32[]{:S(2)}) collective-permute-start(bf16[272,1280]{1,0:T(8,128)(2,1)S(1)} %collective-permute-done.1.x2_ref), channel_id=1, source_target_pairs={{0,1},{1,0},{2,3},{3,2},{4,5},{5,4},{6,7},{7,6},{8,9},{9,8},{10,11... | collective-permute-start | bytes 2088968 | tf_op jit(solution)/shard_map/ppermute | solution.py:309
  39.1 11.8 %collective-permute-start.3 = (bf16[256,1280]{1,0:T(8,128)(2,1)S(1)}, bf16[256,1280]{1,0:T(8,128)(2,1)S(1)}, u32[]{:S(2)}, u32[]{:S(2)}) collective-permute-start(bf16[256,1280]{1,0:T(8,128)(2,1)S(1)} %copy-done.1), channel_id=1, source_target_pairs={{0,1},{1,0},{2,3},{3,2},{4,5},{5,4},{6,7},{7,6},{8,9},{9,8},{10,11... | collective-permute-start | bytes 1966088 | tf_op jit(solution)/shard_map/ppermute | solution.py:309
  47.4 3.5 %copy-start.6 = (bf16[256,1280]{1,0:T(8,128)(2,1)}, bf16[256,1280]{1,0:T(8,128)(2,1)S(1)}, u32[]{:S(2)}) copy-start(bf16[256,1280]{1,0:T(8,128)(2,1)S(1)} %collective-permute-done.4.c2_ref) | copy-start | bytes 1966084
  47.4 5.2 %collective-permute-start.5 = (bf16[256,1280]{1,0:T(8,128)(2,1)S(1)}, bf16[256,1280]{1,0:T(8,128)(2,1)S(1)}, u32[]{:S(2)}, u32[]{:S(2)}) collective-permute-start(bf16[256,1280]{1,0:T(8,128)(2,1)S(1)} %collective-permute-done.4.c2_ref), channel_id=1, source_target_pairs={{0,1},{1,0},{2,3},{3,2},{4,5},{5,4},{6,7},{7,6},{8,9},{9,8},{10,11... | collective-permute-start | bytes 1966088 | tf_op jit(solution)/shard_map/ppermute | solution.py:309
  50.9 2.5 %copy-start.5 = (bf16[272,1280]{1,0:T(8,128)(2,1)}, bf16[272,1280]{1,0:T(8,128)(2,1)S(1)}, u32[]{:S(2)}) copy-start(bf16[272,1280]{1,0:T(8,128)(2,1)S(1)} %collective-permute-done.x1_ref) | copy-start | bytes 2088964
  52.6 0.8 copy-start.7
  63.4 15.6 %all-to-all-start.1 = ((bf16[8,40,1280]{2,1,0:T(8,128)(2,1)}), bf16[8,40,1280]{2,1,0:T(8,128)(2,1)S(1)}, u32[]{:S(2)}, u32[]{:S(2)}) async-start(bf16[8,40,1280]{2,1,0:T(8,128)(2,1)} %bitcast.31), calls=%async_computation.1 | async-start | bytes 1638400 | tf_op jit(solution)/shard_map/all_to_all | solution.py:397
  72.9 12.5 %collective-permute-start.6 = (bf16[2,256,1280]{2,1,0:T(8,128)(2,1)}, bf16[2,256,1280]{2,1,0:T(8,128)(2,1)}, u32[]{:S(2)}, u32[]{:S(2)}) collective-permute-start(bf16[2,256,1280]{2,1,0:T(8,128)(2,1)} %get-tuple-element.22), channel_id=1, source_target_pairs={{0,1},{1,0},{2,3},{3,2},{4,5},{5,4},{6,7},{7,6},{8,9},{9,8},{10,11... | collective-permute-start | bytes 3932168 | tf_op jit(solution)/shard_map/ppermute | solution.py:309
  79.8 14.3 %all-to-all-start.2 = ((bf16[4,40,1280]{2,1,0:T(8,128)(2,1)}), bf16[4,40,1280]{2,1,0:T(8,128)(2,1)S(1)}, u32[]{:S(2)}, u32[]{:S(2)}) async-start(bf16[4,40,1280]{2,1,0:T(8,128)(2,1)} %shard_map.107), calls=%async_computation.2 | async-start | bytes 819200 | tf_op jit(solution)/shard_map/all_to_all | solution.py:402
  87.4 35.5 %copy-start.2 = (bf16[256,1280]{1,0:T(8,128)(2,1)S(1)}, bf16[256,1280]{1,0:T(8,128)(2,1)}, u32[]{:S(2)}) copy-start(bf16[256,1280]{1,0:T(8,128)(2,1)} %patches_ref.1) | copy-start | bytes 1966084
  87.4 20.0 %collective-permute-start.7 = (bf16[256,1280]{1,0:T(8,128)(2,1)}, bf16[256,1280]{1,0:T(8,128)(2,1)S(1)}, u32[]{:S(2)}, u32[]{:S(2)}) collective-permute-start(bf16[256,1280]{1,0:T(8,128)(2,1)} %fusion.3), channel_id=1, source_target_pairs={{0,2},{2,0},{1,3},{3,1},{4,6},{6,4},{5,7},{7,5},{8,10},{10,8},{9,1... | collective-permute-start | bytes 1966088 | tf_op jit(solution)/shard_map/ppermute | solution.py:312
  94.9 23.8 %all-to-all-start.3 = ((bf16[4,40,1280]{2,1,0:T(8,128)(2,1)}), bf16[4,40,1280]{2,1,0:T(8,128)(2,1)S(1)}, u32[]{:S(2)}, u32[]{:S(2)}) async-start(bf16[4,40,1280]{2,1,0:T(8,128)(2,1)} %shard_map.108), calls=%async_computation.3 | async-start | bytes 819200 | tf_op jit(solution)/shard_map/all_to_all | solution.py:406
  118.7 9.1 %collective-permute-start.9 = (bf16[40,1280]{1,0:T(8,128)(2,1)S(1)}, bf16[40,1280]{1,0:T(8,128)(2,1)S(1)}, u32[]{:S(2)}, u32[]{:S(2)}) collective-permute-start(bf16[40,1280]{1,0:T(8,128)(2,1)S(1)} %bitcast.28), channel_id=1, source_target_pairs={{0,64},{2,0},{64,66},{66,2},{128,130},{130,194},{192,128},{194,192... | collective-permute-start | bytes 307208 | tf_op jit(solution)/shard_map/ppermute | solution.py:410
  120.7 7.1 %collective-permute-start.8 = (bf16[40,1280]{1,0:T(8,128)(2,1)S(1)}, bf16[40,1280]{1,0:T(8,128)(2,1)S(1)}, u32[]{:S(2)}, u32[]{:S(2)}) collective-permute-start(bf16[40,1280]{1,0:T(8,128)(2,1)S(1)} %bitcast.29), channel_id=1, source_target_pairs={{0,66},{66,0},{130,192},{192,130},{1,67},{67,1},{131,193},{193,131... | collective-permute-start | bytes 307208 | tf_op jit(solution)/shard_map/ppermute | solution.py:411
  127.9 3.4 %collective-permute-start.10 = (bf16[80,1280]{1,0:T(8,128)(2,1)S(1)}, bf16[80,1280]{1,0:T(8,128)(2,1)S(1)}, u32[]{:S(2)}, u32[]{:S(2)}) collective-permute-start(bf16[80,1280]{1,0:T(8,128)(2,1)S(1)} %bitcast_select_fusion.1), channel_id=1, source_target_pairs={{0,1},{1,0},{2,3},{3,2},{4,5},{5,4},{6,7},{7,6},{8,9},{9,8},{10,11... | collective-permute-start | bytes 614408 | tf_op jit(solution)/shard_map/ppermute | solution.py:309
